TPU v7x, 256 devices: a whole 4x4x8 slice. The times are simulated.
256 devices in a mesh: pipe: 8 (over x, core), ctx: 32 (over y, z).
Axes of the slice: x: 4, y: 4, z: 8, core: 2. Of those that a mesh axis runs over, the one named last changes fastest.
Arguments:
- queries: bfloat16 [8, 4096, 4096], P('pipe', 'ctx'), may hold values from -60 to 60
- key_projection: bfloat16 [8, 4096, 512], P('pipe', 'ctx'), may hold values from -6 to 6
- value_projection: bfloat16 [8, 4096, 512], P('pipe', 'ctx'), may hold values from -6 to 6
- forward_out: bfloat16 [8, 4096, 4096], P('pipe', 'ctx'), may hold values from -6 to 6
- incoming: bfloat16 [8, 4096, 4096], P('pipe', 'ctx'), may hold values from -6 to 6
- doc_lengths: int32 [8, 16], P('pipe'), may hold values from 1 to 1024, 4096 in all within a row
- pair_of: int32 [8, 32], P('pipe'), may hold values from 0 to 31, each once within a row
Outputs:
- query_grad: bfloat16 [8, 4096, 4096], P('pipe', 'ctx')
- key_gradient: bfloat16 [8, 4096, 512], P('pipe', 'ctx')
- value_gradient: bfloat16 [8, 4096, 512], P('pipe', 'ctx')
All inputs are finite; a program needn't handle non-finite values.
Results may differ from a plain program's by a relative error of at most 0.005.
Values may be sent and summed in bfloat16 or wider, within the bound.
No kernel may reach another device: no remote copies, remote signals or barrier semaphores. Data moves between devices by JAX's collectives and lax.ppermute only.
A program may use at most 128 MiB of HBM per device.

v0:
```python
import math

import jax
import jax.numpy as jnp
from jax import lax
from jax.sharding import PartitionSpec as P

QUERY_HEADS = 32
KEY_VALUE_HEADS = 4
HEAD_SIZE = 128
TOK_DEV = 128


def shifted(x, axis, by):
    count = lax.axis_size(axis)
    return lax.ppermute(x, axis, [(i, (i + by) % count) for i in range(count)])


def head_tiles(block_of_rows, query_group_size):
    count_of_rows = block_of_rows.shape[0]
    return (
        block_of_rows.reshape(count_of_rows, KEY_VALUE_HEADS, query_group_size, HEAD_SIZE)
        .transpose(1, 2, 0, 3)
        .reshape(KEY_VALUE_HEADS, query_group_size * count_of_rows, HEAD_SIZE)
    )


def tile_rows(query_blocks, query_group_size):
    count_of_rows = query_blocks.shape[1] // query_group_size
    return (
        query_blocks.reshape(KEY_VALUE_HEADS, query_group_size, count_of_rows, HEAD_SIZE)
        .transpose(2, 0, 1, 3)
        .reshape(count_of_rows, KEY_VALUE_HEADS * query_group_size * HEAD_SIZE)
    )


def visible(query_pos, query_start, key_pos):
    return (key_pos[None, :] <= query_pos[:, None]) & (key_pos[None, :] >= query_start[:, None])


def head_split(rows_per_block):
    return rows_per_block.reshape(rows_per_block.shape[0], KEY_VALUE_HEADS, HEAD_SIZE)


def block_scores(query_blocks, key_block, score_scale):
    return score_scale * jnp.einsum(
        "hrd,khd->hrk", query_blocks, head_split(key_block), preferred_element_type=jnp.float32
    )


def block_grads(kept_half, key_block, value_block, key_pos, score_scale):
    query_blocks, grad_tiles, log_total, row_delta, query_pos, query_start = kept_half
    keep_mask = visible(query_pos, query_start, key_pos)
    scores = block_scores(query_blocks, key_block, score_scale)
    prob_rows = jnp.where(keep_mask[None], jnp.exp(scores - log_total[:, :, None]), 0.0)
    dprobs = jnp.einsum(
        "hrd,khd->hrk", grad_tiles, head_split(value_block), preferred_element_type=jnp.float32
    )
    dscores = (prob_rows * (dprobs - row_delta[:, :, None])).astype(jnp.bfloat16)
    return (prob_rows.astype(jnp.bfloat16), dscores)


def key_value_terms(kept_half, prob_low, dscores, score_scale):
    query_blocks, grad_tiles = (kept_half[0], kept_half[1])
    count_of_keys = dscores.shape[2]
    key_contribution = score_scale * jnp.einsum(
        "hrk,hrd->khd", dscores, query_blocks, preferred_element_type=jnp.float32
    )
    value_contribution = jnp.einsum(
        "hrk,hrd->khd", prob_low, grad_tiles, preferred_element_type=jnp.float32
    )
    return (
        key_contribution.reshape(count_of_keys, KEY_VALUE_HEADS * HEAD_SIZE),
        value_contribution.reshape(count_of_keys, KEY_VALUE_HEADS * HEAD_SIZE),
    )


def row_stats(
    query_blocks, sorted_keys, query_pos, query_start, block_low, block_high, key_width, score_scale
):
    count_of_rows = query_blocks.shape[1]

    def row_advance(block_index, loop_state):
        running_max, running_sum = loop_state
        key_block = lax.dynamic_slice_in_dim(sorted_keys, block_index * key_width, key_width, 0)
        key_pos = block_index * key_width + jnp.arange(key_width, dtype=jnp.int32)
        keep_mask = visible(query_pos, query_start, key_pos)
        scores = jnp.where(
            keep_mask[None], block_scores(query_blocks, key_block, score_scale), -jnp.inf
        )
        new_max = jnp.maximum(running_max, jnp.max(scores, axis=2))
        running_sum = running_sum * jnp.exp(running_max - new_max) + jnp.sum(
            jnp.exp(scores - new_max[:, :, None]), axis=2
        )
        return (new_max, running_sum)

    start_state = (
        jnp.full((KEY_VALUE_HEADS, count_of_rows), -1e30, jnp.float32),
        jnp.zeros((KEY_VALUE_HEADS, count_of_rows), jnp.float32),
    )
    running_max, running_sum = lax.fori_loop(block_low, block_high, row_advance, start_state)
    return running_max + jnp.log(running_sum)


def query_pass(
    kept_half, sorted_keys, sorted_values, block_low, block_high, key_width, score_scale, kv_state
):
    query_blocks = kept_half[0]

    def query_advance(block_index, loop_state):
        offset = block_index * key_width
        key_block = lax.dynamic_slice_in_dim(sorted_keys, offset, key_width, 0)
        value_block = lax.dynamic_slice_in_dim(sorted_values, offset, key_width, 0)
        key_pos = offset + jnp.arange(key_width, dtype=jnp.int32)
        prob_low, dscores = block_grads(kept_half, key_block, value_block, key_pos, score_scale)
        query_acc = loop_state[0] + jnp.einsum(
            "hrk,khd->hrd", dscores, head_split(key_block), preferred_element_type=jnp.float32
        )
        key_contribution, value_contribution = key_value_terms(
            kept_half, prob_low, dscores, score_scale
        )
        key_acc = lax.dynamic_update_slice_in_dim(
            loop_state[1],
            lax.dynamic_slice_in_dim(loop_state[1], offset, key_width, 0) + key_contribution,
            offset,
            0,
        )
        value_acc = lax.dynamic_update_slice_in_dim(
            loop_state[2],
            lax.dynamic_slice_in_dim(loop_state[2], offset, key_width, 0) + value_contribution,
            offset,
            0,
        )
        return (query_acc, key_acc, value_acc)

    start_state = (jnp.zeros(query_blocks.shape, jnp.float32),) + kv_state
    return lax.fori_loop(block_low, block_high, query_advance, start_state)


def per_device(
    queries, key_projection, value_projection, forward_out, incoming, doc_lengths, pair_of
):
    ctx_count = lax.axis_size("ctx")
    slot_rows = TOK_DEV // 2
    every_row = TOK_DEV * ctx_count
    key_width = min(256, every_row)
    query_group_size = QUERY_HEADS // KEY_VALUE_HEADS
    score_scale = 1.0 / math.sqrt(HEAD_SIZE)
    out_grad = shifted(incoming[0], "pipe", -1)
    gathered_keys, gathered_values = (
        lax.all_gather(key_projection[0], "ctx", axis=0, tiled=True),
        lax.all_gather(value_projection[0], "ctx", axis=0, tiled=True),
    )
    pair_ids = pair_of[0]
    slot_blocks = jnp.stack([pair_ids, 2 * ctx_count - 1 - pair_ids], axis=1).reshape(-1)
    ordinal = jnp.arange(2 * ctx_count, dtype=jnp.int32)
    slot_of_block = jnp.sum(
        jnp.where(slot_blocks[None, :] == ordinal[:, None], ordinal[None, :], 0), axis=1
    )
    sorted_keys = gathered_keys.reshape(2 * ctx_count, slot_rows, -1)[slot_of_block].reshape(
        every_row, -1
    )
    sorted_values = gathered_values.reshape(2 * ctx_count, slot_rows, -1)[slot_of_block].reshape(
        every_row, -1
    )
    lengths_row = doc_lengths[0]
    doc_ends = jnp.cumsum(lengths_row)
    own_index = lax.axis_index("ctx")
    kv_state = ()
    kv_state = (
        jnp.zeros((every_row, KEY_VALUE_HEADS * HEAD_SIZE), jnp.float32),
        jnp.zeros((every_row, KEY_VALUE_HEADS * HEAD_SIZE), jnp.float32),
    )
    saved_halves = []
    windows = []
    query_parts = []
    for half_index in range(2):
        own_block = slot_blocks[2 * own_index + half_index]
        local_pos = own_block * slot_rows + jnp.arange(slot_rows, dtype=jnp.int32)
        local_start = jnp.sum(
            jnp.where(doc_ends[None, :] <= local_pos[:, None], lengths_row[None, :], 0), axis=1
        )
        query_pos = jnp.tile(local_pos, query_group_size)
        query_start = jnp.tile(local_start, query_group_size)
        row_begin = half_index * slot_rows
        query_blocks = head_tiles(queries[0, row_begin : row_begin + slot_rows], query_group_size)
        grad_tiles = head_tiles(out_grad[row_begin : row_begin + slot_rows], query_group_size)
        output_tiles = head_tiles(
            forward_out[0, row_begin : row_begin + slot_rows], query_group_size
        )
        row_delta = jnp.sum(
            grad_tiles.astype(jnp.float32) * output_tiles.astype(jnp.float32), axis=2
        )
        block_high = (own_block * slot_rows + slot_rows - 1) // key_width + 1
        block_low = jnp.int32(0)
        log_total = row_stats(
            query_blocks,
            sorted_keys,
            query_pos,
            query_start,
            block_low,
            block_high,
            key_width,
            score_scale,
        )
        kept_half = (query_blocks, grad_tiles, log_total, row_delta, query_pos, query_start)
        result = query_pass(
            kept_half,
            sorted_keys,
            sorted_values,
            block_low,
            block_high,
            key_width,
            score_scale,
            kv_state,
        )
        query_parts.append(tile_rows(score_scale * result[0], query_group_size))
        kv_state = tuple(result[1:])
        saved_halves.append(kept_half)
        windows.append((block_low * key_width, own_block * slot_rows + slot_rows - 1))
    query_grad = jnp.concatenate(query_parts, axis=0).astype(jnp.bfloat16)
    key_slots = (
        kv_state[0].reshape(2 * ctx_count, slot_rows, -1)[slot_blocks].reshape(every_row, -1)
    )
    value_slots = (
        kv_state[1].reshape(2 * ctx_count, slot_rows, -1)[slot_blocks].reshape(every_row, -1)
    )
    key_gradient, value_gradient = (
        lax.psum_scatter(key_slots, "ctx", scatter_dimension=0, tiled=True),
        lax.psum_scatter(value_slots, "ctx", scatter_dimension=0, tiled=True),
    )
    return (
        query_grad[None],
        key_gradient.astype(jnp.bfloat16)[None],
        value_gradient.astype(jnp.bfloat16)[None],
    )


def solution(mesh):
    placed = (
        P("pipe", "ctx", None),
        P("pipe", "ctx", None),
        P("pipe", "ctx", None),
        P("pipe", "ctx", None),
        P("pipe", "ctx", None),
        P("pipe", None),
        P("pipe", None),
    )
    return jax.shard_map(
        per_device,
        mesh=mesh,
        in_specs=placed,
        out_specs=(P("pipe", "ctx", None), P("pipe", "ctx", None), P("pipe", "ctx", None)),
        check_vma=False,
    )
```

profile of v0, /device:TPU:2, one launch (start us, length us, event | category | flops | bytes accessed | tf_op | source)
XLA Modules:
  0.0 882.2 jit_solution(338568196362333845)
XLA Ops:
  16.7 2.4 copy.245
  19.1 2.4 copy.242
  27.9 1.7 fusion.24
  31.6 63.8 %all-gather.7.cloned.1.call-done = bf16[1,4096,512]{2,1,0:T(8,128)(2,1)} async-done(((bf16[1,128,512]{2,1,0:T(8,128)(2,1)}), bf16[1,4096,512]{2,1,0:T(8,128)(2,1)}) %all-gather.7.cloned.1.call-update) | async-done | bytes 4194320 | tf_op jit(solution)/shard_map/all_gather | solution.py:152
  95.4 5.0 gather_fusion.1
  100.4 76.7 %all-gather.5.cloned.1.call-done = bf16[1,4096,512]{2,1,0:T(8,128)(2,1)} async-done(((bf16[1,128,512]{2,1,0:T(8,128)(2,1)}), bf16[1,4096,512]{2,1,0:T(8,128)(2,1)}) %all-gather.5.cloned.1.call-update) | async-done | bytes 4194320 | tf_op jit(solution)/shard_map/all_gather | solution.py:151
  177.1 5.0 gather_fusion
  182.0 6.4 copy.205
  188.4 6.4 copy.207
  194.8 24.6 %while.58 = (s32[]{:T(128)}, f32[4,512]{1,0:T(4,128)S(1)}, f32[4,512]{1,0:T(4,128)S(1)}, s32[]{:T(128)}, bf16[4096,512]{0,1:T(8,128)(2,1)}, /*index=5*/bf16[4,51...) while((s32[]{:T(128)}, f32[4,512]{1,0:T(4,128)S(1)}, ...), condition=%wide.region_14.15_spmd.clone, body=%wide.region_11.14_spmd.clone.sunk | while | flops 138285312 | bytes 6023851 | solution.py:101
  219.5 17.3 %while.56 = (s32[]{:T(128)}, f32[4,512]{1,0:T(4,128)S(1)}, f32[4,512]{1,0:T(4,128)S(1)}, s32[]{:T(128)}, bf16[4096,512]{0,1:T(8,128)(2,1)}, /*index=5*/bf16[4,51...) while((s32[]{:T(128)}, f32[4,512]{1,0:T(4,128)S(1)}, ...), condition=%wide.region_6.7_spmd.clone, body=%wide.region_3.6_spmd.clone.sunk | while | flops 138285312 | bytes 6023851 | solution.py:101
  236.9 4.3 broadcast.269.clone
  241.1 4.2 broadcast.269
  245.4 53.0 %while.57 = (s32[]{:T(128)}, f32[4,512,128]{2,1,0:T(8,128)S(1)}, f32[4096,512]{0,1:T(8,128)}, f32[4096,512]{0,1:T(8,128)}, s32[]{:T(128)}, /*index=5*/bf16[4096,...) while((s32[]{:T(128)}, f32[4,512,128]{2,1,0:T(8,128)S(1)}, ...), condition=%wide.region_9.10_spmd.clone, body=%wide.region_8.9_spmd.clone.sunk | while | flops 675807488 | bytes 19958492 | solution.py:137
  250.6 2.4 constant_dynamic-update-slice_fusion.6
  258.2 2.4 constant_dynamic-update-slice_fusion.6
  265.8 2.4 constant_dynamic-update-slice_fusion.6
  273.3 2.4 constant_dynamic-update-slice_fusion.6
  280.9 2.4 constant_dynamic-update-slice_fusion.6
  288.5 2.3 constant_dynamic-update-slice_fusion.6
  296.0 2.4 constant_dynamic-update-slice_fusion.6
  298.5 91.4 %while.59 = (s32[]{:T(128)}, f32[4,512,128]{2,1,0:T(8,128)S(1)}, f32[4096,512]{0,1:T(8,128)}, f32[4096,512]{0,1:T(8,128)}, s32[]{:T(128)}, /*index=5*/bf16[4096,...) while((s32[]{:T(128)}, f32[4,512,128]{2,1,0:T(8,128)S(1)}, ...), condition=%wide.region_17.18_spmd.clone, body=%wide.region_16.17_spmd.clone.sunk | while | flops 675807488 | bytes 22055672 | solution.py:137
  300.9 1.8 bitcast_select_fusion.7
  305.4 2.4 constant_dynamic-update-slice_fusion.7
  310.0 1.8 bitcast_select_fusion.7
  314.5 2.4 constant_dynamic-update-slice_fusion.7
  319.2 1.8 bitcast_select_fusion.7
  323.7 2.4 constant_dynamic-update-slice_fusion.7
  328.3 1.8 bitcast_select_fusion.7
  332.8 2.4 constant_dynamic-update-slice_fusion.7
  337.5 1.8 bitcast_select_fusion.7
  342.0 2.4 constant_dynamic-update-slice_fusion.7
  346.6 1.8 bitcast_select_fusion.7
  351.1 2.3 constant_dynamic-update-slice_fusion.7
  355.8 1.8 bitcast_select_fusion.7
  360.3 2.4 constant_dynamic-update-slice_fusion.7
  364.9 1.8 bitcast_select_fusion.7
  369.4 2.3 constant_dynamic-update-slice_fusion.7
  374.1 1.8 bitcast_select_fusion.7
  378.6 2.3 constant_dynamic-update-slice_fusion.7
  383.1 1.8 bitcast_select_fusion.7
  387.6 2.3 constant_dynamic-update-slice_fusion.7
  390.0 9.0 %copy.221 = f32[4096,512]{1,0:T(8,128)} copy(f32[4096,512]{0,1:T(8,128)} %get-tuple-element.240) | data formatting | bytes 16777216 | tf_op jit(solution)/shard_map/while | solution.py:137
  399.0 7.7 gather_fusion.3
  406.7 9.0 %copy.219 = f32[4096,512]{1,0:T(8,128)} copy(f32[4096,512]{0,1:T(8,128)} %get-tuple-element.239) | data formatting | bytes 16777216 | tf_op jit(solution)/shard_map/while | solution.py:137
  415.7 7.7 gather_fusion.2
  425.9 216.1 %reduce-scatter.5.cloned.1.call-done = f32[128,512]{1,0:T(8,128)} async-done(((f32[4096,512]{1,0:T(8,128)}), f32[128,512]{1,0:T(8,128)}) %reduce-scatter.5.cloned.1.call-update) | async-done | bytes 262160 | tf_op jit(solution)/shard_map/reduce_scatter | solution.py:230
  643.7 230.4 %reduce-scatter.3.cloned.1.call-done = f32[128,512]{1,0:T(8,128)} async-done(((f32[4096,512]{1,0:T(8,128)}), f32[128,512]{1,0:T(8,128)}) %reduce-scatter.3.cloned.1.call-update) | async-done | bytes 262160 | tf_op jit(solution)/shard_map/reduce_scatter | solution.py:229
  (506 shorter events, 148.7 us)
Async XLA Ops:
  7.2 3.5 copy-start.2
  7.2 88.2 %all-gather.7.cloned.1.call-start = ((), (), s32[]{:S(2)}) async-start(), calls=%async_computation.5 | async-start | bytes 4325376 | tf_op jit(solution)/shard_map/all_gather | solution.py:152
  7.9 169.2 %all-gather.5.cloned.1.call-start = ((), (), s32[]{:S(2)}) async-start(), calls=%async_computation.4 | async-start | bytes 4325376 | tf_op jit(solution)/shard_map/all_gather | solution.py:151
  8.7 633.4 %reduce-scatter.5.cloned.1.call-start = ((), (), s32[]{:S(2)}) async-start(), calls=%async_computation.3 | async-start | bytes 8650752 | tf_op jit(solution)/shard_map/reduce_scatter | solution.py:230
  8.7 13.1 %collective-permute-start = (bf16[128,4096]{1,0:T(8,128)(2,1)}, bf16[128,4096]{1,0:T(8,128)(2,1)}, u32[]{:S(2)}, u32[]{:S(2)}) collective-permute-start(bf16[128,4096]{1,0:T(8,128)(2,1)} %bitcast.264), channel_id=1, source_target_pairs={{0,224},{32,0},{64,32},{96,64},{128,96},{160,128},{192,160},{224,1... | collective-permute-start | bytes 3145736 | tf_op jit(solution)/shard_map/ppermute | solution.py:16
  10.7 1.6 copy-start.4
  10.7 3.9 copy-start.3
  23.1 3.5 copy-start.1
  303.1 1.0 copy-start
  312.3 1.0 copy-start
  321.4 1.0 copy-start
  330.6 1.0 copy-start
  339.8 1.0 copy-start
  348.9 1.0 copy-start
  358.0 1.0 copy-start
  367.2 1.0 copy-start
  376.3 1.0 copy-start
  385.4 1.0 copy-start
  406.7 467.4 %reduce-scatter.3.cloned.1.call-start = ((), (), s32[]{:S(2)}) async-start(), calls=%async_computation.2 | async-start | bytes 8650752 | tf_op jit(solution)/shard_map/reduce_scatter | solution.py:229
Sparse Core Ops, SparseCore 0:
  10.6 84.7 all-gather.6
  98.0 79.0 all-gather.4
  406.8 235.2 reduce-scatter.4
  646.5 227.5 reduce-scatter.2
where the time goes:
time: 887 us; the launch traced here: 882 us
  waiting for transfers between devices  588 us (66%)
  local copies, waits for them, and re-layouts  142 us (16%)
  matrix products  69.3 us (8%)
  other arithmetic  64.7 us (7%)
  between operations  15.5 us (2%)
    reduce_scatter x1, waiting for transfers between devices, per_device(): lax.psum_scatter(key_slots, 'ctx', scatter_dimension=0, tiled=True)  230 us
    reduce_scatter x1, waiting for transfers between devices, per_device(): lax.psum_scatter(value_slots, 'ctx', scatter_dimension=0, tiled=True)  216 us
    all_gather x1, waiting for transfers between devices, per_device(): lax.all_gather(key_projection[0], 'ctx', axis=0, tiled=True)  76.7 us
    all_gather x1, waiting for transfers between devices, per_device(): lax.all_gather(value_projection[0], 'ctx', axis=0, tiled=True)  63.8 us
    dynamic_update_slice x17, other arithmetic, query_advance(): lax.dynamic_update_slice_in_dim(loop_state[2], lax.dynamic_slice_in_dim(l...  39.9 us
    dot_general x34, matrix products, block_scores(): jnp.einsum('hrd,khd->hrk', query_blocks, head_split(key_block), preferred...  32.9 us
    unnamed x22, local copies, waits for them, and re-layouts  24.3 us
    while x2, local copies, waits for them, and re-layouts, query_pass(): return lax.fori_loop(block_low, block_high, query_advance, start_state)  18 us
  transfers between devices with their start and end apart: 5, of which 4 were waited for; matrix products, arithmetic and copies ran while one was open for 5% of the time, Pallas kernels for 0%

commit v1 on v0

v1 whole, which is shorter than its diff:
```python
import functools
import math

import jax
import jax.numpy as jnp
from jax import lax
from jax.experimental import pallas as pl
from jax.experimental.pallas import tpu as pltpu
from jax.sharding import PartitionSpec as P

HEADS = 4
GROUP = 8
DIM = 128
TOK = 128
SLOT = 64
ROWS = GROUP * SLOT
DOCS = 16
NY = 4
NZ = 8
SECTIONS = 8
ALL = TOK * NY * NZ
BLOCKS = 2 * NY
TILE = 256
WINDOW = 1024
MAX_TILES = (WINDOW + SLOT - 2) // TILE + 2
SCALE = 1.0 / math.sqrt(DIM)
LOG2E = 1.4426950408889634
LOW = -1e30
WIDE = GROUP * DIM

NT = (((1,), (1,)), ((), ()))
NN = (((1,), (0,)), ((), ()))


def along_y(x, by):
    return lax.ppermute(
        x, "ctx", [(c, (c // NZ + by) % NY * NZ + c % NZ) for c in range(NY * NZ)]
    )


def along_pipe_y(x, by):
    count = NY * NZ
    return lax.ppermute(
        x,
        ("pipe", "ctx"),
        [
            (p * count + c, (p - 1) % SECTIONS * count + (c // NZ + by) % NY * NZ + c % NZ)
            for p in range(SECTIONS)
            for c in range(count)
        ],
    )


def dot(a, b, dims):
    return lax.dot_general(a, b, dims, preferred_element_type=jnp.float32)


def whole(count):
    return [pl.BlockSpec(memory_space=pltpu.VMEM)] * count


def scalars():
    return pl.BlockSpec(memory_space=pltpu.SMEM)


def params(mib):
    return pltpu.CompilerParams(vmem_limit_bytes=mib << 20)


def column(y, k, width):
    return pl.ds(pl.multiple_of(lax.rem(y + k, NY) * width, width), width)


def pack_kv_body(info, key, value, *outs):
    for k in range(NY):
        outs[k][:, :DIM] = key[:, column(info[48], k, DIM)]
        outs[k][:, DIM:] = value[:, column(info[48], k, DIM)]


def pack_kv(info, key, value):
    return pl.pallas_call(
        pack_kv_body,
        out_shape=[jax.ShapeDtypeStruct((TOK, 2 * DIM), jnp.bfloat16)] * NY,
        in_specs=[scalars()] + whole(2),
        out_specs=whole(NY),
        name="pack_kv",
    )(info, key, value)


def pack_wide_body(info, x, *outs):
    for k in range(NY):
        outs[k][...] = x[:, column(info[48], k, WIDE)]


def pack_wide(info, x):
    return pl.pallas_call(
        pack_wide_body,
        out_shape=[jax.ShapeDtypeStruct((TOK, WIDE), jnp.bfloat16)] * NY,
        in_specs=[scalars()] + whole(1),
        out_specs=whole(NY),
        name="pack_wide",
    )(info, x)


def delta_body(info, grad, out, *outs):
    ones = jnp.ones((8, DIM), jnp.bfloat16)
    for k in range(NY):
        columns = column(info[48], k, WIDE)
        product = grad[:, columns].astype(jnp.float32) * out[:, columns].astype(jnp.float32)
        high = product.astype(jnp.bfloat16)
        low = (product - high.astype(jnp.float32)).astype(jnp.bfloat16)
        for s in range(2):
            rows = slice(s * SLOT, (s + 1) * SLOT)
            parts = []
            for part in (high, low):
                stacked = jnp.concatenate(
                    [part[rows, h * DIM : (h + 1) * DIM] for h in range(GROUP)], axis=0
                )
                parts.append(dot(ones, stacked, NT))
            outs[k][s * 8 : (s + 1) * 8, :] = parts[0] + parts[1]


def row_deltas(info, grad, out):
    return pl.pallas_call(
        delta_body,
        out_shape=[jax.ShapeDtypeStruct((16, ROWS), jnp.float32)] * NY,
        in_specs=[scalars()] + whole(2),
        out_specs=whole(NY),
        name="row_deltas",
    )(info, grad, out)


def main_body(info, *refs):
    queries, grads, deltas = refs[0:NY], refs[NY : 2 * NY], refs[2 * NY : 3 * NY]
    gathered = refs[3 * NY]
    query_outs = refs[3 * NY + 1 : 4 * NY + 1]
    kv_out = refs[4 * NY + 1]
    (keys, values, keys_t, key_acc, value_acc, scores, query_acc, q_rows, g_rows, d_rows, dq_rows) = refs[
        4 * NY + 2 :
    ]
    y, z = info[48], info[49]

    def block_at(zi, yr, s):
        pid = info[lax.rem(y + NY - yr, NY) * NZ + zi]
        return jnp.where(s == 0, pid, 2 * NY * NZ - 1 - pid)

    def sort_in(zi, carry):
        for yr in range(NY):
            for s in range(2):
                dst = pl.ds(pl.multiple_of(block_at(zi, yr, s) * SLOT, SLOT), SLOT)
                src = pl.ds(pl.multiple_of(zi * (NY * TOK) + yr * TOK + s * SLOT, SLOT), SLOT)
                keys[dst, :] = gathered[src, :DIM]
                values[dst, :] = gathered[src, DIM:]
        return carry

    lax.fori_loop(0, NZ, sort_in, 0)

    for t in range(ALL // TILE):
        keys_t[t] = keys[t * TILE : (t + 1) * TILE, :].T
    key_acc[...] = jnp.zeros_like(key_acc)
    value_acc[...] = jnp.zeros_like(value_acc)

    for yr in range(NY):
        for s in range(2):
            rows = slice(s * SLOT, (s + 1) * SLOT)
            for h in range(GROUP):
                at = slice(h * SLOT, (h + 1) * SLOT)
                q_rows[2 * yr + s, at, :] = queries[yr][rows, h * DIM : (h + 1) * DIM]
                g_rows[2 * yr + s, at, :] = grads[yr][rows, h * DIM : (h + 1) * DIM]
            d_rows[2 * yr + s] = deltas[yr][s * 8 : (s + 1) * 8, :]

    def start_of(pos):
        start = jnp.zeros_like(pos)
        for i in range(DOCS):
            end = info[32 + i]
            start = jnp.where(end <= pos, end, start)
        return start

    def block_step(i, carry):
        qb = q_rows[i]
        gb = g_rows[i]
        first = block_at(z, i // 2, lax.rem(i, 2)) * SLOT
        lane = lax.broadcasted_iota(jnp.int32, (1, ROWS), 1)
        q_pos = first + (lane & (SLOT - 1))
        q_start = start_of(q_pos)
        low_tile = start_of(first) // TILE
        high_tile = (first + SLOT - 1) // TILE + 1

        def score_step(t, peak):
            kt = keys[pl.ds(pl.multiple_of(t * TILE, TILE), TILE), :]
            st = dot(kt, qb, NT)
            k_pos = t * TILE + lax.broadcasted_iota(jnp.int32, (TILE, ROWS), 0)
            st = jnp.where((k_pos <= q_pos) & (k_pos >= q_start), st, LOW)
            scores[t - low_tile] = st
            return jnp.maximum(peak, jnp.max(st.reshape(TILE // 8, 8, ROWS), axis=0))

        peak = lax.fori_loop(
            low_tile, high_tile, score_step, jnp.full((8, ROWS), LOW, jnp.float32)
        )
        peak = jnp.max(peak, axis=0, keepdims=True)

        def exp_step(t, total):
            e = jnp.exp2((scores[t - low_tile] - peak) * (SCALE * LOG2E))
            scores[t - low_tile] = e
            return total + jnp.sum(e.reshape(TILE // 8, 8, ROWS), axis=0)

        total = lax.fori_loop(low_tile, high_tile, exp_step, jnp.zeros((8, ROWS), jnp.float32))
        inverse = 1.0 / jnp.sum(total, axis=0, keepdims=True)
        delta = d_rows[i][0:1, :]
        query_acc[...] = jnp.zeros_like(query_acc)

        def grad_step(t, carry):
            rows = pl.ds(pl.multiple_of(t * TILE, TILE), TILE)
            prob = scores[t - low_tile] * inverse
            dprob = dot(values[rows, :], gb, NT)
            dscore = (prob * (dprob - delta)).astype(jnp.bfloat16)
            key_acc[rows, :] += dot(dscore, qb, NN)
            value_acc[rows, :] += dot(prob.astype(jnp.bfloat16), gb, NN)
            query_acc[...] += dot(keys_t[t], dscore, NN)
            return carry

        lax.fori_loop(low_tile, high_tile, grad_step, 0)
        dq_rows[i] = (query_acc[...].T * SCALE).astype(jnp.bfloat16)
        return carry

    lax.fori_loop(0, BLOCKS, block_step, 0)

    for yr in range(NY):
        for s in range(2):
            for h in range(GROUP):
                query_outs[yr][s * SLOT : (s + 1) * SLOT, h * DIM : (h + 1) * DIM] = dq_rows[
                    2 * yr + s, h * SLOT : (h + 1) * SLOT, :
                ]

    def sort_out(zi, carry):
        for yr in range(NY):
            for s in range(2):
                src = pl.ds(pl.multiple_of(block_at(zi, yr, s) * SLOT, SLOT), SLOT)
                dst = pl.ds(pl.multiple_of(zi * (NY * TOK) + yr * TOK + s * SLOT, SLOT), SLOT)
                kv_out[dst, :DIM] = (key_acc[src, :] * SCALE).astype(kv_out.dtype)
                kv_out[dst, DIM:] = value_acc[src, :].astype(kv_out.dtype)
        return carry

    lax.fori_loop(0, NZ, sort_out, 0)


def attention_grads(info, queries, grads, deltas, gathered):
    bf16, f32 = jnp.bfloat16, jnp.float32
    return pl.pallas_call(
        main_body,
        out_shape=[jax.ShapeDtypeStruct((TOK, WIDE), bf16)] * NY
        + [jax.ShapeDtypeStruct((ALL, 2 * DIM), bf16)],
        in_specs=[scalars()] + whole(3 * NY + 1),
        out_specs=whole(NY + 1),
        scratch_shapes=[
            pltpu.VMEM((ALL, DIM), bf16),
            pltpu.VMEM((ALL, DIM), bf16),
            pltpu.VMEM((ALL // TILE, DIM, TILE), bf16),
            pltpu.VMEM((ALL, DIM), f32),
            pltpu.VMEM((ALL, DIM), f32),
            pltpu.VMEM((MAX_TILES, TILE, ROWS), f32),
            pltpu.VMEM((DIM, ROWS), f32),
            pltpu.VMEM((BLOCKS, ROWS, DIM), bf16),
            pltpu.VMEM((BLOCKS, ROWS, DIM), bf16),
            pltpu.VMEM((BLOCKS, 8, ROWS), f32),
            pltpu.VMEM((BLOCKS, ROWS, DIM), bf16),
        ],
        compiler_params=params(48),
        name="attention_grads",
    )(info, *queries, *grads, *deltas, gathered)


def place_wide_body(info, *refs):
    for k in range(NY):
        refs[NY][:, column(info[48], k, WIDE)] = refs[k][...]


def place_wide(info, pieces):
    return pl.pallas_call(
        place_wide_body,
        out_shape=jax.ShapeDtypeStruct((TOK, HEADS * WIDE), jnp.bfloat16),
        in_specs=[scalars()] + whole(NY),
        out_specs=pl.BlockSpec(memory_space=pltpu.VMEM),
        name="place_wide",
    )(info, *pieces)


def place_kv_body(info, *refs):
    for k in range(NY):
        refs[NY][:, column(info[48], k, DIM)] = refs[k][:, :DIM]
        refs[NY + 1][:, column(info[48], k, DIM)] = refs[k][:, DIM:]


def place_kv(info, pieces):
    return pl.pallas_call(
        place_kv_body,
        out_shape=[jax.ShapeDtypeStruct((TOK, HEADS * DIM), jnp.bfloat16)] * 2,
        in_specs=[scalars()] + whole(NY),
        out_specs=whole(2),
        name="place_kv",
    )(info, *pieces)


def per_device(
    queries, key_projection, value_projection, forward_out, incoming, doc_lengths, pair_of
):
    place = lax.axis_index("ctx").astype(jnp.int32)
    info = jnp.concatenate(
        [
            pair_of[0].astype(jnp.int32),
            jnp.cumsum(doc_lengths[0]).astype(jnp.int32),
            jnp.stack([place // NZ, place % NZ]),
        ]
    )
    columns_of_ring = [[y * NZ + z for z in range(NZ)] for y in range(NY)]

    def to_heads(pieces, move):
        return [pieces[0]] + [move(pieces[k], k) for k in range(1, NY)]

    with jax.named_scope("keys_values_in"):
        kv = to_heads(pack_kv(info, key_projection[0], value_projection[0]), along_y)
        kv = jnp.concatenate(kv, axis=0)
        gathered = lax.all_gather(
            kv, "ctx", axis=0, tiled=True, axis_index_groups=columns_of_ring
        )
    with jax.named_scope("queries_in"):
        query_pieces = to_heads(pack_wide(info, queries[0]), along_y)
    with jax.named_scope("grads_in"):
        grad_pieces = [along_pipe_y(x, k) for k, x in enumerate(pack_wide(info, incoming[0]))]
    with jax.named_scope("deltas_in"):
        next_out = lax.ppermute(
            forward_out[0], "pipe", [(p, (p + 1) % SECTIONS) for p in range(SECTIONS)]
        )
        delta_pieces = [
            along_pipe_y(x, k) for k, x in enumerate(row_deltas(info, incoming[0], next_out))
        ]
    *query_parts, kv_part = attention_grads(
        info, query_pieces, grad_pieces, delta_pieces, gathered
    )
    with jax.named_scope("query_grads_out"):
        query_grad = place_wide(info, to_heads(query_parts, lambda x, k: along_y(x, -k)))
    with jax.named_scope("key_value_grads_out"):
        kv_sum = lax.psum_scatter(
            kv_part, "ctx", scatter_dimension=0, tiled=True, axis_index_groups=columns_of_ring
        )
        kv_pieces = [kv_sum[k * TOK : (k + 1) * TOK] for k in range(NY)]
        key_gradient, value_gradient = place_kv(
            info, to_heads(kv_pieces, lambda x, k: along_y(x, -k))
        )
    return query_grad[None], key_gradient[None], value_gradient[None]


def solution(mesh):
    tokens = P("pipe", "ctx", None)
    return jax.shard_map(
        per_device,
        mesh=mesh,
        in_specs=(tokens,) * 5 + (P("pipe", None),) * 2,
        out_specs=(tokens,) * 3,
        check_vma=False,
    )
```

time: 887 us -> 151 us (0.17)
  waiting for transfers between devices: 588 us -> 60.2 us
  local copies, waits for them, and re-layouts: 142 us -> 4.43 us
  matrix products: 69.3 us -> 0 us
  other arithmetic: 64.7 us -> 3.01 us
  Pallas kernels: 0 us -> 34.2 us
  starting transfers between devices: 0.17 us -> 33.6 us
    reduce_scatter x2 -> x1, waiting for transfers between devices: 447 us -> 38.2 us  [per_device(): lax.psum_scatter(kv_part, 'ctx', scatter_dimension=0, tiled=True, axis_in...]
    all_gather x2 -> x1, waiting for transfers between devices: 140 us -> 9.7 us  [per_device(): lax.all_gather(kv, 'ctx', axis=0, tiled=True, axis_index_groups=columns_o...]
    dot_general x102 -> x0, matrix products: 69.3 us -> none  [the longest x34 32.9 us: block_scores(): jnp.einsum('hrd,khd->hrk', query_blocks, head_split(key_block), preferred...]
    dynamic_slice x52 -> x0, local copies, waits for them, and re-layouts: 50.4 us -> none  [the longest x17 16.6 us: row_advance(): lax.dynamic_slice_in_dim(sorted_keys, block_index * key_width, key_width, 0)]
    dynamic_update_slice x17 -> x0, other arithmetic: 39.9 us -> none  [query_advance(): lax.dynamic_update_slice_in_dim(loop_state[2], lax.dynamic_slice_in_dim(l...]
    pallas_call x0 -> x7, Pallas kernels: none -> 34.2 us  [the longest x1 21.2 us: attention_grads(): pl.pallas_call(main_body, out_shape=[jax.ShapeDtypeStruct((TOK, WIDE), bf...]
    ppermute x1 -> x21, starting transfers between devices: 0.02 us -> 33.5 us  [the longest x12 22.8 us: along_y(): lax.ppermute(x, 'ctx', [(c, (c // NZ + by) % NY * NZ + c % NZ) for c in r...]
    gather x4 -> x0, local copies, waits for them, and re-layouts: 25.3 us -> none  [the longest x1 7.69 us: per_device(): kv_state[1].reshape(2 * ctx_count, slot_rows, -1)[slot_blocks]]
  transfers between devices with their start and end apart: 5 -> 23, of which waited for: 4 -> 9; matrix products, arithmetic and copies ran while one was open for 5% -> 1% of each run, Pallas kernels for 0% -> 6%
where the time goes in v1:
time: 151 us; the launch traced here: 150 us
  waiting for transfers between devices  60.2 us (40%)
  Pallas kernels  34.2 us (23%)
  starting transfers between devices  33.6 us (22%)
  between operations  14.2 us (9%)
  local copies, waits for them, and re-layouts  4.43 us (3%)
  other arithmetic  3.01 us (2%)
    reduce_scatter x1, waiting for transfers between devices, per_device(): lax.psum_scatter(kv_part, 'ctx', scatter_dimension=0, tiled=True, axis_in...  38.2 us
    ppermute x12, starting transfers between devices, along_y(): lax.ppermute(x, 'ctx', [(c, (c // NZ + by) % NY * NZ + c % NZ) for c in r...  22.8 us
    pallas_call x1, Pallas kernels, attention_grads(): pl.pallas_call(main_body, out_shape=[jax.ShapeDtypeStruct((TOK, WIDE), bf...  21.2 us
    ppermute x8, starting transfers between devices, along_pipe_y(): lax.ppermute(x, ('pipe', 'ctx'), [(p * count + c, (p - 1) % SECTIONS * co...  10.7 us
    all_gather x1, waiting for transfers between devices, per_device(): lax.all_gather(kv, 'ctx', axis=0, tiled=True, axis_index_groups=columns_o...  9.7 us
    ppermute x12, waiting for transfers between devices, along_y(): lax.ppermute(x, 'ctx', [(c, (c // NZ + by) % NY * NZ + c % NZ) for c in r...  7.65 us
    pallas_call x2, Pallas kernels, pack_wide(): pl.pallas_call(pack_wide_body, out_shape=[jax.ShapeDtypeStruct((TOK, WIDE...  4.55 us
    ppermute x8, waiting for transfers between devices, along_pipe_y(): lax.ppermute(x, ('pipe', 'ctx'), [(p * count + c, (p - 1) % SECTIONS * co...  3.86 us
  transfers between devices with their start and end apart: 23, of which 9 were waited for; matrix products, arithmetic and copies ran while one was open for 1% of the time, Pallas kernels for 6%

profile of v1, /device:TPU:2, one launch (start us, length us, event | category | flops | bytes accessed | tf_op | source)
XLA Modules:
  0.0 149.6 jit_solution(14511339219790616906)
XLA Ops:
  7.2 0.0 all-gather.2.cloned.1.call-start
  7.2 0.7 copy.11
  8.0 0.1 reduce
  8.1 1.3 pad_add_fusion.info
  9.4 1.7 %pack_kv.1 = (bf16[128,256]{1,0:T(8,128)(2,1)}, bf16[128,256]{1,0:T(8,128)(2,1)}, bf16[128,256]{1,0:T(8,128)(2,1)}, bf16[128,256]{1,0:T(8,128)(2,1)}) custom-call(s32[50]{0:T(128)} %pad_add_fusion.info, bf16[128,512]{1,0:T(8,128)(2,1)} %bitcast.16, bf16[128,512]{1,0:T(8,128)(2,1)} %bitcast.17), custom_call_target="tpu_custom_call" | custom-call | tf_op jit(solution)/shard_map/keys_values_in/pack_kv/pallas_call | solution.py:81
  11.1 1.6 %collective-permute-start.12 = (bf16[128,256]{1,0:T(8,128)(2,1)}, bf16[128,256]{1,0:T(8,128)(2,1)S(1)}, u32[]{:S(2)}, u32[]{:S(2)}) collective-permute-start(bf16[128,256]{1,0:T(8,128)(2,1)} %get-tuple-element.39), channel_id=1, source_target_pairs={{0,8},{1,9},{2,10},{3,11},{4,12},{5,13},{6,14},{7,15},{8,16},{9,17... | collective-permute-start | bytes 196616 | tf_op jit(solution)/shard_map/keys_values_in/ppermute | solution.py:36
  12.7 2.9 %collective-permute-start.13 = (bf16[128,256]{1,0:T(8,128)(2,1)}, bf16[128,256]{1,0:T(8,128)(2,1)S(1)}, u32[]{:S(2)}, u32[]{:S(2)}) collective-permute-start(bf16[128,256]{1,0:T(8,128)(2,1)} %get-tuple-element.40), channel_id=1, source_target_pairs={{0,16},{1,17},{2,18},{3,19},{4,20},{5,21},{6,22},{7,23},{8,24},{9,... | collective-permute-start | bytes 196616 | tf_op jit(solution)/shard_map/keys_values_in/ppermute | solution.py:36
  15.6 1.3 collective-permute-start.14
  17.0 2.1 %collective-permute-done.13 = bf16[128,256]{1,0:T(8,128)(2,1)S(1)} collective-permute-done((bf16[128,256]{1,0:T(8,128)(2,1)}, bf16[128,256]{1,0:T(8,128)(2,1)S(1)}, u32[]{:S(2)}, u32[]{:S(2)}) %collective-permute-start.13) | collective-permute-done | bytes 65568 | tf_op jit(solution)/shard_map/keys_values_in/ppermute | solution.py:36
  19.0 1.1 collective-permute-done.14
  20.1 1.6 %pad_maximum_fusion = bf16[512,256]{1,0:T(8,128)(2,1)} fusion(bf16[128,256]{1,0:T(8,128)(2,1)S(1)} %collective-permute-done.14, bf16[128,256]{1,0:T(8,128)(2,1)S(1)} %collective-permute-done.13, bf16[128,256]{1,0:T(8,128)(2,1)S(1)} %collective-permute-done.12, bf16[128,256]{1,0:T(8,128)(2,1)} %get-tuple-element.38), kind=kLoop, calls=%fused_computation | loop fusion | flops 1048576 | bytes 524288 | tf_op jit(solution)/shard_map/keys_values_in/concatenate | solution.py:322
  21.7 0.0 reduce-scatter.2.cloned.1.call-start
  21.7 0.0 collective-permute-start.7
  21.7 2.3 %pack_wide.3 = (bf16[128,1024]{1,0:T(8,128)(2,1)}, bf16[128,1024]{1,0:T(8,128)(2,1)}, bf16[128,1024]{1,0:T(8,128)(2,1)}, bf16[128,1024]{1,0:T(8,128)(2,1)}) custom-call(s32[50]{0:T(128)} %pad_add_fusion.info, bf16[128,4096]{1,0:T(8,128)(2,1)} %bitcast.12), custom_call_target="tpu_custom_call" | custom-call | tf_op jit(solution)/shard_map/grads_in/pack_wide/pallas_call | solution.py:96
  24.0 1.7 %collective-permute-start.3 = (bf16[128,1024]{1,0:T(8,128)(2,1)}, bf16[128,1024]{1,0:T(8,128)(2,1)S(1)}, u32[]{:S(2)}, u32[]{:S(2)}) collective-permute-start(bf16[128,1024]{1,0:T(8,128)(2,1)} %get-tuple-element.30), channel_id=1, source_target_pairs={{0,224},{1,225},{2,226},{3,227},{4,228},{5,229},{6,230},{7,231},{8... | collective-permute-start | bytes 786440 | tf_op jit(solution)/shard_map/grads_in/ppermute | solution.py:43
  25.7 5.1 %collective-permute-start.5 = (bf16[128,1024]{1,0:T(8,128)(2,1)}, bf16[128,1024]{1,0:T(8,128)(2,1)S(1)}, u32[]{:S(2)}, u32[]{:S(2)}) collective-permute-start(bf16[128,1024]{1,0:T(8,128)(2,1)} %get-tuple-element.32), channel_id=1, source_target_pairs={{0,240},{1,241},{2,242},{3,243},{4,244},{5,245},{6,246},{7,247},{8... | collective-permute-start | bytes 786440 | tf_op jit(solution)/shard_map/grads_in/ppermute | solution.py:43
  30.8 2.3 %pack_wide.2 = (bf16[128,1024]{1,0:T(8,128)(2,1)}, bf16[128,1024]{1,0:T(8,128)(2,1)}, bf16[128,1024]{1,0:T(8,128)(2,1)}, bf16[128,1024]{1,0:T(8,128)(2,1)}) custom-call(s32[50]{0:T(128)} %pad_add_fusion.info, bf16[128,4096]{1,0:T(8,128)(2,1)} %bitcast.15), custom_call_target="tpu_custom_call" | custom-call | tf_op jit(solution)/shard_map/queries_in/pack_wide/pallas_call | solution.py:96
  33.1 1.5 %collective-permute-start = (bf16[128,1024]{1,0:T(8,128)(2,1)}, bf16[128,1024]{1,0:T(8,128)(2,1)S(1)}, u32[]{:S(2)}, u32[]{:S(2)}) collective-permute-start(bf16[128,1024]{1,0:T(8,128)(2,1)} %get-tuple-element.27), channel_id=1, source_target_pairs={{0,8},{1,9},{2,10},{3,11},{4,12},{5,13},{6,14},{7,15},{8,16},{9,17... | collective-permute-start | bytes 786440 | tf_op jit(solution)/shard_map/queries_in/ppermute | solution.py:36
  34.6 0.7 collective-permute-start.1
  35.3 0.8 collective-permute-done.7.out
  36.2 4.5 %collective-permute-start.2 = (bf16[128,1024]{1,0:T(8,128)(2,1)}, bf16[128,1024]{1,0:T(8,128)(2,1)S(1)}, u32[]{:S(2)}, u32[]{:S(2)}) collective-permute-start(bf16[128,1024]{1,0:T(8,128)(2,1)} %get-tuple-element.29), channel_id=1, source_target_pairs={{0,24},{1,25},{2,26},{3,27},{4,28},{5,29},{6,30},{7,31},{8,0},{9,1... | collective-permute-start | bytes 786440 | tf_op jit(solution)/shard_map/queries_in/ppermute | solution.py:36
  40.7 2.9 %row_deltas.1 = (f32[16,512]{1,0:T(8,128)}, f32[16,512]{1,0:T(8,128)}, f32[16,512]{1,0:T(8,128)}, f32[16,512]{1,0:T(8,128)}) custom-call(s32[50]{0:T(128)} %pad_add_fusion.info, bf16[128,4096]{1,0:T(8,128)(2,1)} %bitcast.13, bf16[128,4096]{1,0:T(8,128)(2,1)} %copy-done.3), custom_call_target="tpu_custom_call" | custom-call | tf_op jit(solution)/shard_map/deltas_in/row_deltas/pallas_call | solution.py:124
  43.5 2.1 %collective-permute-done.5.refs_6_ = bf16[128,1024]{1,0:T(8,128)(2,1)S(1)} collective-permute-done((bf16[128,1024]{1,0:T(8,128)(2,1)}, bf16[128,1024]{1,0:T(8,128)(2,1)S(1)}, u32[]{:S(2)}, u32[]{:S(2)}) %collective-permute-start.5) | collective-permute-done | bytes 262176 | tf_op jit(solution)/shard_map/grads_in/ppermute | solution.py:43
  45.7 0.1 collective-permute-start.8
  45.8 1.9 %collective-permute-start.9 = (f32[16,512]{1,0:T(8,128)}, f32[16,512]{1,0:T(8,128)S(1)}, u32[]{:S(2)}, u32[]{:S(2)}) collective-permute-start(f32[16,512]{1,0:T(8,128)} %get-tuple-element.35), channel_id=1, source_target_pairs={{0,232},{1,233},{2,234},{3,235},{4,236},{5,237},{6,238},{7,239},{8... | collective-permute-start | bytes 98312 | tf_op jit(solution)/shard_map/deltas_in/ppermute | solution.py:43
  47.7 3.1 %collective-permute-done.refs_1_ = bf16[128,1024]{1,0:T(8,128)(2,1)S(1)} collective-permute-done((bf16[128,1024]{1,0:T(8,128)(2,1)}, bf16[128,1024]{1,0:T(8,128)(2,1)S(1)}, u32[]{:S(2)}, u32[]{:S(2)}) %collective-permute-start) | collective-permute-done | bytes 262176 | tf_op jit(solution)/shard_map/queries_in/ppermute | solution.py:36
  50.7 1.0 collective-permute-start.10
  51.7 0.9 collective-permute-start.11
  52.6 1.5 collective-permute-done.2.refs_3_
  54.1 1.7 %collective-permute-done.10.refs_10_ = f32[16,512]{1,0:T(8,128)S(1)} collective-permute-done((f32[16,512]{1,0:T(8,128)}, f32[16,512]{1,0:T(8,128)S(1)}, u32[]{:S(2)}, u32[]{:S(2)}) %collective-permute-start.10) | collective-permute-done | bytes 32800 | tf_op jit(solution)/shard_map/deltas_in/ppermute | solution.py:43
  55.8 9.7 %all-gather.2.cloned.1.call-done.refs_12_ = bf16[4096,256]{1,0:T(8,128)(2,1)} async-done(((bf16[512,256]{1,0:T(8,128)(2,1)}), bf16[4096,256]{1,0:T(8,128)(2,1)}) %all-gather.2.cloned.1.call-update) | async-done | bytes 2097168 | tf_op jit(solution)/shard_map/keys_values_in/all_gather | solution.py:323
  65.5 21.2 %attention_grads.1 = (bf16[128,1024]{1,0:T(8,128)(2,1)S(1)}, bf16[128,1024]{1,0:T(8,128)(2,1)S(1)}, bf16[128,1024]{1,0:T(8,128)(2,1)S(1)}, bf16[128,1024]{1,0:T(8,128)(2,1)S(1)}, bf16[4096,256]{1,0:T(8,128)(2,1)}) custom-call(s32[50]{0:T(128)S(1)} %copy-done.2, bf16[128,1024]{1,0:T(8,128)(2,1)S(1)} %copy-done, ...), custom_call_target="tpu_custom_call" | custom-call | tf_op jit(solution)/shard_map/attention_grads/pallas_call | solution.py:249
  86.6 0.7 copy-done.1
  87.3 3.0 %collective-permute-start.15 = (bf16[128,1024]{1,0:T(8,128)(2,1)S(1)}, bf16[128,1024]{1,0:T(8,128)(2,1)S(1)}, u32[]{:S(2)}, u32[]{:S(2)}) collective-permute-start(bf16[128,1024]{1,0:T(8,128)(2,1)S(1)} %get-tuple-element.43), channel_id=1, source_target_pairs={{0,24},{1,25},{2,26},{3,27},{4,28},{5,29},{6,30},{7,31},{8,0},{9,1... | collective-permute-start | bytes 786440 | tf_op jit(solution)/shard_map/query_grads_out/ppermute | solution.py:36
  90.3 0.8 collective-permute-start.16
  91.2 0.9 collective-permute-start.17
  92.0 38.2 %reduce-scatter.2.cloned.1.call-done = bf16[512,256]{1,0:T(8,128)(2,1)} async-done(((bf16[4096,256]{1,0:T(8,128)(2,1)}), bf16[512,256]{1,0:T(8,128)(2,1)}) %reduce-scatter.2.cloned.1.call-update) | async-done | bytes 262160 | tf_op jit(solution)/shard_map/key_value_grads_out/reduce_scatter | solution.py:343
  130.2 1.6 %fusion = (bf16[128,256]{1,0:T(8,128)(2,1)S(1)}, bf16[128,256]{1,0:T(8,128)(2,1)S(1)}, bf16[128,256]{1,0:T(8,128)(2,1)S(1)}, bf16[128,256]{1,0:T(8,128)(2,1)}) fusion(bf16[512,256]{1,0:T(8,128)(2,1)} %reduce-scatter.2.cloned.1.call-done), kind=kLoop, calls=%fused_computation.2 | loop fusion | bytes 524288 | tf_op jit(solution)/shard_map/key_value_grads_out/slice | solution.py:346
  131.8 1.3 collective-permute-start.20
  133.1 2.9 %collective-permute-start.19 = (bf16[128,256]{1,0:T(8,128)(2,1)S(1)}, bf16[128,256]{1,0:T(8,128)(2,1)S(1)}, u32[]{:S(2)}, u32[]{:S(2)}) collective-permute-start(bf16[128,256]{1,0:T(8,128)(2,1)S(1)} %get-tuple-element.50), channel_id=1, source_target_pairs={{0,16},{1,17},{2,18},{3,19},{4,20},{5,21},{6,22},{7,23},{8,24},{9,... | collective-permute-start | bytes 196616 | tf_op jit(solution)/shard_map/key_value_grads_out/ppermute | solution.py:36
  136.0 1.3 collective-permute-start.18
  137.4 0.7 copy-done.5
  138.0 0.1 copy-done.6
  138.1 2.2 %place_wide.1 = bf16[128,4096]{1,0:T(8,128)(2,1)} custom-call(s32[50]{0:T(128)} %pad_add_fusion.info, bf16[128,1024]{1,0:T(8,128)(2,1)} %copy-done.1, bf16[128,1024]{1,0:T(8,128)(2,1)} %copy-done.4, bf16[128,1024]{1,0:T(8,128)(2,1)} %copy-done.5, bf16[128,1024]{1,0:T(8,128)(2,1)} %copy-done.6), custom_call_target="tpu_custom_call" | custom-call | tf_op jit(solution)/shard_map/query_grads_out/place_wide/pallas_call | solution.py:279
  140.4 0.6 copy-done.7
  141.0 0.0 copy-done.8
  141.0 0.0 copy-done.9
  141.1 1.7 %place_kv.1 = (bf16[128,512]{1,0:T(8,128)(2,1)}, bf16[128,512]{1,0:T(8,128)(2,1)}) custom-call(s32[50]{0:T(128)} %pad_add_fusion.info, bf16[128,256]{1,0:T(8,128)(2,1)} %get-tuple-element.52.refs_0_, bf16[128,256]{1,0:T(8,128)(2,1)} %copy-done.9, bf16[128,256]{1,0:T(8,128)(2,1)} %copy-done.8, bf16[128,256]{1,0:T(8,128)(2,1)} %copy-done.7), custom_call_target="tpu_custom_call" | custom-call | tf_op jit(solution)/shard_map/key_value_grads_out/place_kv/pallas_call | solution.py:295
  (33 shorter events, 0.1 us)
Async XLA Ops:
  7.2 58.3 %all-gather.2.cloned.1.call-start = ((), (), s32[]{:S(2)}) async-start(), calls=%async_computation.1 | async-start | bytes 2359296 | tf_op jit(solution)/shard_map/keys_values_in/all_gather | solution.py:323
  11.1 5.8 %collective-permute-start.12 = (bf16[128,256]{1,0:T(8,128)(2,1)}, bf16[128,256]{1,0:T(8,128)(2,1)S(1)}, u32[]{:S(2)}, u32[]{:S(2)}) collective-permute-start(bf16[128,256]{1,0:T(8,128)(2,1)} %get-tuple-element.39), channel_id=1, source_target_pairs={{0,8},{1,9},{2,10},{3,11},{4,12},{5,13},{6,14},{7,15},{8,16},{9,17... | collective-permute-start | bytes 196616 | tf_op jit(solution)/shard_map/keys_values_in/ppermute | solution.py:36
  12.7 6.3 %collective-permute-start.13 = (bf16[128,256]{1,0:T(8,128)(2,1)}, bf16[128,256]{1,0:T(8,128)(2,1)S(1)}, u32[]{:S(2)}, u32[]{:S(2)}) collective-permute-start(bf16[128,256]{1,0:T(8,128)(2,1)} %get-tuple-element.40), channel_id=1, source_target_pairs={{0,16},{1,17},{2,18},{3,19},{4,20},{5,21},{6,22},{7,23},{8,24},{9,... | collective-permute-start | bytes 196616 | tf_op jit(solution)/shard_map/keys_values_in/ppermute | solution.py:36
  15.6 4.5 %collective-permute-start.14 = (bf16[128,256]{1,0:T(8,128)(2,1)}, bf16[128,256]{1,0:T(8,128)(2,1)S(1)}, u32[]{:S(2)}, u32[]{:S(2)}) collective-permute-start(bf16[128,256]{1,0:T(8,128)(2,1)} %get-tuple-element.41), channel_id=1, source_target_pairs={{0,24},{1,25},{2,26},{3,27},{4,28},{5,29},{6,30},{7,31},{8,0},{9,1... | collective-permute-start | bytes 196616 | tf_op jit(solution)/shard_map/keys_values_in/ppermute | solution.py:36
  21.7 108.6 %reduce-scatter.2.cloned.1.call-start = ((), (), s32[]{:S(2)}) async-start(), calls=%async_computation.2 | async-start | bytes 2359296 | tf_op jit(solution)/shard_map/key_value_grads_out/reduce_scatter | solution.py:343
  21.7 14.4 %collective-permute-start.7 = (bf16[128,4096]{1,0:T(8,128)(2,1)}, bf16[128,4096]{1,0:T(8,128)(2,1)S(1)}, u32[]{:S(2)}, u32[]{:S(2)}) collective-permute-start(bf16[128,4096]{1,0:T(8,128)(2,1)} %bitcast.20), channel_id=1, source_target_pairs={{0,32},{32,64},{64,96},{96,128},{128,160},{160,192},{192,224},{224... | collective-permute-start | bytes 3145736 | tf_op jit(solution)/shard_map/deltas_in/ppermute | solution.py:331
  21.7 43.7 %copy-start.2 = (s32[50]{0:T(128)S(1)}, s32[50]{0:T(128)}, u32[]{:S(2)}) copy-start(s32[50]{0:T(128)} %pad_add_fusion.info) | copy-start | bytes 604
  24.0 9.1 %collective-permute-start.3 = (bf16[128,1024]{1,0:T(8,128)(2,1)}, bf16[128,1024]{1,0:T(8,128)(2,1)S(1)}, u32[]{:S(2)}, u32[]{:S(2)}) collective-permute-start(bf16[128,1024]{1,0:T(8,128)(2,1)} %get-tuple-element.30), channel_id=1, source_target_pairs={{0,224},{1,225},{2,226},{3,227},{4,228},{5,229},{6,230},{7,231},{8... | collective-permute-start | bytes 786440 | tf_op jit(solution)/shard_map/grads_in/ppermute | solution.py:43
  25.7 8.9 %collective-permute-start.4 = (bf16[128,1024]{1,0:T(8,128)(2,1)}, bf16[128,1024]{1,0:T(8,128)(2,1)S(1)}, u32[]{:S(2)}, u32[]{:S(2)}) collective-permute-start(bf16[128,1024]{1,0:T(8,128)(2,1)} %get-tuple-element.31), channel_id=1, source_target_pairs={{0,232},{1,233},{2,234},{3,235},{4,236},{5,237},{6,238},{7,239},{8... | collective-permute-start | bytes 786440 | tf_op jit(solution)/shard_map/grads_in/ppermute | solution.py:43
  25.7 19.9 %collective-permute-start.5 = (bf16[128,1024]{1,0:T(8,128)(2,1)}, bf16[128,1024]{1,0:T(8,128)(2,1)S(1)}, u32[]{:S(2)}, u32[]{:S(2)}) collective-permute-start(bf16[128,1024]{1,0:T(8,128)(2,1)} %get-tuple-element.32), channel_id=1, source_target_pairs={{0,240},{1,241},{2,242},{3,243},{4,244},{5,245},{6,246},{7,247},{8... | collective-permute-start | bytes 786440 | tf_op jit(solution)/shard_map/grads_in/ppermute | solution.py:43
  30.8 15.0 %collective-permute-start.6 = (bf16[128,1024]{1,0:T(8,128)(2,1)}, bf16[128,1024]{1,0:T(8,128)(2,1)S(1)}, u32[]{:S(2)}, u32[]{:S(2)}) collective-permute-start(bf16[128,1024]{1,0:T(8,128)(2,1)} %get-tuple-element.33), channel_id=1, source_target_pairs={{0,248},{1,249},{2,250},{3,251},{4,252},{5,253},{6,254},{7,255},{8... | collective-permute-start | bytes 786440 | tf_op jit(solution)/shard_map/grads_in/ppermute | solution.py:43
  33.1 32.4 %copy-start = (bf16[128,1024]{1,0:T(8,128)(2,1)S(1)}, bf16[128,1024]{1,0:T(8,128)(2,1)}, u32[]{:S(2)}) copy-start(bf16[128,1024]{1,0:T(8,128)(2,1)} %get-tuple-element.26.refs_0_) | copy-start | bytes 786436
  33.1 17.6 %collective-permute-start = (bf16[128,1024]{1,0:T(8,128)(2,1)}, bf16[128,1024]{1,0:T(8,128)(2,1)S(1)}, u32[]{:S(2)}, u32[]{:S(2)}) collective-permute-start(bf16[128,1024]{1,0:T(8,128)(2,1)} %get-tuple-element.27), channel_id=1, source_target_pairs={{0,8},{1,9},{2,10},{3,11},{4,12},{5,13},{6,14},{7,15},{8,16},{9,17... | collective-permute-start | bytes 786440 | tf_op jit(solution)/shard_map/queries_in/ppermute | solution.py:36
  34.6 17.1 %collective-permute-start.1 = (bf16[128,1024]{1,0:T(8,128)(2,1)}, bf16[128,1024]{1,0:T(8,128)(2,1)S(1)}, u32[]{:S(2)}, u32[]{:S(2)}) collective-permute-start(bf16[128,1024]{1,0:T(8,128)(2,1)} %get-tuple-element.28), channel_id=1, source_target_pairs={{0,16},{1,17},{2,18},{3,19},{4,20},{5,21},{6,22},{7,23},{8,24},{9,... | collective-permute-start | bytes 786440 | tf_op jit(solution)/shard_map/queries_in/ppermute | solution.py:36
  36.2 4.5 %copy-start.3 = (bf16[128,4096]{1,0:T(8,128)(2,1)}, bf16[128,4096]{1,0:T(8,128)(2,1)S(1)}, u32[]{:S(2)}) copy-start(bf16[128,4096]{1,0:T(8,128)(2,1)S(1)} %collective-permute-done.7.out) | copy-start | bytes 3145732
  36.2 17.9 %collective-permute-start.2 = (bf16[128,1024]{1,0:T(8,128)(2,1)}, bf16[128,1024]{1,0:T(8,128)(2,1)S(1)}, u32[]{:S(2)}, u32[]{:S(2)}) collective-permute-start(bf16[128,1024]{1,0:T(8,128)(2,1)} %get-tuple-element.29), channel_id=1, source_target_pairs={{0,24},{1,25},{2,26},{3,27},{4,28},{5,29},{6,30},{7,31},{8,0},{9,1... | collective-permute-start | bytes 786440 | tf_op jit(solution)/shard_map/queries_in/ppermute | solution.py:36
  45.7 8.4 %collective-permute-start.8 = (f32[16,512]{1,0:T(8,128)}, f32[16,512]{1,0:T(8,128)S(1)}, u32[]{:S(2)}, u32[]{:S(2)}) collective-permute-start(f32[16,512]{1,0:T(8,128)} %get-tuple-element.34), channel_id=1, source_target_pairs={{0,224},{1,225},{2,226},{3,227},{4,228},{5,229},{6,230},{7,231},{8... | collective-permute-start | bytes 98312 | tf_op jit(solution)/shard_map/deltas_in/ppermute | solution.py:43
  45.8 8.3 %collective-permute-start.9 = (f32[16,512]{1,0:T(8,128)}, f32[16,512]{1,0:T(8,128)S(1)}, u32[]{:S(2)}, u32[]{:S(2)}) collective-permute-start(f32[16,512]{1,0:T(8,128)} %get-tuple-element.35), channel_id=1, source_target_pairs={{0,232},{1,233},{2,234},{3,235},{4,236},{5,237},{6,238},{7,239},{8... | collective-permute-start | bytes 98312 | tf_op jit(solution)/shard_map/deltas_in/ppermute | solution.py:43
  50.7 5.1 %collective-permute-start.10 = (f32[16,512]{1,0:T(8,128)}, f32[16,512]{1,0:T(8,128)S(1)}, u32[]{:S(2)}, u32[]{:S(2)}) collective-permute-start(f32[16,512]{1,0:T(8,128)} %get-tuple-element.36), channel_id=1, source_target_pairs={{0,240},{1,241},{2,242},{3,243},{4,244},{5,245},{6,246},{7,247},{8... | collective-permute-start | bytes 98312 | tf_op jit(solution)/shard_map/deltas_in/ppermute | solution.py:43
  51.7 4.1 %collective-permute-start.11 = (f32[16,512]{1,0:T(8,128)}, f32[16,512]{1,0:T(8,128)S(1)}, u32[]{:S(2)}, u32[]{:S(2)}) collective-permute-start(f32[16,512]{1,0:T(8,128)} %get-tuple-element.37), channel_id=1, source_target_pairs={{0,248},{1,249},{2,250},{3,251},{4,252},{5,253},{6,254},{7,255},{8... | collective-permute-start | bytes 98312 | tf_op jit(solution)/shard_map/deltas_in/ppermute | solution.py:43
  86.6 0.7 copy-start.1
  87.3 48.7 %collective-permute-start.15 = (bf16[128,1024]{1,0:T(8,128)(2,1)S(1)}, bf16[128,1024]{1,0:T(8,128)(2,1)S(1)}, u32[]{:S(2)}, u32[]{:S(2)}) collective-permute-start(bf16[128,1024]{1,0:T(8,128)(2,1)S(1)} %get-tuple-element.43), channel_id=1, source_target_pairs={{0,24},{1,25},{2,26},{3,27},{4,28},{5,29},{6,30},{7,31},{8,0},{9,1... | collective-permute-start | bytes 786440 | tf_op jit(solution)/shard_map/query_grads_out/ppermute | solution.py:36
  90.3 47.0 %collective-permute-start.16 = (bf16[128,1024]{1,0:T(8,128)(2,1)S(1)}, bf16[128,1024]{1,0:T(8,128)(2,1)S(1)}, u32[]{:S(2)}, u32[]{:S(2)}) collective-permute-start(bf16[128,1024]{1,0:T(8,128)(2,1)S(1)} %get-tuple-element.44), channel_id=1, source_target_pairs={{0,16},{1,17},{2,18},{3,19},{4,20},{5,21},{6,22},{7,23},{8,24},{9,... | collective-permute-start | bytes 786440 | tf_op jit(solution)/shard_map/query_grads_out/ppermute | solution.py:36
  91.2 46.2 %collective-permute-start.17 = (bf16[128,1024]{1,0:T(8,128)(2,1)S(1)}, bf16[128,1024]{1,0:T(8,128)(2,1)S(1)}, u32[]{:S(2)}, u32[]{:S(2)}) collective-permute-start(bf16[128,1024]{1,0:T(8,128)(2,1)S(1)} %get-tuple-element.45), channel_id=1, source_target_pairs={{0,8},{1,9},{2,10},{3,11},{4,12},{5,13},{6,14},{7,15},{8,16},{9,17... | collective-permute-start | bytes 786440 | tf_op jit(solution)/shard_map/query_grads_out/ppermute | solution.py:36
  131.8 8.6 %collective-permute-start.20 = (bf16[128,256]{1,0:T(8,128)(2,1)S(1)}, bf16[128,256]{1,0:T(8,128)(2,1)S(1)}, u32[]{:S(2)}, u32[]{:S(2)}) collective-permute-start(bf16[128,256]{1,0:T(8,128)(2,1)S(1)} %get-tuple-element.49), channel_id=1, source_target_pairs={{0,8},{1,9},{2,10},{3,11},{4,12},{5,13},{6,14},{7,15},{8,16},{9,17... | collective-permute-start | bytes 196616 | tf_op jit(solution)/shard_map/key_value_grads_out/ppermute | solution.py:36
  133.1 7.3 %collective-permute-start.19 = (bf16[128,256]{1,0:T(8,128)(2,1)S(1)}, bf16[128,256]{1,0:T(8,128)(2,1)S(1)}, u32[]{:S(2)}, u32[]{:S(2)}) collective-permute-start(bf16[128,256]{1,0:T(8,128)(2,1)S(1)} %get-tuple-element.50), channel_id=1, source_target_pairs={{0,16},{1,17},{2,18},{3,19},{4,20},{5,21},{6,22},{7,23},{8,24},{9,... | collective-permute-start | bytes 196616 | tf_op jit(solution)/shard_map/key_value_grads_out/ppermute | solution.py:36
  136.0 1.4 copy-start.4
  136.0 4.4 %collective-permute-start.18 = (bf16[128,256]{1,0:T(8,128)(2,1)S(1)}, bf16[128,256]{1,0:T(8,128)(2,1)S(1)}, u32[]{:S(2)}, u32[]{:S(2)}) collective-permute-start(bf16[128,256]{1,0:T(8,128)(2,1)S(1)} %get-tuple-element.51), channel_id=1, source_target_pairs={{0,24},{1,25},{2,26},{3,27},{4,28},{5,29},{6,30},{7,31},{8,0},{9,1... | collective-permute-start | bytes 196616 | tf_op jit(solution)/shard_map/key_value_grads_out/ppermute | solution.py:36
  137.3 0.7 copy-start.5
  137.3 0.8 copy-start.6
  140.4 0.6 copy-start.7
  140.4 0.6 copy-start.8
  140.4 0.6 copy-start.9
Sparse Core Ops, SparseCore 0:
  21.8 43.6 all-gather.1
  87.5 42.7 reduce-scatter.1

commit v2 on v1

v2 whole, which is shorter than its diff:
```python
import functools
import math

import jax
import jax.numpy as jnp
from jax import lax
from jax.experimental import pallas as pl
from jax.experimental.pallas import tpu as pltpu
from jax.sharding import PartitionSpec as P

HEADS = 4
GROUP = 8
DIM = 128
TOK = 128
SLOT = 64
ROWS = GROUP * SLOT
DOCS = 16
NY = 4
NZ = 8
SECTIONS = 8
ALL = TOK * NY * NZ
BLOCKS = 2 * NY
TILE = 256
PACE = 2
QUERY_STEP = 2
GRAD_STEP = 3
BACK_STEP = 3
WINDOW = 1024
MAX_TILES = 5
MAX_VISITS = 48
VISITS = 64
VISIT_BLOCK = 80
VISIT_TILE = VISIT_BLOCK + MAX_VISITS
VISIT_SLOT = VISIT_TILE + MAX_VISITS
VISIT_FIRST = VISIT_SLOT + MAX_VISITS
PLAN_SIZE = VISIT_FIRST + MAX_VISITS
SCALE = 1.0 / math.sqrt(DIM)
LOG2E = 1.4426950408889634
LOW = -1e30
WIDE = GROUP * DIM
EXTRA = 32
GRAD_ROWS = 2 * ROWS + 2 * (ROWS // DIM) * (EXTRA // 2)
OFFSETS = tuple(range(-(NZ // 2), NZ // 2))

NT = (((1,), (1,)), ((), ()))
NN = (((1,), (0,)), ((), ()))


def along_y(x, by):
    return lax.ppermute(
        x, "ctx", [(c, (c // NZ + by) % NY * NZ + c % NZ) for c in range(NY * NZ)]
    )


def along_z(x, by):
    return lax.ppermute(
        x, "ctx", [(c, c // NZ * NZ + (c % NZ + by) % NZ) for c in range(NY * NZ)]
    )


def together(*arrays):
    return lax.optimization_barrier(arrays)


def gather_z(x, query_pieces, packed, send):
    right = left = x
    pieces = {0: x}
    for step in range(1, NZ // 2 + 1):
        right = along_z(right, 1)
        if step < NZ // 2:
            left = along_z(left, -1)
            held = [right, left]
            if step == 1:
                held += packed
            if step == QUERY_STEP:
                held += query_pieces
            if step == GRAD_STEP:
                held += grad_pieces
            right, left, *held = together(*held)
            if step == 1:
                plan, grad_pieces = held[:2], send(held[2 : 2 + NY])
                held = held[2 + NY :]
            if step == QUERY_STEP:
                query_pieces, held = held[:NY], held[NY:]
            if step == GRAD_STEP:
                grad_pieces = held
            pieces[step] = left
        pieces[-step] = right
    return [pieces[off] for off in OFFSETS], query_pieces, plan, grad_pieces


def add_low(moving, own):
    return (moving.astype(jnp.float32) + own).astype(jnp.bfloat16)


def sum_z(parts, queries):
    parts = dict(zip(OFFSETS, parts))
    half = NZ // 2
    left, right = parts[-half], parts[half - 1]
    for step in range(1, half + 1):
        left = along_z(left, -1)
        if step < half:
            right = along_z(right, 1)
            if step == BACK_STEP:
                left, right, *queries = together(left, right, *queries)
            else:
                left, right = together(left, right)
            left = add_low(left, parts[step - half])
            if step < half - 1:
                right = add_low(right, parts[half - 1 - step])
    total = parts[0] + left.astype(jnp.float32) + right.astype(jnp.float32)
    return total.astype(jnp.bfloat16), queries


def dot(a, b, dims):
    return lax.dot_general(a, b, dims, preferred_element_type=jnp.float32)


def whole(count):
    return [pl.BlockSpec(memory_space=pltpu.VMEM)] * count


def scalars():
    return pl.BlockSpec(memory_space=pltpu.SMEM)


def params(mib):
    return pltpu.CompilerParams(vmem_limit_bytes=mib << 20)


def own_y():
    return lax.axis_index("ctx") // NZ


def column(y, k, width):
    return pl.ds(pl.multiple_of(lax.rem(y + k, NY) * width, width), width)


def pack_kv_body(key, value, *outs):
    y = own_y()
    for k in range(NY):
        outs[k][:, :DIM] = key[:, column(y, k, DIM)]
        outs[k][:, DIM:] = value[:, column(y, k, DIM)]


def pack_kv(key, value):
    return pl.pallas_call(
        pack_kv_body,
        out_shape=[jax.ShapeDtypeStruct((TOK, 2 * DIM), jnp.bfloat16)] * NY,
        in_specs=whole(2),
        out_specs=whole(NY),
        name="pack_kv",
    )(key, value)


def stacked(piece, s):
    rows = slice(s * SLOT, (s + 1) * SLOT)
    return jnp.concatenate([piece[rows, h * DIM : (h + 1) * DIM] for h in range(GROUP)], axis=0)


def pack_queries_body(x, *outs):
    y = own_y()
    for k in range(NY):
        piece = x[:, column(y, k, WIDE)]
        for s in range(2):
            outs[k][s * ROWS : (s + 1) * ROWS, :] = stacked(piece, s)


def pack_queries(x):
    return pl.pallas_call(
        pack_queries_body,
        out_shape=[jax.ShapeDtypeStruct((2 * ROWS, DIM), jnp.bfloat16)] * NY,
        in_specs=whole(1),
        out_specs=whole(NY),
        name="pack_queries",
    )(x)


def pack_grads_body(grad, out, *outs):
    y = own_y()
    ones = jnp.ones((EXTRA // 2, DIM), jnp.bfloat16)
    line = lax.broadcasted_iota(jnp.int32, (EXTRA // 2, DIM), 0)
    for k in range(NY):
        columns = column(y, k, WIDE)
        piece = grad[:, columns]
        product = piece.astype(jnp.float32) * out[:, columns].astype(jnp.float32)
        high = product.astype(jnp.bfloat16)
        low = (product - high.astype(jnp.float32)).astype(jnp.bfloat16)
        for s in range(2):
            outs[k][s * ROWS : (s + 1) * ROWS, :] = stacked(piece, s)
            delta = dot(ones, stacked(high, s), NT) + dot(ones, stacked(low, s), NT)
            for c in range(ROWS // DIM):
                part = delta[:, c * DIM : (c + 1) * DIM]
                first = part.astype(jnp.bfloat16).astype(jnp.float32)
                second = (part - first).astype(jnp.bfloat16).astype(jnp.float32)
                third = part - first - second
                coded = jnp.where(line == 0, first, jnp.where(line == 1, second, third))
                at = 2 * ROWS + (s * (ROWS // DIM) + c) * (EXTRA // 2)
                outs[k][at : at + EXTRA // 2, :] = coded.astype(jnp.bfloat16)


def pack_grads(grad, out):
    return pl.pallas_call(
        pack_grads_body,
        out_shape=[jax.ShapeDtypeStruct((GRAD_ROWS, DIM), jnp.bfloat16)] * NY,
        in_specs=whole(2),
        out_specs=whole(NY),
        name="pack_grads",
    )(grad, out)


def plan_body(pairs, lengths, plan, starts):
    own = lax.axis_index("ctx")
    y, z = own // NZ, lax.rem(own, NZ)

    def block_at(zi, yr, s):
        pid = pairs[0, lax.rem(y + NY - yr, NY) * NZ + zi]
        return pid if s == 0 else 2 * NY * NZ - 1 - pid

    for n, off in enumerate(OFFSETS):
        for yr in range(NY):
            for s in range(2):
                plan[(n * NY + yr) * 2 + s] = block_at(lax.rem(z + NZ + off, NZ), yr, s) * SLOT

    ends = []
    for i in range(DOCS):
        ends.append(lengths[0, i] + (ends[-1] if ends else 0))

    def start_of(pos):
        start = jnp.zeros_like(pos)
        for end in ends:
            start = jnp.where(end <= pos, end, start)
        return start

    lane = lax.broadcasted_iota(jnp.int32, (BLOCKS, ROWS), 1) & (SLOT - 1)
    line = lax.broadcasted_iota(jnp.int32, (BLOCKS, ROWS), 0)
    firsts = jnp.zeros((BLOCKS, ROWS), jnp.int32)
    count = jnp.int32(0)
    for i in range(BLOCKS):
        first = block_at(z, i // 2, i % 2) * SLOT
        firsts = jnp.where(line == i, first, firsts)
        low_tile = start_of(first) // TILE
        high_tile = (first + SLOT - 1) // TILE + 1

        def list_tile(t, n, i=i, first=first, low_tile=low_tile):
            plan[VISIT_BLOCK + n] = i
            plan[VISIT_TILE + n] = t
            plan[VISIT_SLOT + n] = t - low_tile
            plan[VISIT_FIRST + n] = first
            return n + 1

        count = lax.fori_loop(low_tile, high_tile, list_tile, count)
    for extra in range(PACE - 1):
        plan[VISIT_BLOCK + count + extra] = 0
        plan[VISIT_TILE + count + extra] = 0
        plan[VISIT_SLOT + count + extra] = MAX_TILES
        plan[VISIT_FIRST + count + extra] = 0
    plan[VISITS] = count
    starts[...] = start_of(firsts + lane)


def make_plan(pairs, lengths):
    return pl.pallas_call(
        plan_body,
        out_shape=[
            jax.ShapeDtypeStruct((PLAN_SIZE,), jnp.int32),
            jax.ShapeDtypeStruct((BLOCKS, ROWS), jnp.int32),
        ],
        in_specs=[scalars(), scalars()],
        out_specs=[scalars(), pl.BlockSpec(memory_space=pltpu.VMEM)],
        name="make_plan",
    )(pairs, lengths)


def main_body(plan, starts, *refs):
    queries, grads, gathered = refs[0:NY], refs[NY : 2 * NY], refs[2 * NY : 2 * NY + NZ]
    query_outs = refs[2 * NY + NZ : 3 * NY + NZ]
    kv_outs = refs[3 * NY + NZ : 3 * NY + 2 * NZ]
    keys, values, keys_t, key_acc, value_acc, scores, tops, sums, query_acc = refs[
        3 * NY + 2 * NZ : 3 * NY + 2 * NZ + 9
    ]
    q_rows, g_rows, d_rows, sems = refs[3 * NY + 2 * NZ + 9 :]

    loads = [pltpu.make_async_copy(queries[k], q_rows.at[k], sems.at[k]) for k in range(NY)]
    loads += [pltpu.make_async_copy(grads[k], g_rows.at[k], sems.at[NY + k]) for k in range(NY)]
    for load in loads:
        load.start()

    def sorted_rows(n, yr, s):
        return pl.ds(pl.multiple_of(plan[(n * NY + yr) * 2 + s], SLOT), SLOT)

    for n, piece in enumerate(gathered):
        for yr in range(NY):
            for s in range(2):
                dst = sorted_rows(n, yr, s)
                src = slice(yr * TOK + s * SLOT, yr * TOK + (s + 1) * SLOT)
                keys[dst, :] = piece[src, :DIM]
                values[dst, :] = piece[src, DIM:]

    for t in range(ALL // TILE):
        keys_t[t] = keys[t * TILE : (t + 1) * TILE, :].T
    key_acc[...] = jnp.zeros_like(key_acc)
    value_acc[...] = jnp.zeros_like(value_acc)
    query_acc[...] = jnp.zeros_like(query_acc)
    tops[...] = jnp.full_like(tops, LOW)
    sums[...] = jnp.zeros_like(sums)

    lane = lax.broadcasted_iota(jnp.int32, (1, ROWS), 1) & (SLOT - 1)
    for load in loads:
        load.wait()
    for i in range(BLOCKS):
        for c in range(ROWS // DIM):
            at = 2 * ROWS + ((i % 2) * (ROWS // DIM) + c) * (EXTRA // 2)
            coded = g_rows[i // 2, at : at + EXTRA // 2, :].astype(jnp.float32)
            d_rows[i : i + 1, c * DIM : (c + 1) * DIM] = coded[0:1] + coded[1:2] + coded[2:3]

    def place_of(v):
        i = plan[VISIT_BLOCK + v]
        return i, i // 2, pl.ds(pl.multiple_of(lax.rem(i, 2) * ROWS, ROWS), ROWS)

    def score_step(n, carry):
        raw = []
        for u in range(PACE):
            v = n * PACE + u
            i, yr, own = place_of(v)
            t = plan[VISIT_TILE + v]
            kt = keys[pl.ds(pl.multiple_of(t * TILE, TILE), TILE), :]
            raw.append(dot(kt, q_rows[yr, own, :], NT))
        for u, st in enumerate(raw):
            v = n * PACE + u
            i, slot = plan[VISIT_BLOCK + v], plan[VISIT_SLOT + v]
            k_pos = plan[VISIT_TILE + v] * TILE + lax.broadcasted_iota(jnp.int32, (TILE, ROWS), 0)
            q_pos = plan[VISIT_FIRST + v] + lane
            st = jnp.where((k_pos <= q_pos) & (k_pos >= starts[pl.ds(i, 1), :]), st, LOW)
            top = jnp.max(st, axis=0, keepdims=True)
            e = jnp.exp2((st - top) * (SCALE * LOG2E))
            scores[v] = e
            tops[slot, pl.ds(i, 1), :] = top
            sums[slot, pl.ds(i, 1), :] = jnp.sum(e, axis=0, keepdims=True)
        return carry

    steps = (plan[VISITS] + PACE - 1) // PACE
    lax.fori_loop(0, steps, score_step, 0)

    found = tops[:MAX_TILES]
    weights = jnp.exp2((found - jnp.max(found, axis=0, keepdims=True)) * (SCALE * LOG2E))
    total = jnp.sum(weights * sums[:MAX_TILES], axis=0, keepdims=True)
    tops[:MAX_TILES] = weights * (1.0 / total)
    tops[MAX_TILES] = jnp.zeros((BLOCKS, ROWS), jnp.float32)

    def grad_step(n, carry):
        low_pairs = []
        for u in range(PACE):
            v = n * PACE + u
            i, yr, own = place_of(v)
            rows = pl.ds(pl.multiple_of(plan[VISIT_TILE + v] * TILE, TILE), TILE)
            dprob = dot(values[rows, :], g_rows[yr, own, :], NT)
            prob = scores[v] * tops[plan[VISIT_SLOT + v], pl.ds(i, 1), :]
            dscore = prob * (dprob - d_rows[pl.ds(i, 1), :])
            low_pairs.append((prob.astype(jnp.bfloat16), dscore.astype(jnp.bfloat16)))
        terms = []
        for u, (prob, dscore) in enumerate(low_pairs):
            v = n * PACE + u
            i, yr, own = place_of(v)
            terms.append(
                (
                    dot(prob, g_rows[yr, own, :], NN),
                    dot(dscore, q_rows[yr, own, :], NN),
                    dot(keys_t[plan[VISIT_TILE + v]], dscore, NN),
                )
            )
        for u, (value_term, key_term, query_term) in enumerate(terms):
            v = n * PACE + u
            rows = pl.ds(pl.multiple_of(plan[VISIT_TILE + v] * TILE, TILE), TILE)
            value_acc[rows, :] += value_term
            key_acc[rows, :] += key_term
            query_acc[plan[VISIT_BLOCK + v]] += query_term
        return carry

    lax.fori_loop(0, steps, grad_step, 0)

    for i in range(BLOCKS):
        own = slice((i % 2) * ROWS, (i % 2 + 1) * ROWS)
        q_rows[i // 2, own, :] = (query_acc[i] * SCALE).astype(jnp.bfloat16).T

    stores = [
        pltpu.make_async_copy(q_rows.at[k], query_outs[k], sems.at[k]) for k in range(NY)
    ]
    for store in stores:
        store.start()
    for n, piece in enumerate(kv_outs):
        for yr in range(NY):
            for s in range(2):
                src = sorted_rows(n, yr, s)
                dst = slice(yr * TOK + s * SLOT, yr * TOK + (s + 1) * SLOT)
                piece[dst, :DIM] = (key_acc[src, :] * SCALE).astype(piece.dtype)
                piece[dst, DIM:] = value_acc[src, :].astype(piece.dtype)
    for store in stores:
        store.wait()


def attention_grads(plan, queries, grads, gathered):
    bf16, f32 = jnp.bfloat16, jnp.float32
    anywhere = pl.BlockSpec(memory_space=pl.ANY)
    return pl.pallas_call(
        main_body,
        out_shape=[jax.ShapeDtypeStruct((2 * ROWS, DIM), bf16)] * NY
        + [
            jax.ShapeDtypeStruct(
                (NY * TOK, 2 * DIM), bf16 if off in (NZ // 2 - 1, -(NZ // 2)) else f32
            )
            for off in OFFSETS
        ],
        in_specs=[scalars()] + whole(1) + [anywhere] * (2 * NY) + whole(NZ),
        out_specs=[anywhere] * NY + whole(NZ),
        scratch_shapes=[
            pltpu.VMEM((ALL, DIM), bf16),
            pltpu.VMEM((ALL, DIM), bf16),
            pltpu.VMEM((ALL // TILE, DIM, TILE), bf16),
            pltpu.VMEM((ALL, DIM), f32),
            pltpu.VMEM((ALL, DIM), f32),
            pltpu.VMEM((BLOCKS * MAX_TILES + PACE, TILE, ROWS), f32),
            pltpu.VMEM((MAX_TILES + 1, BLOCKS, ROWS), f32),
            pltpu.VMEM((MAX_TILES + 1, BLOCKS, ROWS), f32),
            pltpu.VMEM((BLOCKS, DIM, ROWS), f32),
            pltpu.VMEM((NY, 2 * ROWS, DIM), bf16),
            pltpu.VMEM((NY, GRAD_ROWS, DIM), bf16),
            pltpu.VMEM((BLOCKS, ROWS), f32),
            pltpu.SemaphoreType.DMA((2 * NY,)),
        ],
        compiler_params=params(40),
        name="attention_grads",
    )(*plan, *queries, *grads, *gathered)


def place_wide_body(*refs):
    y = own_y()
    for k in range(NY):
        start = lax.rem(y + k, NY) * WIDE
        for s in range(2):
            for h in range(GROUP):
                refs[NY][
                    s * SLOT : (s + 1) * SLOT,
                    pl.ds(pl.multiple_of(start + h * DIM, DIM), DIM),
                ] = refs[k][s * ROWS + h * SLOT : s * ROWS + (h + 1) * SLOT, :]


def place_wide(pieces):
    return pl.pallas_call(
        place_wide_body,
        out_shape=jax.ShapeDtypeStruct((TOK, HEADS * WIDE), jnp.bfloat16),
        in_specs=whole(NY),
        out_specs=pl.BlockSpec(memory_space=pltpu.VMEM),
        name="place_wide",
    )(*pieces)


def place_kv_body(*refs):
    y = own_y()
    for k in range(NY):
        refs[NY][:, column(y, k, DIM)] = refs[k][:, :DIM]
        refs[NY + 1][:, column(y, k, DIM)] = refs[k][:, DIM:]


def place_kv(pieces):
    return pl.pallas_call(
        place_kv_body,
        out_shape=[jax.ShapeDtypeStruct((TOK, HEADS * DIM), jnp.bfloat16)] * 2,
        in_specs=whole(NY),
        out_specs=whole(2),
        name="place_kv",
    )(*pieces)


def per_device(
    queries, key_projection, value_projection, forward_out, incoming, doc_lengths, pair_of
):
    def to_heads(pieces, move):
        return [pieces[0]] + [move(pieces[k], k) for k in range(1, NY)]

    with jax.named_scope("grads_shift"):
        out_grad = lax.ppermute(
            incoming[0], "pipe", [(p, (p - 1) % SECTIONS) for p in range(SECTIONS)]
        )
    with jax.named_scope("keys_values_in"):
        kv = to_heads(pack_kv(key_projection[0], value_projection[0]), along_y)
        packed_queries = pack_queries(queries[0])
        *kv, first, second, third, fourth = together(*kv, *packed_queries)
        packed_queries = [first, second, third, fourth]
        kv = jnp.concatenate(kv, axis=0)
    with jax.named_scope("queries_in"):
        query_pieces = to_heads(packed_queries, along_y)
    with jax.named_scope("plan"):
        plan = make_plan(pair_of, doc_lengths)
    with jax.named_scope("grads_pack"):
        packed_grads = pack_grads(out_grad, forward_out[0])
    with jax.named_scope("keys_values_ring"):
        gathered, query_pieces, plan, grad_pieces = gather_z(
            kv, query_pieces, [*plan, *packed_grads], lambda x: to_heads(x, along_y)
        )
    parts = attention_grads(plan, query_pieces, grad_pieces, gathered)
    query_parts, kv_parts = parts[:NY], parts[NY:]
    with jax.named_scope("query_grads_out"):
        query_parts = to_heads(query_parts, lambda x, k: along_y(x, -k))
    with jax.named_scope("key_value_grads_ring"):
        kv_sum, query_parts = sum_z(kv_parts, query_parts)
    with jax.named_scope("query_grads_place"):
        query_grad = place_wide(query_parts)
    with jax.named_scope("key_value_grads_out"):
        kv_pieces = [kv_sum[k * TOK : (k + 1) * TOK] for k in range(NY)]
        key_gradient, value_gradient = place_kv(
            to_heads(kv_pieces, lambda x, k: along_y(x, -k))
        )
    return query_grad[None], key_gradient[None], value_gradient[None]


def solution(mesh):
    tokens = P("pipe", "ctx", None)
    return jax.shard_map(
        per_device,
        mesh=mesh,
        in_specs=(tokens,) * 5 + (P("pipe", None),) * 2,
        out_specs=(tokens,) * 3,
        check_vma=False,
    )
```

time: 151 us -> 121 us (0.80)
  the two profiles are of different devices: /device:TPU:2 before, /device:TPU:6 now
where the time goes in v2:
time: 121 us; the launch traced here: 122 us
  starting transfers between devices  47.9 us (40%)
  waiting for transfers between devices  42.7 us (35%)
  Pallas kernels  26.9 us (22%)
  local copies, waits for them, and re-layouts  2.89 us (2%)
    ppermute x14, waiting for transfers between devices, along_z(): lax.ppermute(x, 'ctx', [(c, c // NZ * NZ + (c % NZ + by) % NZ) for c in r...  24.6 us
    ppermute x15, starting transfers between devices, along_y(): lax.ppermute(x, 'ctx', [(c, (c // NZ + by) % NY * NZ + c % NZ) for c in r...  23.9 us
    ppermute x14, starting transfers between devices, along_z(): lax.ppermute(x, 'ctx', [(c, c // NZ * NZ + (c % NZ + by) % NZ) for c in r...  23.6 us
    ppermute x15, waiting for transfers between devices, along_y(): lax.ppermute(x, 'ctx', [(c, (c // NZ + by) % NY * NZ + c % NZ) for c in r...  18 us
    pallas_call x1, Pallas kernels, attention_grads(): pl.pallas_call(main_body, out_shape=[jax.ShapeDtypeStruct((2 * ROWS, DIM)...  14 us
    pallas_call x1, Pallas kernels, pack_grads(): pl.pallas_call(pack_grads_body, out_shape=[jax.ShapeDtypeStruct((GRAD_ROW...  3.03 us
    pallas_call x1, Pallas kernels, place_wide(): pl.pallas_call(place_wide_body, out_shape=jax.ShapeDtypeStruct((TOK, HEAD...  2.44 us
  transfers between devices with their start and end apart: 30, of which 15 were waited for; matrix products, arithmetic and copies ran while one was open for 0% of the time, Pallas kernels for 9%

profile of v2, /device:TPU:6, one launch (start us, length us, event | category | flops | bytes accessed | tf_op | source)
XLA Modules:
  0.0 121.5 jit_solution(4218567430548155651)
XLA Ops:
  0.6 0.3 collective-permute-start.5
  0.9 1.7 %pack_kv.1 = (bf16[128,256]{1,0:T(8,128)(2,1)}, bf16[128,256]{1,0:T(8,128)(2,1)}, bf16[128,256]{1,0:T(8,128)(2,1)}, bf16[128,256]{1,0:T(8,128)(2,1)}) custom-call(bf16[128,512]{1,0:T(8,128)(2,1)} %bitcast.11, bf16[128,512]{1,0:T(8,128)(2,1)} %bitcast.12), custom_call_target="tpu_custom_call" | custom-call | tf_op jit(solution)/shard_map/keys_values_in/pack_kv/pallas_call | solution.py:147
  2.6 1.6 %collective-permute-start = (bf16[128,256]{1,0:T(8,128)(2,1)}, bf16[128,256]{1,0:T(8,128)(2,1)S(1)}, u32[]{:S(2)}, u32[]{:S(2)}) collective-permute-start(bf16[128,256]{1,0:T(8,128)(2,1)} %get-tuple-element.70), channel_id=1, source_target_pairs={{0,8},{1,9},{2,10},{3,11},{4,12},{5,13},{6,14},{7,15},{8,16},{9,17... | collective-permute-start | bytes 196616 | tf_op jit(solution)/shard_map/keys_values_in/ppermute | solution.py:50
  4.2 2.9 %collective-permute-start.1 = (bf16[128,256]{1,0:T(8,128)(2,1)}, bf16[128,256]{1,0:T(8,128)(2,1)S(1)}, u32[]{:S(2)}, u32[]{:S(2)}) collective-permute-start(bf16[128,256]{1,0:T(8,128)(2,1)} %get-tuple-element.71), channel_id=1, source_target_pairs={{0,16},{1,17},{2,18},{3,19},{4,20},{5,21},{6,22},{7,23},{8,24},{9,... | collective-permute-start | bytes 196616 | tf_op jit(solution)/shard_map/keys_values_in/ppermute | solution.py:50
  7.1 1.3 %collective-permute-start.2 = (bf16[128,256]{1,0:T(8,128)(2,1)}, bf16[128,256]{1,0:T(8,128)(2,1)S(1)}, u32[]{:S(2)}, u32[]{:S(2)}) collective-permute-start(bf16[128,256]{1,0:T(8,128)(2,1)} %get-tuple-element.72), channel_id=1, source_target_pairs={{0,24},{1,25},{2,26},{3,27},{4,28},{5,29},{6,30},{7,31},{8,0},{9,1... | collective-permute-start | bytes 196616 | tf_op jit(solution)/shard_map/keys_values_in/ppermute | solution.py:50
  8.4 2.2 %pack_queries.1 = (bf16[1024,128]{1,0:T(8,128)(2,1)}, bf16[1024,128]{1,0:T(8,128)(2,1)}, bf16[1024,128]{1,0:T(8,128)(2,1)}, bf16[1024,128]{1,0:T(8,128)(2,1)}) custom-call(bf16[128,4096]{1,0:T(8,128)(2,1)} %bitcast.8), custom_call_target="tpu_custom_call" | custom-call | tf_op jit(solution)/shard_map/keys_values_in/pack_queries/pallas_call | solution.py:170
  10.9 0.6 collective-permute-done.2
  11.6 5.9 %collective-permute-start.4 = (bf16[512,256]{1,0:T(8,128)(2,1)S(1)}, bf16[512,256]{1,0:T(8,128)(2,1)S(1)}, u32[]{:S(2)}, u32[]{:S(2)}) collective-permute-start(bf16[512,256]{1,0:T(8,128)(2,1)S(1)} %constant_dynamic-update-slice_fusion.refs_12_), channel_id=1, source_target_pairs={{0,7},{1,0},{2,1},{3,2},{4,3},{5,4},{6,5},{7,6},{8,15},{9,8},{10,9... | collective-permute-start | bytes 786440 | tf_op jit(solution)/shard_map/keys_values_ring/ppermute | solution.py:56
  17.5 0.6 collective-permute-start.8
  18.1 3.4 %collective-permute-start.9 = (bf16[1024,128]{1,0:T(8,128)(2,1)S(1)}, bf16[1024,128]{1,0:T(8,128)(2,1)S(1)}, u32[]{:S(2)}, u32[]{:S(2)}) collective-permute-start(bf16[1024,128]{1,0:T(8,128)(2,1)S(1)} %copy-done.14), channel_id=1, source_target_pairs={{0,16},{1,17},{2,18},{3,19},{4,20},{5,21},{6,22},{7,23},{8,24},{9,... | collective-permute-start | bytes 786440 | tf_op jit(solution)/shard_map/queries_in/ppermute | solution.py:50
  21.6 0.6 collective-permute-start.10
  22.1 1.8 %make_plan.1 = (s32[272]{0:T(512)}, s32[8,512]{1,0:T(8,128)}) custom-call(s32[1,32]{1,0:T(1,128)} %pairs.1, s32[1,16]{1,0:T(1,128)} %lengths.1), custom_call_target="tpu_custom_call" | custom-call | tf_op jit(solution)/shard_map/plan/make_plan/pallas_call | solution.py:263
  24.0 3.0 %pack_grads.1 = (bf16[1152,128]{1,0:T(8,128)(2,1)}, bf16[1152,128]{1,0:T(8,128)(2,1)}, bf16[1152,128]{1,0:T(8,128)(2,1)}, bf16[1152,128]{1,0:T(8,128)(2,1)}) custom-call(bf16[128,4096]{1,0:T(8,128)(2,1)} %copy-done.5, bf16[128,4096]{1,0:T(8,128)(2,1)} %bitcast.9), custom_call_target="tpu_custom_call" | custom-call | tf_op jit(solution)/shard_map/grads_pack/pack_grads/pallas_call | solution.py:203
  27.1 3.3 %collective-permute-start.7 = (bf16[512,256]{1,0:T(8,128)(2,1)S(1)}, bf16[512,256]{1,0:T(8,128)(2,1)S(1)}, u32[]{:S(2)}, u32[]{:S(2)}) collective-permute-start(bf16[512,256]{1,0:T(8,128)(2,1)S(1)} %collective-permute-done.4.refs_13_), channel_id=1, source_target_pairs={{0,7},{1,0},{2,1},{3,2},{4,3},{5,4},{6,5},{7,6},{8,15},{9,8},{10,9... | collective-permute-start | bytes 786440 | tf_op jit(solution)/shard_map/keys_values_ring/ppermute | solution.py:56
  30.5 1.5 %collective-permute-start.13 = (bf16[1152,128]{1,0:T(8,128)(2,1)}, bf16[1152,128]{1,0:T(8,128)(2,1)S(1)}, u32[]{:S(2)}, u32[]{:S(2)}) collective-permute-start(bf16[1152,128]{1,0:T(8,128)(2,1)} %get-tuple-element.102), channel_id=1, source_target_pairs={{0,8},{1,9},{2,10},{3,11},{4,12},{5,13},{6,14},{7,15},{8,16},{9,17... | collective-permute-start | bytes 884744 | tf_op jit(solution)/shard_map/keys_values_ring/ppermute | solution.py:50
  32.0 0.5 collective-permute-start.14
  32.5 2.4 %collective-permute-start.15 = (bf16[1152,128]{1,0:T(8,128)(2,1)}, bf16[1152,128]{1,0:T(8,128)(2,1)S(1)}, u32[]{:S(2)}, u32[]{:S(2)}) collective-permute-start(bf16[1152,128]{1,0:T(8,128)(2,1)} %get-tuple-element.104), channel_id=1, source_target_pairs={{0,24},{1,25},{2,26},{3,27},{4,28},{5,29},{6,30},{7,31},{8,0},{9,1... | collective-permute-start | bytes 884744 | tf_op jit(solution)/shard_map/keys_values_ring/ppermute | solution.py:50
  34.9 1.6 %collective-permute-done.6.refs_10_ = bf16[512,256]{1,0:T(8,128)(2,1)S(1)} collective-permute-done((bf16[512,256]{1,0:T(8,128)(2,1)S(1)}, bf16[512,256]{1,0:T(8,128)(2,1)S(1)}, u32[]{:S(2)}, u32[]{:S(2)}) %collective-permute-start.6) | collective-permute-done | bytes 262176 | tf_op jit(solution)/shard_map/keys_values_ring/ppermute | solution.py:56
  36.5 3.2 %collective-permute-start.12 = (bf16[512,256]{1,0:T(8,128)(2,1)S(1)}, bf16[512,256]{1,0:T(8,128)(2,1)S(1)}, u32[]{:S(2)}, u32[]{:S(2)}) collective-permute-start(bf16[512,256]{1,0:T(8,128)(2,1)S(1)} %collective-permute-done.7.refs_14_), channel_id=1, source_target_pairs={{0,7},{1,0},{2,1},{3,2},{4,3},{5,4},{6,5},{7,6},{8,15},{9,8},{10,9... | collective-permute-start | bytes 786440 | tf_op jit(solution)/shard_map/keys_values_ring/ppermute | solution.py:56
  39.7 6.8 %collective-permute-done.13.refs_5_ = bf16[1152,128]{1,0:T(8,128)(2,1)S(1)} collective-permute-done((bf16[1152,128]{1,0:T(8,128)(2,1)}, bf16[1152,128]{1,0:T(8,128)(2,1)S(1)}, u32[]{:S(2)}, u32[]{:S(2)}) %collective-permute-start.13) | collective-permute-done | bytes 294944 | tf_op jit(solution)/shard_map/keys_values_ring/ppermute | solution.py:50
  46.5 0.6 collective-permute-done.15.refs_7_
  47.1 1.0 collective-permute-start.16
  48.1 7.5 %collective-permute-done.16.refs_8_ = bf16[512,256]{1,0:T(8,128)(2,1)S(1)} collective-permute-done((bf16[512,256]{1,0:T(8,128)(2,1)S(1)}, bf16[512,256]{1,0:T(8,128)(2,1)S(1)}, u32[]{:S(2)}, u32[]{:S(2)}) %collective-permute-start.16) | collective-permute-done | bytes 262176 | tf_op jit(solution)/shard_map/keys_values_ring/ppermute | solution.py:56
  55.6 1.0 copy-done
  56.6 14.0 %attention_grads.1 = (bf16[1024,128]{1,0:T(8,128)(2,1)S(1)}, bf16[1024,128]{1,0:T(8,128)(2,1)S(1)}, bf16[1024,128]{1,0:T(8,128)(2,1)S(1)}, bf16[1024,128]{1,0:T(...) custom-call(s32[272]{0:T(512)S(1)} %copy-done.4, ...), custom_call_target="tpu_custom_call" | custom-call | tf_op jit(solution)/shard_map/attention_grads/pallas_call | solution.py:405
  70.6 3.0 %collective-permute-start.17 = (bf16[512,256]{1,0:T(8,128)(2,1)S(1)}, bf16[512,256]{1,0:T(8,128)(2,1)S(1)}, u32[]{:S(2)}, u32[]{:S(2)}) collective-permute-start(bf16[512,256]{1,0:T(8,128)(2,1)S(1)} %get-tuple-element.111), channel_id=1, source_target_pairs={{0,7},{1,0},{2,1},{3,2},{4,3},{5,4},{6,5},{7,6},{8,15},{9,8},{10,9... | collective-permute-start | bytes 786440 | tf_op jit(solution)/shard_map/key_value_grads_ring/ppermute | solution.py:56
  73.6 5.1 %collective-permute-done.17 = bf16[512,256]{1,0:T(8,128)(2,1)S(1)} collective-permute-done((bf16[512,256]{1,0:T(8,128)(2,1)S(1)}, bf16[512,256]{1,0:T(8,128)(2,1)S(1)}, u32[]{:S(2)}, u32[]{:S(2)}) %collective-permute-start.17) | collective-permute-done | bytes 262176 | tf_op jit(solution)/shard_map/key_value_grads_ring/ppermute | solution.py:56
  78.7 3.4 %collective-permute-done.18 = bf16[512,256]{1,0:T(8,128)(2,1)S(1)} collective-permute-done((bf16[512,256]{1,0:T(8,128)(2,1)S(1)}, bf16[512,256]{1,0:T(8,128)(2,1)S(1)}, u32[]{:S(2)}, u32[]{:S(2)}) %collective-permute-start.18) | collective-permute-done | bytes 262176 | tf_op jit(solution)/shard_map/key_value_grads_ring/ppermute | solution.py:56
  82.2 1.2 collective-permute-start.19
  83.5 1.0 collective-permute-start.20
  84.5 4.6 %collective-permute-start.23 = (bf16[1024,128]{1,0:T(8,128)(2,1)S(1)}, bf16[1024,128]{1,0:T(8,128)(2,1)S(1)}, u32[]{:S(2)}, u32[]{:S(2)}) collective-permute-start(bf16[1024,128]{1,0:T(8,128)(2,1)S(1)} %get-tuple-element.122), channel_id=1, source_target_pairs={{0,24},{1,25},{2,26},{3,27},{4,28},{5,29},{6,30},{7,31},{8,0},{9,1... | collective-permute-start | bytes 786440 | tf_op jit(solution)/shard_map/query_grads_out/ppermute | solution.py:50
  89.1 0.9 collective-permute-start.25
  90.0 1.6 %collective-permute-done.20 = bf16[512,256]{1,0:T(8,128)(2,1)S(1)} collective-permute-done((bf16[512,256]{1,0:T(8,128)(2,1)S(1)}, bf16[512,256]{1,0:T(8,128)(2,1)S(1)}, u32[]{:S(2)}, u32[]{:S(2)}) %collective-permute-start.20) | collective-permute-done | bytes 262176 | tf_op jit(solution)/shard_map/key_value_grads_ring/ppermute | solution.py:56
  91.6 1.8 %collective-permute-start.21 = (bf16[512,256]{1,0:T(8,128)(2,1)S(1)}, bf16[512,256]{1,0:T(8,128)(2,1)S(1)}, u32[]{:S(2)}, u32[]{:S(2)}) collective-permute-start(bf16[512,256]{1,0:T(8,128)(2,1)S(1)} %add_convert_fusion.3), channel_id=1, source_target_pairs={{0,7},{1,0},{2,1},{3,2},{4,3},{5,4},{6,5},{7,6},{8,15},{9,8},{10,9... | collective-permute-start | bytes 786440 | tf_op jit(solution)/shard_map/key_value_grads_ring/ppermute | solution.py:56
  93.5 0.4 collective-permute-start.22
  93.9 5.3 %collective-permute-done.23.refs_1_ = bf16[1024,128]{1,0:T(8,128)(2,1)S(1)} collective-permute-done((bf16[1024,128]{1,0:T(8,128)(2,1)S(1)}, bf16[1024,128]{1,0:T(8,128)(2,1)S(1)}, u32[]{:S(2)}, u32[]{:S(2)}) %collective-permute-start.23) | collective-permute-done | bytes 262176 | tf_op jit(solution)/shard_map/query_grads_out/ppermute | solution.py:50
  99.2 0.6 collective-permute-done.24.refs_2_
  99.8 2.8 %collective-permute-done.25.refs_3_ = bf16[1024,128]{1,0:T(8,128)(2,1)S(1)} collective-permute-done((bf16[1024,128]{1,0:T(8,128)(2,1)S(1)}, bf16[1024,128]{1,0:T(8,128)(2,1)S(1)}, u32[]{:S(2)}, u32[]{:S(2)}) %collective-permute-start.25) | collective-permute-done | bytes 262176 | tf_op jit(solution)/shard_map/query_grads_out/ppermute | solution.py:50
  102.7 0.6 copy-done.8
  103.3 2.7 %collective-permute-start.26 = (bf16[512,256]{1,0:T(8,128)(2,1)S(1)}, bf16[512,256]{1,0:T(8,128)(2,1)S(1)}, u32[]{:S(2)}, u32[]{:S(2)}) collective-permute-start(bf16[512,256]{1,0:T(8,128)(2,1)S(1)} %add_convert_fusion.1), channel_id=1, source_target_pairs={{0,7},{1,0},{2,1},{3,2},{4,3},{5,4},{6,5},{7,6},{8,15},{9,8},{10,9... | collective-permute-start | bytes 786440 | tf_op jit(solution)/shard_map/key_value_grads_ring/ppermute | solution.py:56
  106.0 5.4 %collective-permute-done.26 = bf16[512,256]{1,0:T(8,128)(2,1)S(1)} collective-permute-done((bf16[512,256]{1,0:T(8,128)(2,1)S(1)}, bf16[512,256]{1,0:T(8,128)(2,1)S(1)}, u32[]{:S(2)}, u32[]{:S(2)}) %collective-permute-start.26) | collective-permute-done | bytes 262176 | tf_op jit(solution)/shard_map/key_value_grads_ring/ppermute | solution.py:56
  111.5 0.6 fusion
  112.2 2.0 %collective-permute-start.28 = (bf16[128,256]{1,0:T(8,128)(2,1)S(1)}, bf16[128,256]{1,0:T(8,128)(2,1)S(1)}, u32[]{:S(2)}, u32[]{:S(2)}) collective-permute-start(bf16[128,256]{1,0:T(8,128)(2,1)S(1)} %get-tuple-element.136), channel_id=1, source_target_pairs={{0,16},{1,17},{2,18},{3,19},{4,20},{5,21},{6,22},{7,23},{8,24},{9,... | collective-permute-start | bytes 196616 | tf_op jit(solution)/shard_map/key_value_grads_out/ppermute | solution.py:50
  114.2 1.5 %collective-permute-start.27 = (bf16[128,256]{1,0:T(8,128)(2,1)S(1)}, bf16[128,256]{1,0:T(8,128)(2,1)S(1)}, u32[]{:S(2)}, u32[]{:S(2)}) collective-permute-start(bf16[128,256]{1,0:T(8,128)(2,1)S(1)} %get-tuple-element.137), channel_id=1, source_target_pairs={{0,24},{1,25},{2,26},{3,27},{4,28},{5,29},{6,30},{7,31},{8,0},{9,1... | collective-permute-start | bytes 196616 | tf_op jit(solution)/shard_map/key_value_grads_out/ppermute | solution.py:50
  115.7 2.4 %place_wide.1 = bf16[128,4096]{1,0:T(8,128)(2,1)} custom-call(bf16[1024,128]{1,0:T(8,128)(2,1)} %copy-done.1, bf16[1024,128]{1,0:T(8,128)(2,1)} %copy-done.6, bf16[1024,128]{1,0:T(8,128)(2,1)} %copy-done.7, bf16[1024,128]{1,0:T(8,128)(2,1)} %copy-done.8), custom_call_target="tpu_custom_call" | custom-call | tf_op jit(solution)/shard_map/query_grads_place/place_wide/pallas_call | solution.py:449
  118.3 0.8 collective-permute-done.27.refs_1_
  119.2 0.6 copy-done.12
  119.8 1.7 %place_kv.1 = (bf16[128,512]{1,0:T(8,128)(2,1)}, bf16[128,512]{1,0:T(8,128)(2,1)}) custom-call(bf16[128,256]{1,0:T(8,128)(2,1)} %get-tuple-element.138.refs_0_, bf16[128,256]{1,0:T(8,128)(2,1)} %copy-done.12, bf16[128,256]{1,0:T(8,128)(2,1)} %copy-done.11, bf16[128,256]{1,0:T(8,128)(2,1)} %copy-done.10), custom_call_target="tpu_custom_call" | custom-call | tf_op jit(solution)/shard_map/key_value_grads_out/place_kv/pallas_call | solution.py:466
  (60 shorter events, 1.0 us)
Async XLA Ops:
  0.6 20.9 %collective-permute-start.5 = (bf16[128,4096]{1,0:T(8,128)(2,1)}, bf16[128,4096]{1,0:T(8,128)(2,1)S(1)}, u32[]{:S(2)}, u32[]{:S(2)}) collective-permute-start(bf16[128,4096]{1,0:T(8,128)(2,1)} %bitcast.13), channel_id=1, source_target_pairs={{0,224},{32,0},{64,32},{96,64},{128,96},{160,128},{192,160},{224,1... | collective-permute-start | bytes 3145736 | tf_op jit(solution)/shard_map/grads_shift/ppermute | solution.py:482
  2.6 8.1 %collective-permute-start = (bf16[128,256]{1,0:T(8,128)(2,1)}, bf16[128,256]{1,0:T(8,128)(2,1)S(1)}, u32[]{:S(2)}, u32[]{:S(2)}) collective-permute-start(bf16[128,256]{1,0:T(8,128)(2,1)} %get-tuple-element.70), channel_id=1, source_target_pairs={{0,8},{1,9},{2,10},{3,11},{4,12},{5,13},{6,14},{7,15},{8,16},{9,17... | collective-permute-start | bytes 196616 | tf_op jit(solution)/shard_map/keys_values_in/ppermute | solution.py:50
  4.2 6.7 %collective-permute-start.1 = (bf16[128,256]{1,0:T(8,128)(2,1)}, bf16[128,256]{1,0:T(8,128)(2,1)S(1)}, u32[]{:S(2)}, u32[]{:S(2)}) collective-permute-start(bf16[128,256]{1,0:T(8,128)(2,1)} %get-tuple-element.71), channel_id=1, source_target_pairs={{0,16},{1,17},{2,18},{3,19},{4,20},{5,21},{6,22},{7,23},{8,24},{9,... | collective-permute-start | bytes 196616 | tf_op jit(solution)/shard_map/keys_values_in/ppermute | solution.py:50
  7.1 4.5 %collective-permute-start.2 = (bf16[128,256]{1,0:T(8,128)(2,1)}, bf16[128,256]{1,0:T(8,128)(2,1)S(1)}, u32[]{:S(2)}, u32[]{:S(2)}) collective-permute-start(bf16[128,256]{1,0:T(8,128)(2,1)} %get-tuple-element.72), channel_id=1, source_target_pairs={{0,24},{1,25},{2,26},{3,27},{4,28},{5,29},{6,30},{7,31},{8,0},{9,1... | collective-permute-start | bytes 196616 | tf_op jit(solution)/shard_map/keys_values_in/ppermute | solution.py:50
  8.4 3.1 %copy-start.9 = (bf16[128,256]{1,0:T(8,128)(2,1)S(1)}, bf16[128,256]{1,0:T(8,128)(2,1)}, u32[]{:S(2)}) copy-start(bf16[128,256]{1,0:T(8,128)(2,1)} %get-tuple-element.77) | copy-start | bytes 196612
  11.6 6.6 %copy-start.14 = (bf16[1024,128]{1,0:T(8,128)(2,1)S(1)}, bf16[1024,128]{1,0:T(8,128)(2,1)}, u32[]{:S(2)}) copy-start(bf16[1024,128]{1,0:T(8,128)(2,1)} %get-tuple-element.93) | copy-start | bytes 786436
  11.6 10.0 %copy-start.13 = (bf16[1024,128]{1,0:T(8,128)(2,1)S(1)}, bf16[1024,128]{1,0:T(8,128)(2,1)}, u32[]{:S(2)}) copy-start(bf16[1024,128]{1,0:T(8,128)(2,1)} %get-tuple-element.94) | copy-start | bytes 786436
  11.6 15.4 %collective-permute-start.4 = (bf16[512,256]{1,0:T(8,128)(2,1)S(1)}, bf16[512,256]{1,0:T(8,128)(2,1)S(1)}, u32[]{:S(2)}, u32[]{:S(2)}) collective-permute-start(bf16[512,256]{1,0:T(8,128)(2,1)S(1)} %constant_dynamic-update-slice_fusion.refs_12_), channel_id=1, source_target_pairs={{0,7},{1,0},{2,1},{3,2},{4,3},{5,4},{6,5},{7,6},{8,15},{9,8},{10,9... | collective-permute-start | bytes 786440 | tf_op jit(solution)/shard_map/keys_values_ring/ppermute | solution.py:56
  17.5 9.5 %collective-permute-start.3 = (bf16[512,256]{1,0:T(8,128)(2,1)S(1)}, bf16[512,256]{1,0:T(8,128)(2,1)S(1)}, u32[]{:S(2)}, u32[]{:S(2)}) collective-permute-start(bf16[512,256]{1,0:T(8,128)(2,1)S(1)} %constant_dynamic-update-slice_fusion.refs_12_), channel_id=1, source_target_pairs={{0,1},{1,2},{2,3},{3,4},{4,5},{5,6},{6,7},{7,0},{8,9},{9,10},{10,1... | collective-permute-start | bytes 786440 | tf_op jit(solution)/shard_map/keys_values_ring/ppermute | solution.py:56
  17.5 12.9 %collective-permute-start.8 = (bf16[1024,128]{1,0:T(8,128)(2,1)}, bf16[1024,128]{1,0:T(8,128)(2,1)S(1)}, u32[]{:S(2)}, u32[]{:S(2)}) collective-permute-start(bf16[1024,128]{1,0:T(8,128)(2,1)} %get-tuple-element.92), channel_id=1, source_target_pairs={{0,8},{1,9},{2,10},{3,11},{4,12},{5,13},{6,14},{7,15},{8,16},{9,17... | collective-permute-start | bytes 786440 | tf_op jit(solution)/shard_map/queries_in/ppermute | solution.py:50
  18.1 13.9 %collective-permute-start.9 = (bf16[1024,128]{1,0:T(8,128)(2,1)S(1)}, bf16[1024,128]{1,0:T(8,128)(2,1)S(1)}, u32[]{:S(2)}, u32[]{:S(2)}) collective-permute-start(bf16[1024,128]{1,0:T(8,128)(2,1)S(1)} %copy-done.14), channel_id=1, source_target_pairs={{0,16},{1,17},{2,18},{3,19},{4,20},{5,21},{6,22},{7,23},{8,24},{9,... | collective-permute-start | bytes 786440 | tf_op jit(solution)/shard_map/queries_in/ppermute | solution.py:50
  21.6 2.4 %copy-start.5 = (bf16[128,4096]{1,0:T(8,128)(2,1)}, bf16[128,4096]{1,0:T(8,128)(2,1)S(1)}, u32[]{:S(2)}) copy-start(bf16[128,4096]{1,0:T(8,128)(2,1)S(1)} %collective-permute-done.5.grad) | copy-start | bytes 3145732
  21.6 10.9 %collective-permute-start.10 = (bf16[1024,128]{1,0:T(8,128)(2,1)S(1)}, bf16[1024,128]{1,0:T(8,128)(2,1)S(1)}, u32[]{:S(2)}, u32[]{:S(2)}) collective-permute-start(bf16[1024,128]{1,0:T(8,128)(2,1)S(1)} %copy-done.13), channel_id=1, source_target_pairs={{0,24},{1,25},{2,26},{3,27},{4,28},{5,29},{6,30},{7,31},{8,0},{9,1... | collective-permute-start | bytes 786440 | tf_op jit(solution)/shard_map/queries_in/ppermute | solution.py:50
  24.0 31.6 %copy-start.2 = (bf16[1024,128]{1,0:T(8,128)(2,1)S(1)}, bf16[1024,128]{1,0:T(8,128)(2,1)}, u32[]{:S(2)}) copy-start(bf16[1024,128]{1,0:T(8,128)(2,1)} %get-tuple-element.95.refs_0_) | copy-start | bytes 786436
  24.0 31.6 %copy-start.3 = (s32[8,512]{1,0:T(8,128)S(1)}, s32[8,512]{1,0:T(8,128)}, u32[]{:S(2)}) copy-start(s32[8,512]{1,0:T(8,128)} %get-tuple-element.88.starts) | copy-start | bytes 49156
  27.0 28.6 %copy-start.4 = (s32[272]{0:T(512)S(1)}, s32[272]{0:T(512)}, u32[]{:S(2)}) copy-start(s32[272]{0:T(512)} %get-tuple-element.87.plan) | copy-start | bytes 3268
  27.0 9.5 %collective-permute-start.6 = (bf16[512,256]{1,0:T(8,128)(2,1)S(1)}, bf16[512,256]{1,0:T(8,128)(2,1)S(1)}, u32[]{:S(2)}, u32[]{:S(2)}) collective-permute-start(bf16[512,256]{1,0:T(8,128)(2,1)S(1)} %collective-permute-done.3.refs_11_), channel_id=1, source_target_pairs={{0,1},{1,2},{2,3},{3,4},{4,5},{5,6},{6,7},{7,0},{8,9},{9,10},{10,1... | collective-permute-start | bytes 786440 | tf_op jit(solution)/shard_map/keys_values_ring/ppermute | solution.py:56
  27.1 9.4 %collective-permute-start.7 = (bf16[512,256]{1,0:T(8,128)(2,1)S(1)}, bf16[512,256]{1,0:T(8,128)(2,1)S(1)}, u32[]{:S(2)}, u32[]{:S(2)}) collective-permute-start(bf16[512,256]{1,0:T(8,128)(2,1)S(1)} %collective-permute-done.4.refs_13_), channel_id=1, source_target_pairs={{0,7},{1,0},{2,1},{3,2},{4,3},{5,4},{6,5},{7,6},{8,15},{9,8},{10,9... | collective-permute-start | bytes 786440 | tf_op jit(solution)/shard_map/keys_values_ring/ppermute | solution.py:56
  30.5 16.0 %collective-permute-start.13 = (bf16[1152,128]{1,0:T(8,128)(2,1)}, bf16[1152,128]{1,0:T(8,128)(2,1)S(1)}, u32[]{:S(2)}, u32[]{:S(2)}) collective-permute-start(bf16[1152,128]{1,0:T(8,128)(2,1)} %get-tuple-element.102), channel_id=1, source_target_pairs={{0,8},{1,9},{2,10},{3,11},{4,12},{5,13},{6,14},{7,15},{8,16},{9,17... | collective-permute-start | bytes 884744 | tf_op jit(solution)/shard_map/keys_values_ring/ppermute | solution.py:50
  32.0 14.5 %collective-permute-start.14 = (bf16[1152,128]{1,0:T(8,128)(2,1)}, bf16[1152,128]{1,0:T(8,128)(2,1)S(1)}, u32[]{:S(2)}, u32[]{:S(2)}) collective-permute-start(bf16[1152,128]{1,0:T(8,128)(2,1)} %get-tuple-element.103), channel_id=1, source_target_pairs={{0,16},{1,17},{2,18},{3,19},{4,20},{5,21},{6,22},{7,23},{8,24},{9,... | collective-permute-start | bytes 884744 | tf_op jit(solution)/shard_map/keys_values_ring/ppermute | solution.py:50
  32.5 14.6 %collective-permute-start.15 = (bf16[1152,128]{1,0:T(8,128)(2,1)}, bf16[1152,128]{1,0:T(8,128)(2,1)S(1)}, u32[]{:S(2)}, u32[]{:S(2)}) collective-permute-start(bf16[1152,128]{1,0:T(8,128)(2,1)} %get-tuple-element.104), channel_id=1, source_target_pairs={{0,24},{1,25},{2,26},{3,27},{4,28},{5,29},{6,30},{7,31},{8,0},{9,1... | collective-permute-start | bytes 884744 | tf_op jit(solution)/shard_map/keys_values_ring/ppermute | solution.py:50
  36.5 10.6 %collective-permute-start.11 = (bf16[512,256]{1,0:T(8,128)(2,1)S(1)}, bf16[512,256]{1,0:T(8,128)(2,1)S(1)}, u32[]{:S(2)}, u32[]{:S(2)}) collective-permute-start(bf16[512,256]{1,0:T(8,128)(2,1)S(1)} %collective-permute-done.6.refs_10_), channel_id=1, source_target_pairs={{0,1},{1,2},{2,3},{3,4},{4,5},{5,6},{6,7},{7,0},{8,9},{9,10},{10,1... | collective-permute-start | bytes 786440 | tf_op jit(solution)/shard_map/keys_values_ring/ppermute | solution.py:56
  36.5 10.6 %collective-permute-start.12 = (bf16[512,256]{1,0:T(8,128)(2,1)S(1)}, bf16[512,256]{1,0:T(8,128)(2,1)S(1)}, u32[]{:S(2)}, u32[]{:S(2)}) collective-permute-start(bf16[512,256]{1,0:T(8,128)(2,1)S(1)} %collective-permute-done.7.refs_14_), channel_id=1, source_target_pairs={{0,7},{1,0},{2,1},{3,2},{4,3},{5,4},{6,5},{7,6},{8,15},{9,8},{10,9... | collective-permute-start | bytes 786440 | tf_op jit(solution)/shard_map/keys_values_ring/ppermute | solution.py:56
  47.1 8.5 %collective-permute-start.16 = (bf16[512,256]{1,0:T(8,128)(2,1)S(1)}, bf16[512,256]{1,0:T(8,128)(2,1)S(1)}, u32[]{:S(2)}, u32[]{:S(2)}) collective-permute-start(bf16[512,256]{1,0:T(8,128)(2,1)S(1)} %collective-permute-done.11.refs_9_), channel_id=1, source_target_pairs={{0,1},{1,2},{2,3},{3,4},{4,5},{5,6},{6,7},{7,0},{8,9},{9,10},{10,1... | collective-permute-start | bytes 786440 | tf_op jit(solution)/shard_map/keys_values_ring/ppermute | solution.py:56
  55.6 1.0 copy-start
  70.6 11.6 %copy-start.1 = (bf16[1024,128]{1,0:T(8,128)(2,1)}, bf16[1024,128]{1,0:T(8,128)(2,1)S(1)}, u32[]{:S(2)}) copy-start(bf16[1024,128]{1,0:T(8,128)(2,1)S(1)} %get-tuple-element.125.refs_0_) | copy-start | bytes 786436
  70.6 8.1 %collective-permute-start.17 = (bf16[512,256]{1,0:T(8,128)(2,1)S(1)}, bf16[512,256]{1,0:T(8,128)(2,1)S(1)}, u32[]{:S(2)}, u32[]{:S(2)}) collective-permute-start(bf16[512,256]{1,0:T(8,128)(2,1)S(1)} %get-tuple-element.111), channel_id=1, source_target_pairs={{0,7},{1,0},{2,1},{3,2},{4,3},{5,4},{6,5},{7,6},{8,15},{9,8},{10,9... | collective-permute-start | bytes 786440 | tf_op jit(solution)/shard_map/key_value_grads_ring/ppermute | solution.py:56
  73.6 8.5 %collective-permute-start.18 = (bf16[512,256]{1,0:T(8,128)(2,1)S(1)}, bf16[512,256]{1,0:T(8,128)(2,1)S(1)}, u32[]{:S(2)}, u32[]{:S(2)}) collective-permute-start(bf16[512,256]{1,0:T(8,128)(2,1)S(1)} %get-tuple-element.112), channel_id=1, source_target_pairs={{0,1},{1,2},{2,3},{3,4},{4,5},{5,6},{6,7},{7,0},{8,9},{9,10},{10,1... | collective-permute-start | bytes 786440 | tf_op jit(solution)/shard_map/key_value_grads_ring/ppermute | solution.py:56
  82.2 7.7 %collective-permute-start.19 = (bf16[512,256]{1,0:T(8,128)(2,1)S(1)}, bf16[512,256]{1,0:T(8,128)(2,1)S(1)}, u32[]{:S(2)}, u32[]{:S(2)}) collective-permute-start(bf16[512,256]{1,0:T(8,128)(2,1)S(1)} %add_convert_fusion.5), channel_id=1, source_target_pairs={{0,7},{1,0},{2,1},{3,2},{4,3},{5,4},{6,5},{7,6},{8,15},{9,8},{10,9... | collective-permute-start | bytes 786440 | tf_op jit(solution)/shard_map/key_value_grads_ring/ppermute | solution.py:56
  83.5 8.1 %collective-permute-start.20 = (bf16[512,256]{1,0:T(8,128)(2,1)S(1)}, bf16[512,256]{1,0:T(8,128)(2,1)S(1)}, u32[]{:S(2)}, u32[]{:S(2)}) collective-permute-start(bf16[512,256]{1,0:T(8,128)(2,1)S(1)} %add_convert_fusion.4), channel_id=1, source_target_pairs={{0,1},{1,2},{2,3},{3,4},{4,5},{5,6},{6,7},{7,0},{8,9},{9,10},{10,1... | collective-permute-start | bytes 786440 | tf_op jit(solution)/shard_map/key_value_grads_ring/ppermute | solution.py:56
  84.5 14.7 %collective-permute-start.23 = (bf16[1024,128]{1,0:T(8,128)(2,1)S(1)}, bf16[1024,128]{1,0:T(8,128)(2,1)S(1)}, u32[]{:S(2)}, u32[]{:S(2)}) collective-permute-start(bf16[1024,128]{1,0:T(8,128)(2,1)S(1)} %get-tuple-element.122), channel_id=1, source_target_pairs={{0,24},{1,25},{2,26},{3,27},{4,28},{5,29},{6,30},{7,31},{8,0},{9,1... | collective-permute-start | bytes 786440 | tf_op jit(solution)/shard_map/query_grads_out/ppermute | solution.py:50
  89.1 10.7 %collective-permute-start.24 = (bf16[1024,128]{1,0:T(8,128)(2,1)S(1)}, bf16[1024,128]{1,0:T(8,128)(2,1)S(1)}, u32[]{:S(2)}, u32[]{:S(2)}) collective-permute-start(bf16[1024,128]{1,0:T(8,128)(2,1)S(1)} %get-tuple-element.123), channel_id=1, source_target_pairs={{0,16},{1,17},{2,18},{3,19},{4,20},{5,21},{6,22},{7,23},{8,24},{9,... | collective-permute-start | bytes 786440 | tf_op jit(solution)/shard_map/query_grads_out/ppermute | solution.py:50
  89.1 13.5 %collective-permute-start.25 = (bf16[1024,128]{1,0:T(8,128)(2,1)S(1)}, bf16[1024,128]{1,0:T(8,128)(2,1)S(1)}, u32[]{:S(2)}, u32[]{:S(2)}) collective-permute-start(bf16[1024,128]{1,0:T(8,128)(2,1)S(1)} %get-tuple-element.124), channel_id=1, source_target_pairs={{0,8},{1,9},{2,10},{3,11},{4,12},{5,13},{6,14},{7,15},{8,16},{9,17... | collective-permute-start | bytes 786440 | tf_op jit(solution)/shard_map/query_grads_out/ppermute | solution.py:50
  91.6 11.0 %collective-permute-start.21 = (bf16[512,256]{1,0:T(8,128)(2,1)S(1)}, bf16[512,256]{1,0:T(8,128)(2,1)S(1)}, u32[]{:S(2)}, u32[]{:S(2)}) collective-permute-start(bf16[512,256]{1,0:T(8,128)(2,1)S(1)} %add_convert_fusion.3), channel_id=1, source_target_pairs={{0,7},{1,0},{2,1},{3,2},{4,3},{5,4},{6,5},{7,6},{8,15},{9,8},{10,9... | collective-permute-start | bytes 786440 | tf_op jit(solution)/shard_map/key_value_grads_ring/ppermute | solution.py:56
  93.5 9.1 %collective-permute-start.22 = (bf16[512,256]{1,0:T(8,128)(2,1)S(1)}, bf16[512,256]{1,0:T(8,128)(2,1)S(1)}, u32[]{:S(2)}, u32[]{:S(2)}) collective-permute-start(bf16[512,256]{1,0:T(8,128)(2,1)S(1)} %add_convert_fusion.2), channel_id=1, source_target_pairs={{0,1},{1,2},{2,3},{3,4},{4,5},{5,6},{6,7},{7,0},{8,9},{9,10},{10,1... | collective-permute-start | bytes 786440 | tf_op jit(solution)/shard_map/key_value_grads_ring/ppermute | solution.py:56
  99.2 3.5 %copy-start.6 = (bf16[1024,128]{1,0:T(8,128)(2,1)}, bf16[1024,128]{1,0:T(8,128)(2,1)S(1)}, u32[]{:S(2)}) copy-start(bf16[1024,128]{1,0:T(8,128)(2,1)S(1)} %collective-permute-done.23.refs_1_) | copy-start | bytes 786436
  99.8 2.9 %copy-start.7 = (bf16[1024,128]{1,0:T(8,128)(2,1)}, bf16[1024,128]{1,0:T(8,128)(2,1)S(1)}, u32[]{:S(2)}) copy-start(bf16[1024,128]{1,0:T(8,128)(2,1)S(1)} %collective-permute-done.24.refs_2_) | copy-start | bytes 786436
  102.6 0.7 copy-start.8
  103.3 8.1 %collective-permute-start.26 = (bf16[512,256]{1,0:T(8,128)(2,1)S(1)}, bf16[512,256]{1,0:T(8,128)(2,1)S(1)}, u32[]{:S(2)}, u32[]{:S(2)}) collective-permute-start(bf16[512,256]{1,0:T(8,128)(2,1)S(1)} %add_convert_fusion.1), channel_id=1, source_target_pairs={{0,7},{1,0},{2,1},{3,2},{4,3},{5,4},{6,5},{7,6},{8,15},{9,8},{10,9... | collective-permute-start | bytes 786440 | tf_op jit(solution)/shard_map/key_value_grads_ring/ppermute | solution.py:56
  112.2 6.2 %collective-permute-start.29 = (bf16[128,256]{1,0:T(8,128)(2,1)S(1)}, bf16[128,256]{1,0:T(8,128)(2,1)S(1)}, u32[]{:S(2)}, u32[]{:S(2)}) collective-permute-start(bf16[128,256]{1,0:T(8,128)(2,1)S(1)} %get-tuple-element.135), channel_id=1, source_target_pairs={{0,8},{1,9},{2,10},{3,11},{4,12},{5,13},{6,14},{7,15},{8,16},{9,17... | collective-permute-start | bytes 196616 | tf_op jit(solution)/shard_map/key_value_grads_out/ppermute | solution.py:50
  112.2 6.2 %collective-permute-start.28 = (bf16[128,256]{1,0:T(8,128)(2,1)S(1)}, bf16[128,256]{1,0:T(8,128)(2,1)S(1)}, u32[]{:S(2)}, u32[]{:S(2)}) collective-permute-start(bf16[128,256]{1,0:T(8,128)(2,1)S(1)} %get-tuple-element.136), channel_id=1, source_target_pairs={{0,16},{1,17},{2,18},{3,19},{4,20},{5,21},{6,22},{7,23},{8,24},{9,... | collective-permute-start | bytes 196616 | tf_op jit(solution)/shard_map/key_value_grads_out/ppermute | solution.py:50
  114.2 5.0 %collective-permute-start.27 = (bf16[128,256]{1,0:T(8,128)(2,1)S(1)}, bf16[128,256]{1,0:T(8,128)(2,1)S(1)}, u32[]{:S(2)}, u32[]{:S(2)}) collective-permute-start(bf16[128,256]{1,0:T(8,128)(2,1)S(1)} %get-tuple-element.137), channel_id=1, source_target_pairs={{0,24},{1,25},{2,26},{3,27},{4,28},{5,29},{6,30},{7,31},{8,0},{9,1... | collective-permute-start | bytes 196616 | tf_op jit(solution)/shard_map/key_value_grads_out/ppermute | solution.py:50
  118.3 0.9 copy-start.10
  118.3 0.9 copy-start.11
  119.2 0.6 copy-start.12

commit v3 on v2

--- a/solution.py
+++ b/solution.py
@@ -21,9 +21,9 @@
 ALL = TOK * NY * NZ
 BLOCKS = 2 * NY
 TILE = 256
-PACE = 2
-QUERY_STEP = 2
-GRAD_STEP = 3
+PACE = 4
+PACK_STEP = 2
+PLAN_STEP = 1
 BACK_STEP = 3
 WINDOW = 1024
 MAX_TILES = 5
@@ -62,31 +62,20 @@
     return lax.optimization_barrier(arrays)
 
 
-def gather_z(x, query_pieces, packed, send):
+def gather_z(x, plan, packed):
     right = left = x
     pieces = {0: x}
-    for step in range(1, NZ // 2 + 1):
-        right = along_z(right, 1)
-        if step < NZ // 2:
-            left = along_z(left, -1)
-            held = [right, left]
-            if step == 1:
-                held += packed
-            if step == QUERY_STEP:
-                held += query_pieces
-            if step == GRAD_STEP:
-                held += grad_pieces
-            right, left, *held = together(*held)
-            if step == 1:
-                plan, grad_pieces = held[:2], send(held[2 : 2 + NY])
-                held = held[2 + NY :]
-            if step == QUERY_STEP:
-                query_pieces, held = held[:NY], held[NY:]
-            if step == GRAD_STEP:
-                grad_pieces = held
-            pieces[step] = left
-        pieces[-step] = right
-    return [pieces[off] for off in OFFSETS], query_pieces, plan, grad_pieces
+    for step in range(1, NZ // 2):
+        right, left = along_z(right, 1), along_z(left, -1)
+        if step == PLAN_STEP:
+            right, left, *plan = together(right, left, *plan)
+        elif step == PACK_STEP:
+            right, left, *packed = together(right, left, *packed)
+        else:
+            right, left = together(right, left)
+        pieces[-step], pieces[step] = right, left
+    pieces[-(NZ // 2)] = along_z(right, 1)
+    return [pieces[off] for off in OFFSETS], plan, packed
 
 
 def add_low(moving, own):
@@ -108,8 +97,10 @@
             left = add_low(left, parts[step - half])
             if step < half - 1:
                 right = add_low(right, parts[half - 1 - step])
+    query_grad = place_wide(queries)
+    left, query_grad = together(left, query_grad)
     total = parts[0] + left.astype(jnp.float32) + right.astype(jnp.float32)
-    return total.astype(jnp.bfloat16), queries
+    return total.astype(jnp.bfloat16), query_grad
 
 
 def dot(a, b, dims):
@@ -149,6 +140,7 @@
         out_shape=[jax.ShapeDtypeStruct((TOK, 2 * DIM), jnp.bfloat16)] * NY,
         in_specs=whole(2),
         out_specs=whole(NY),
+        compiler_params=params(4),
         name="pack_kv",
     )(key, value)
 
@@ -172,6 +164,7 @@
         out_shape=[jax.ShapeDtypeStruct((2 * ROWS, DIM), jnp.bfloat16)] * NY,
         in_specs=whole(1),
         out_specs=whole(NY),
+        compiler_params=params(8),
         name="pack_queries",
     )(x)
 
@@ -205,6 +198,7 @@
         out_shape=[jax.ShapeDtypeStruct((GRAD_ROWS, DIM), jnp.bfloat16)] * NY,
         in_specs=whole(2),
         out_specs=whole(NY),
+        compiler_params=params(16),
         name="pack_grads",
     )(grad, out)
 
@@ -268,6 +262,7 @@
         ],
         in_specs=[scalars(), scalars()],
         out_specs=[scalars(), pl.BlockSpec(memory_space=pltpu.VMEM)],
+        compiler_params=params(4),
         name="make_plan",
     )(pairs, lengths)
 
@@ -451,6 +446,7 @@
         out_shape=jax.ShapeDtypeStruct((TOK, HEADS * WIDE), jnp.bfloat16),
         in_specs=whole(NY),
         out_specs=pl.BlockSpec(memory_space=pltpu.VMEM),
+        compiler_params=params(8),
         name="place_wide",
     )(*pieces)
 
@@ -468,6 +464,7 @@
         out_shape=[jax.ShapeDtypeStruct((TOK, HEADS * DIM), jnp.bfloat16)] * 2,
         in_specs=whole(NY),
         out_specs=whole(2),
+        compiler_params=params(4),
         name="place_kv",
     )(*pieces)
 
@@ -493,19 +490,18 @@
     with jax.named_scope("plan"):
         plan = make_plan(pair_of, doc_lengths)
     with jax.named_scope("grads_pack"):
+        out_grad, *query_pieces = together(out_grad, *query_pieces)
         packed_grads = pack_grads(out_grad, forward_out[0])
     with jax.named_scope("keys_values_ring"):
-        gathered, query_pieces, plan, grad_pieces = gather_z(
-            kv, query_pieces, [*plan, *packed_grads], lambda x: to_heads(x, along_y)
-        )
+        gathered, plan, packed_grads = gather_z(kv, plan, packed_grads)
+    with jax.named_scope("grads_in"):
+        grad_pieces = to_heads(packed_grads, along_y)
     parts = attention_grads(plan, query_pieces, grad_pieces, gathered)
     query_parts, kv_parts = parts[:NY], parts[NY:]
     with jax.named_scope("query_grads_out"):
         query_parts = to_heads(query_parts, lambda x, k: along_y(x, -k))
     with jax.named_scope("key_value_grads_ring"):
-        kv_sum, query_parts = sum_z(kv_parts, query_parts)
-    with jax.named_scope("query_grads_place"):
-        query_grad = place_wide(query_parts)
+        kv_sum, query_grad = sum_z(kv_parts, query_parts)
     with jax.named_scope("key_value_grads_out"):
         kv_pieces = [kv_sum[k * TOK : (k + 1) * TOK] for k in range(NY)]
         key_gradient, value_gradient = place_kv(

time: 121 us -> 114 us (0.942)
  the two profiles are of different devices: /device:TPU:6 before, /device:TPU:2 now
where the time goes in v3:
time: 114 us
  starting transfers between devices  49 us (43%)
  waiting for transfers between devices  41.9 us (37%)
  Pallas kernels  18.4 us (16%)
  local copies, waits for them, and re-layouts  3.09 us (3%)
    ppermute x15, starting transfers between devices, along_y(): lax.ppermute(x, 'ctx', [(c, (c // NZ + by) % NY * NZ + c % NZ) for c in r...  27.6 us
    ppermute x15, waiting for transfers between devices, along_y(): lax.ppermute(x, 'ctx', [(c, (c // NZ + by) % NY * NZ + c % NZ) for c in r...  26.7 us
    ppermute x14, starting transfers between devices, along_z(): lax.ppermute(x, 'ctx', [(c, c // NZ * NZ + (c % NZ + by) % NZ) for c in r...  21.4 us
    ppermute x14, waiting for transfers between devices, along_z(): lax.ppermute(x, 'ctx', [(c, c // NZ * NZ + (c % NZ + by) % NZ) for c in r...  15.2 us
    pallas_call x1, Pallas kernels, attention_grads(): pl.pallas_call(main_body, out_shape=[jax.ShapeDtypeStruct((2 * ROWS, DIM)...  13.8 us
    unnamed x15, local copies, waits for them, and re-layouts  3.06 us
  transfers between devices with their start and end apart: 30, of which 18 were waited for; matrix products, arithmetic and copies ran while one was open for 0% of the time, Pallas kernels for 3%

profile of v3, /device:TPU:2, one launch (start us, length us, event | category | flops | bytes accessed | tf_op | source)
XLA Modules:
  0.0 113.6 jit_solution(11556823739543507146)
XLA Ops:
  0.7 0.9 copy-done.2
  1.6 0.9 copy-done.3
  2.5 1.7 %collective-permute-start = (bf16[128,256]{1,0:T(8,128)(2,1)S(1)}, bf16[128,256]{1,0:T(8,128)(2,1)S(1)}, u32[]{:S(2)}, u32[]{:S(2)}) collective-permute-start(bf16[128,256]{1,0:T(8,128)(2,1)S(1)} %get-tuple-element.69), channel_id=1, source_target_pairs={{0,8},{1,9},{2,10},{3,11},{4,12},{5,13},{6,14},{7,15},{8,16},{9,17... | collective-permute-start | bytes 196616 | tf_op jit(solution)/shard_map/keys_values_in/ppermute | solution.py:50
  4.2 2.9 %collective-permute-start.1 = (bf16[128,256]{1,0:T(8,128)(2,1)S(1)}, bf16[128,256]{1,0:T(8,128)(2,1)S(1)}, u32[]{:S(2)}, u32[]{:S(2)}) collective-permute-start(bf16[128,256]{1,0:T(8,128)(2,1)S(1)} %get-tuple-element.70), channel_id=1, source_target_pairs={{0,16},{1,17},{2,18},{3,19},{4,20},{5,21},{6,22},{7,23},{8,24},{9,... | collective-permute-start | bytes 196616 | tf_op jit(solution)/shard_map/keys_values_in/ppermute | solution.py:50
  7.1 1.3 %collective-permute-start.2 = (bf16[128,256]{1,0:T(8,128)(2,1)S(1)}, bf16[128,256]{1,0:T(8,128)(2,1)S(1)}, u32[]{:S(2)}, u32[]{:S(2)}) collective-permute-start(bf16[128,256]{1,0:T(8,128)(2,1)S(1)} %get-tuple-element.71), channel_id=1, source_target_pairs={{0,24},{1,25},{2,26},{3,27},{4,28},{5,29},{6,30},{7,31},{8,0},{9,1... | collective-permute-start | bytes 196616 | tf_op jit(solution)/shard_map/keys_values_in/ppermute | solution.py:50
  8.4 1.2 %copy-done = bf16[1,128,4096]{2,1,0:T(8,128)(2,1)S(1)} copy-done((bf16[1,128,4096]{2,1,0:T(8,128)(2,1)S(1)}, bf16[1,128,4096]{2,1,0:T(8,128)(2,1)}, u32[]{:S(2)}) %copy-start) | copy-done | bytes 1048600
  9.8 1.1 %collective-permute-done.1 = bf16[128,256]{1,0:T(8,128)(2,1)S(1)} collective-permute-done((bf16[128,256]{1,0:T(8,128)(2,1)S(1)}, bf16[128,256]{1,0:T(8,128)(2,1)S(1)}, u32[]{:S(2)}, u32[]{:S(2)}) %collective-permute-start.1) | collective-permute-done | bytes 65568 | tf_op jit(solution)/shard_map/keys_values_in/ppermute | solution.py:50
  10.9 0.4 collective-permute-done.2
  11.4 5.9 %collective-permute-start.4 = (bf16[512,256]{1,0:T(8,128)(2,1)S(1)}, bf16[512,256]{1,0:T(8,128)(2,1)S(1)}, u32[]{:S(2)}, u32[]{:S(2)}) collective-permute-start(bf16[512,256]{1,0:T(8,128)(2,1)S(1)} %constant_dynamic-update-slice_fusion.refs_12_), channel_id=1, source_target_pairs={{0,7},{1,0},{2,1},{3,2},{4,3},{5,4},{6,5},{7,6},{8,15},{9,8},{10,9... | collective-permute-start | bytes 786440 | tf_op jit(solution)/shard_map/keys_values_ring/ppermute | solution.py:56
  17.3 0.8 collective-permute-start.6
  18.2 1.7 %make_plan.1 = (s32[272]{0:T(512)S(1)}, s32[8,512]{1,0:T(8,128)S(1)}) custom-call(s32[1,32]{1,0:T(1,128)S(1)} %copy-done.4, s32[1,16]{1,0:T(1,128)S(1)} %copy-done.5), custom_call_target="tpu_custom_call" | custom-call | tf_op jit(solution)/shard_map/plan/make_plan/pallas_call | solution.py:257
  19.9 3.3 %collective-permute-start.7 = (bf16[1024,128]{1,0:T(8,128)(2,1)S(1)}, bf16[1024,128]{1,0:T(8,128)(2,1)S(1)}, u32[]{:S(2)}, u32[]{:S(2)}) collective-permute-start(bf16[1024,128]{1,0:T(8,128)(2,1)S(1)} %get-tuple-element.86), channel_id=1, source_target_pairs={{0,16},{1,17},{2,18},{3,19},{4,20},{5,21},{6,22},{7,23},{8,24},{9,... | collective-permute-start | bytes 786440 | tf_op jit(solution)/shard_map/queries_in/ppermute | solution.py:50
  23.1 1.3 %collective-permute-start.8 = (bf16[1024,128]{1,0:T(8,128)(2,1)S(1)}, bf16[1024,128]{1,0:T(8,128)(2,1)S(1)}, u32[]{:S(2)}, u32[]{:S(2)}) collective-permute-start(bf16[1024,128]{1,0:T(8,128)(2,1)S(1)} %get-tuple-element.87), channel_id=1, source_target_pairs={{0,24},{1,25},{2,26},{3,27},{4,28},{5,29},{6,30},{7,31},{8,0},{9,1... | collective-permute-start | bytes 786440 | tf_op jit(solution)/shard_map/queries_in/ppermute | solution.py:50
  24.4 1.4 %collective-permute-done.3.refs_11_ = bf16[512,256]{1,0:T(8,128)(2,1)S(1)} collective-permute-done((bf16[512,256]{1,0:T(8,128)(2,1)S(1)}, bf16[512,256]{1,0:T(8,128)(2,1)S(1)}, u32[]{:S(2)}, u32[]{:S(2)}) %collective-permute-start.3) | collective-permute-done | bytes 262176 | tf_op jit(solution)/shard_map/keys_values_ring/ppermute | solution.py:56
  25.8 2.3 %collective-permute-done.6.refs_1_ = bf16[1024,128]{1,0:T(8,128)(2,1)S(1)} collective-permute-done((bf16[1024,128]{1,0:T(8,128)(2,1)S(1)}, bf16[1024,128]{1,0:T(8,128)(2,1)S(1)}, u32[]{:S(2)}, u32[]{:S(2)}) %collective-permute-start.6) | collective-permute-done | bytes 262176 | tf_op jit(solution)/shard_map/queries_in/ppermute | solution.py:50
  28.1 3.2 %collective-permute-start.10 = (bf16[512,256]{1,0:T(8,128)(2,1)S(1)}, bf16[512,256]{1,0:T(8,128)(2,1)S(1)}, u32[]{:S(2)}, u32[]{:S(2)}) collective-permute-start(bf16[512,256]{1,0:T(8,128)(2,1)S(1)} %collective-permute-done.4.refs_13_), channel_id=1, source_target_pairs={{0,7},{1,0},{2,1},{3,2},{4,3},{5,4},{6,5},{7,6},{8,15},{9,8},{10,9... | collective-permute-start | bytes 786440 | tf_op jit(solution)/shard_map/keys_values_ring/ppermute | solution.py:56
  31.3 0.3 collective-permute-done.7.refs_2_
  31.7 2.1 %collective-permute-done.8.refs_3_ = bf16[1024,128]{1,0:T(8,128)(2,1)S(1)} collective-permute-done((bf16[1024,128]{1,0:T(8,128)(2,1)S(1)}, bf16[1024,128]{1,0:T(8,128)(2,1)S(1)}, u32[]{:S(2)}, u32[]{:S(2)}) %collective-permute-start.8) | collective-permute-done | bytes 262176 | tf_op jit(solution)/shard_map/queries_in/ppermute | solution.py:50
  33.8 0.7 pack_grads.1
  34.5 0.7 collective-permute-done.10.refs_14_
  35.2 3.7 %collective-permute-start.15 = (bf16[512,256]{1,0:T(8,128)(2,1)S(1)}, bf16[512,256]{1,0:T(8,128)(2,1)S(1)}, u32[]{:S(2)}, u32[]{:S(2)}) collective-permute-start(bf16[512,256]{1,0:T(8,128)(2,1)S(1)} %collective-permute-done.10.refs_14_), channel_id=1, source_target_pairs={{0,7},{1,0},{2,1},{3,2},{4,3},{5,4},{6,5},{7,6},{8,15},{9,8},{10,9... | collective-permute-start | bytes 786440 | tf_op jit(solution)/shard_map/keys_values_ring/ppermute | solution.py:56
  38.9 1.6 %collective-permute-start.11 = (bf16[1152,128]{1,0:T(8,128)(2,1)S(1)}, bf16[1152,128]{1,0:T(8,128)(2,1)S(1)}, u32[]{:S(2)}, u32[]{:S(2)}) collective-permute-start(bf16[1152,128]{1,0:T(8,128)(2,1)S(1)} %get-tuple-element.100), channel_id=1, source_target_pairs={{0,8},{1,9},{2,10},{3,11},{4,12},{5,13},{6,14},{7,15},{8,16},{9,17... | collective-permute-start | bytes 884744 | tf_op jit(solution)/shard_map/grads_in/ppermute | solution.py:50
  40.5 2.7 %collective-permute-start.12 = (bf16[1152,128]{1,0:T(8,128)(2,1)S(1)}, bf16[1152,128]{1,0:T(8,128)(2,1)S(1)}, u32[]{:S(2)}, u32[]{:S(2)}) collective-permute-start(bf16[1152,128]{1,0:T(8,128)(2,1)S(1)} %get-tuple-element.101), channel_id=1, source_target_pairs={{0,16},{1,17},{2,18},{3,19},{4,20},{5,21},{6,22},{7,23},{8,24},{9,... | collective-permute-start | bytes 884744 | tf_op jit(solution)/shard_map/grads_in/ppermute | solution.py:50
  43.2 2.6 %collective-permute-start.13 = (bf16[1152,128]{1,0:T(8,128)(2,1)S(1)}, bf16[1152,128]{1,0:T(8,128)(2,1)S(1)}, u32[]{:S(2)}, u32[]{:S(2)}) collective-permute-start(bf16[1152,128]{1,0:T(8,128)(2,1)S(1)} %get-tuple-element.102), channel_id=1, source_target_pairs={{0,24},{1,25},{2,26},{3,27},{4,28},{5,29},{6,30},{7,31},{8,0},{9,1... | collective-permute-start | bytes 884744 | tf_op jit(solution)/shard_map/grads_in/ppermute | solution.py:50
  45.8 3.1 %collective-permute-done.11.refs_5_ = bf16[1152,128]{1,0:T(8,128)(2,1)S(1)} collective-permute-done((bf16[1152,128]{1,0:T(8,128)(2,1)S(1)}, bf16[1152,128]{1,0:T(8,128)(2,1)S(1)}, u32[]{:S(2)}, u32[]{:S(2)}) %collective-permute-start.11) | collective-permute-done | bytes 294944 | tf_op jit(solution)/shard_map/grads_in/ppermute | solution.py:50
  48.9 5.3 %collective-permute-done.12.refs_6_ = bf16[1152,128]{1,0:T(8,128)(2,1)S(1)} collective-permute-done((bf16[1152,128]{1,0:T(8,128)(2,1)S(1)}, bf16[1152,128]{1,0:T(8,128)(2,1)S(1)}, u32[]{:S(2)}, u32[]{:S(2)}) %collective-permute-start.12) | collective-permute-done | bytes 294944 | tf_op jit(solution)/shard_map/grads_in/ppermute | solution.py:50
  54.3 13.8 %attention_grads.1 = (bf16[1024,128]{1,0:T(8,128)(2,1)S(1)}, bf16[1024,128]{1,0:T(8,128)(2,1)S(1)}, bf16[1024,128]{1,0:T(8,128)(2,1)S(1)}, bf16[1024,128]{1,0:T(...) custom-call(s32[272]{0:T(512)S(1)} %get-tuple-element.82.plan, ...), custom_call_target="tpu_custom_call" | custom-call | tf_op jit(solution)/shard_map/attention_grads/pallas_call | solution.py:400
  68.2 2.0 %collective-permute-start.18 = (bf16[512,256]{1,0:T(8,128)(2,1)S(1)}, bf16[512,256]{1,0:T(8,128)(2,1)S(1)}, u32[]{:S(2)}, u32[]{:S(2)}) collective-permute-start(bf16[512,256]{1,0:T(8,128)(2,1)S(1)} %get-tuple-element.108), channel_id=1, source_target_pairs={{0,1},{1,2},{2,3},{3,4},{4,5},{5,6},{6,7},{7,0},{8,9},{9,10},{10,1... | collective-permute-start | bytes 786440 | tf_op jit(solution)/shard_map/key_value_grads_ring/ppermute | solution.py:56
  70.2 4.3 %collective-permute-done.17 = bf16[512,256]{1,0:T(8,128)(2,1)S(1)} collective-permute-done((bf16[512,256]{1,0:T(8,128)(2,1)S(1)}, bf16[512,256]{1,0:T(8,128)(2,1)S(1)}, u32[]{:S(2)}, u32[]{:S(2)}) %collective-permute-start.17) | collective-permute-done | bytes 262176 | tf_op jit(solution)/shard_map/key_value_grads_ring/ppermute | solution.py:56
  74.6 2.5 %collective-permute-done.18 = bf16[512,256]{1,0:T(8,128)(2,1)S(1)} collective-permute-done((bf16[512,256]{1,0:T(8,128)(2,1)S(1)}, bf16[512,256]{1,0:T(8,128)(2,1)S(1)}, u32[]{:S(2)}, u32[]{:S(2)}) %collective-permute-start.18) | collective-permute-done | bytes 262176 | tf_op jit(solution)/shard_map/key_value_grads_ring/ppermute | solution.py:56
  77.1 0.4 collective-permute-start.19
  77.5 1.8 %collective-permute-start.20 = (bf16[512,256]{1,0:T(8,128)(2,1)S(1)}, bf16[512,256]{1,0:T(8,128)(2,1)S(1)}, u32[]{:S(2)}, u32[]{:S(2)}) collective-permute-start(bf16[512,256]{1,0:T(8,128)(2,1)S(1)} %add_convert_fusion.4), channel_id=1, source_target_pairs={{0,1},{1,2},{2,3},{3,4},{4,5},{5,6},{6,7},{7,0},{8,9},{9,10},{10,1... | collective-permute-start | bytes 786440 | tf_op jit(solution)/shard_map/key_value_grads_ring/ppermute | solution.py:56
  79.3 3.3 %collective-permute-start.23 = (bf16[1024,128]{1,0:T(8,128)(2,1)S(1)}, bf16[1024,128]{1,0:T(8,128)(2,1)S(1)}, u32[]{:S(2)}, u32[]{:S(2)}) collective-permute-start(bf16[1024,128]{1,0:T(8,128)(2,1)S(1)} %get-tuple-element.118), channel_id=1, source_target_pairs={{0,24},{1,25},{2,26},{3,27},{4,28},{5,29},{6,30},{7,31},{8,0},{9,1... | collective-permute-start | bytes 786440 | tf_op jit(solution)/shard_map/query_grads_out/ppermute | solution.py:50
  82.7 0.5 collective-permute-start.24
  83.1 1.4 %collective-permute-start.25 = (bf16[1024,128]{1,0:T(8,128)(2,1)S(1)}, bf16[1024,128]{1,0:T(8,128)(2,1)S(1)}, u32[]{:S(2)}, u32[]{:S(2)}) collective-permute-start(bf16[1024,128]{1,0:T(8,128)(2,1)S(1)} %get-tuple-element.120), channel_id=1, source_target_pairs={{0,8},{1,9},{2,10},{3,11},{4,12},{5,13},{6,14},{7,15},{8,16},{9,17... | collective-permute-start | bytes 786440 | tf_op jit(solution)/shard_map/query_grads_out/ppermute | solution.py:50
  84.5 1.0 collective-permute-done.20
  85.6 0.6 collective-permute-start.21
  86.3 1.6 %collective-permute-start.22 = (bf16[512,256]{1,0:T(8,128)(2,1)S(1)}, bf16[512,256]{1,0:T(8,128)(2,1)S(1)}, u32[]{:S(2)}, u32[]{:S(2)}) collective-permute-start(bf16[512,256]{1,0:T(8,128)(2,1)S(1)} %add_convert_fusion.2), channel_id=1, source_target_pairs={{0,1},{1,2},{2,3},{3,4},{4,5},{5,6},{6,7},{7,0},{8,9},{9,10},{10,1... | collective-permute-start | bytes 786440 | tf_op jit(solution)/shard_map/key_value_grads_ring/ppermute | solution.py:56
  87.9 5.4 %collective-permute-done.23.refs_1_ = bf16[1024,128]{1,0:T(8,128)(2,1)S(1)} collective-permute-done((bf16[1024,128]{1,0:T(8,128)(2,1)S(1)}, bf16[1024,128]{1,0:T(8,128)(2,1)S(1)}, u32[]{:S(2)}, u32[]{:S(2)}) %collective-permute-start.23) | collective-permute-done | bytes 262176 | tf_op jit(solution)/shard_map/query_grads_out/ppermute | solution.py:50
  93.4 3.5 %collective-permute-done.25.refs_3_ = bf16[1024,128]{1,0:T(8,128)(2,1)S(1)} collective-permute-done((bf16[1024,128]{1,0:T(8,128)(2,1)S(1)}, bf16[1024,128]{1,0:T(8,128)(2,1)S(1)}, u32[]{:S(2)}, u32[]{:S(2)}) %collective-permute-start.25) | collective-permute-done | bytes 262176 | tf_op jit(solution)/shard_map/query_grads_out/ppermute | solution.py:50
  97.0 2.1 %collective-permute-start.26 = (bf16[512,256]{1,0:T(8,128)(2,1)S(1)}, bf16[512,256]{1,0:T(8,128)(2,1)S(1)}, u32[]{:S(2)}, u32[]{:S(2)}) collective-permute-start(bf16[512,256]{1,0:T(8,128)(2,1)S(1)} %add_convert_fusion.1), channel_id=1, source_target_pairs={{0,7},{1,0},{2,1},{3,2},{4,3},{5,4},{6,5},{7,6},{8,15},{9,8},{10,9... | collective-permute-start | bytes 786440 | tf_op jit(solution)/shard_map/key_value_grads_ring/ppermute | solution.py:56
  99.1 1.3 %place_wide.1 = bf16[128,4096]{1,0:T(8,128)(2,1)} custom-call(bf16[1024,128]{1,0:T(8,128)(2,1)S(1)} %get-tuple-element.123.refs_0_, bf16[1024,128]{1,0:T(8,128)(2,1)S(1)} %collective-permute-done.23.refs_1_, bf16[1024,128]{1,0:T(8,128)(2,1)S(1)} %collective-permute-done.24.refs_2_, bf16[1024,128]{1,0:T(8,128)(2,1)S(1)} %collective-permute-done.25.refs_3_), custom_call_target="tpu_custom_call" | custom-call | tf_op jit(solution)/shard_map/key_value_grads_ring/place_wide/pallas_call | solution.py:444
  100.4 5.2 %collective-permute-done.26 = bf16[512,256]{1,0:T(8,128)(2,1)S(1)} collective-permute-done((bf16[512,256]{1,0:T(8,128)(2,1)S(1)}, bf16[512,256]{1,0:T(8,128)(2,1)S(1)}, u32[]{:S(2)}, u32[]{:S(2)}) %collective-permute-start.26) | collective-permute-done | bytes 262176 | tf_op jit(solution)/shard_map/key_value_grads_ring/ppermute | solution.py:56
  105.8 1.6 %collective-permute-start.28 = (bf16[128,256]{1,0:T(8,128)(2,1)S(1)}, bf16[128,256]{1,0:T(8,128)(2,1)S(1)}, u32[]{:S(2)}, u32[]{:S(2)}) collective-permute-start(bf16[128,256]{1,0:T(8,128)(2,1)S(1)} %get-tuple-element.134), channel_id=1, source_target_pairs={{0,16},{1,17},{2,18},{3,19},{4,20},{5,21},{6,22},{7,23},{8,24},{9,... | collective-permute-start | bytes 196616 | tf_op jit(solution)/shard_map/key_value_grads_out/ppermute | solution.py:50
  107.4 2.5 %collective-permute-start.27 = (bf16[128,256]{1,0:T(8,128)(2,1)S(1)}, bf16[128,256]{1,0:T(8,128)(2,1)S(1)}, u32[]{:S(2)}, u32[]{:S(2)}) collective-permute-start(bf16[128,256]{1,0:T(8,128)(2,1)S(1)} %get-tuple-element.135), channel_id=1, source_target_pairs={{0,24},{1,25},{2,26},{3,27},{4,28},{5,29},{6,30},{7,31},{8,0},{9,1... | collective-permute-start | bytes 196616 | tf_op jit(solution)/shard_map/key_value_grads_out/ppermute | solution.py:50
  110.0 2.0 %collective-permute-done.29.refs_3_ = bf16[128,256]{1,0:T(8,128)(2,1)S(1)} collective-permute-done((bf16[128,256]{1,0:T(8,128)(2,1)S(1)}, bf16[128,256]{1,0:T(8,128)(2,1)S(1)}, u32[]{:S(2)}, u32[]{:S(2)}) %collective-permute-start.29) | collective-permute-done | bytes 65568 | tf_op jit(solution)/shard_map/key_value_grads_out/ppermute | solution.py:50
  111.9 0.9 collective-permute-done.27.refs_1_
  112.8 0.8 place_kv.1
  (42 shorter events, 1.0 us)
Async XLA Ops:
  0.6 33.1 %collective-permute-start.5 = (bf16[128,4096]{1,0:T(8,128)(2,1)}, bf16[128,4096]{1,0:T(8,128)(2,1)S(1)}, u32[]{:S(2)}, u32[]{:S(2)}) collective-permute-start(bf16[128,4096]{1,0:T(8,128)(2,1)} %bitcast.13), channel_id=1, source_target_pairs={{0,224},{32,0},{64,32},{96,64},{128,96},{160,128},{192,160},{224,1... | collective-permute-start | bytes 3145736 | tf_op jit(solution)/shard_map/grads_shift/ppermute | solution.py:479
  0.7 0.9 copy-start.2
  1.6 0.9 copy-start.3
  2.5 7.3 %collective-permute-start = (bf16[128,256]{1,0:T(8,128)(2,1)S(1)}, bf16[128,256]{1,0:T(8,128)(2,1)S(1)}, u32[]{:S(2)}, u32[]{:S(2)}) collective-permute-start(bf16[128,256]{1,0:T(8,128)(2,1)S(1)} %get-tuple-element.69), channel_id=1, source_target_pairs={{0,8},{1,9},{2,10},{3,11},{4,12},{5,13},{6,14},{7,15},{8,16},{9,17... | collective-permute-start | bytes 196616 | tf_op jit(solution)/shard_map/keys_values_in/ppermute | solution.py:50
  4.2 6.8 %collective-permute-start.1 = (bf16[128,256]{1,0:T(8,128)(2,1)S(1)}, bf16[128,256]{1,0:T(8,128)(2,1)S(1)}, u32[]{:S(2)}, u32[]{:S(2)}) collective-permute-start(bf16[128,256]{1,0:T(8,128)(2,1)S(1)} %get-tuple-element.70), channel_id=1, source_target_pairs={{0,16},{1,17},{2,18},{3,19},{4,20},{5,21},{6,22},{7,23},{8,24},{9,... | collective-permute-start | bytes 196616 | tf_op jit(solution)/shard_map/keys_values_in/ppermute | solution.py:50
  7.1 4.3 %collective-permute-start.2 = (bf16[128,256]{1,0:T(8,128)(2,1)S(1)}, bf16[128,256]{1,0:T(8,128)(2,1)S(1)}, u32[]{:S(2)}, u32[]{:S(2)}) collective-permute-start(bf16[128,256]{1,0:T(8,128)(2,1)S(1)} %get-tuple-element.71), channel_id=1, source_target_pairs={{0,24},{1,25},{2,26},{3,27},{4,28},{5,29},{6,30},{7,31},{8,0},{9,1... | collective-permute-start | bytes 196616 | tf_op jit(solution)/shard_map/keys_values_in/ppermute | solution.py:50
  8.4 1.2 %copy-start = (bf16[1,128,4096]{2,1,0:T(8,128)(2,1)S(1)}, bf16[1,128,4096]{2,1,0:T(8,128)(2,1)}, u32[]{:S(2)}) copy-start(bf16[1,128,4096]{2,1,0:T(8,128)(2,1)} %param.7) | copy-start | bytes 3145732
  9.6 24.1 %copy-start.1 = (bf16[1,128,4096]{2,1,0:T(8,128)(2,1)S(1)}, bf16[1,128,4096]{2,1,0:T(8,128)(2,1)}, u32[]{:S(2)}) copy-start(bf16[1,128,4096]{2,1,0:T(8,128)(2,1)} %param.10) | copy-start | bytes 3145732
  11.4 6.8 %copy-start.4 = (s32[1,32]{1,0:T(1,128)S(1)}, s32[1,32]{1,0:T(1,128)}, u32[]{:S(2)}) copy-start(s32[1,32]{1,0:T(1,128)} %pairs.1) | copy-start | bytes 388
  11.4 6.8 %copy-start.5 = (s32[1,16]{1,0:T(1,128)S(1)}, s32[1,16]{1,0:T(1,128)}, u32[]{:S(2)}) copy-start(s32[1,16]{1,0:T(1,128)} %lengths.1) | copy-start | bytes 196
  11.4 11.7 %collective-permute-start.4 = (bf16[512,256]{1,0:T(8,128)(2,1)S(1)}, bf16[512,256]{1,0:T(8,128)(2,1)S(1)}, u32[]{:S(2)}, u32[]{:S(2)}) collective-permute-start(bf16[512,256]{1,0:T(8,128)(2,1)S(1)} %constant_dynamic-update-slice_fusion.refs_12_), channel_id=1, source_target_pairs={{0,7},{1,0},{2,1},{3,2},{4,3},{5,4},{6,5},{7,6},{8,15},{9,8},{10,9... | collective-permute-start | bytes 786440 | tf_op jit(solution)/shard_map/keys_values_ring/ppermute | solution.py:56
  17.3 8.5 %collective-permute-start.3 = (bf16[512,256]{1,0:T(8,128)(2,1)S(1)}, bf16[512,256]{1,0:T(8,128)(2,1)S(1)}, u32[]{:S(2)}, u32[]{:S(2)}) collective-permute-start(bf16[512,256]{1,0:T(8,128)(2,1)S(1)} %constant_dynamic-update-slice_fusion.refs_12_), channel_id=1, source_target_pairs={{0,1},{1,2},{2,3},{3,4},{4,5},{5,6},{6,7},{7,0},{8,9},{9,10},{10,1... | collective-permute-start | bytes 786440 | tf_op jit(solution)/shard_map/keys_values_ring/ppermute | solution.py:56
  17.3 10.8 %collective-permute-start.6 = (bf16[1024,128]{1,0:T(8,128)(2,1)S(1)}, bf16[1024,128]{1,0:T(8,128)(2,1)S(1)}, u32[]{:S(2)}, u32[]{:S(2)}) collective-permute-start(bf16[1024,128]{1,0:T(8,128)(2,1)S(1)} %get-tuple-element.85), channel_id=1, source_target_pairs={{0,8},{1,9},{2,10},{3,11},{4,12},{5,13},{6,14},{7,15},{8,16},{9,17... | collective-permute-start | bytes 786440 | tf_op jit(solution)/shard_map/queries_in/ppermute | solution.py:50
  19.9 11.8 %collective-permute-start.7 = (bf16[1024,128]{1,0:T(8,128)(2,1)S(1)}, bf16[1024,128]{1,0:T(8,128)(2,1)S(1)}, u32[]{:S(2)}, u32[]{:S(2)}) collective-permute-start(bf16[1024,128]{1,0:T(8,128)(2,1)S(1)} %get-tuple-element.86), channel_id=1, source_target_pairs={{0,16},{1,17},{2,18},{3,19},{4,20},{5,21},{6,22},{7,23},{8,24},{9,... | collective-permute-start | bytes 786440 | tf_op jit(solution)/shard_map/queries_in/ppermute | solution.py:50
  23.1 10.6 %collective-permute-start.8 = (bf16[1024,128]{1,0:T(8,128)(2,1)S(1)}, bf16[1024,128]{1,0:T(8,128)(2,1)S(1)}, u32[]{:S(2)}, u32[]{:S(2)}) collective-permute-start(bf16[1024,128]{1,0:T(8,128)(2,1)S(1)} %get-tuple-element.87), channel_id=1, source_target_pairs={{0,24},{1,25},{2,26},{3,27},{4,28},{5,29},{6,30},{7,31},{8,0},{9,1... | collective-permute-start | bytes 786440 | tf_op jit(solution)/shard_map/queries_in/ppermute | solution.py:50
  25.8 8.7 %collective-permute-start.9 = (bf16[512,256]{1,0:T(8,128)(2,1)S(1)}, bf16[512,256]{1,0:T(8,128)(2,1)S(1)}, u32[]{:S(2)}, u32[]{:S(2)}) collective-permute-start(bf16[512,256]{1,0:T(8,128)(2,1)S(1)} %collective-permute-done.3.refs_11_), channel_id=1, source_target_pairs={{0,1},{1,2},{2,3},{3,4},{4,5},{5,6},{6,7},{7,0},{8,9},{9,10},{10,1... | collective-permute-start | bytes 786440 | tf_op jit(solution)/shard_map/keys_values_ring/ppermute | solution.py:56
  28.1 7.1 %collective-permute-start.10 = (bf16[512,256]{1,0:T(8,128)(2,1)S(1)}, bf16[512,256]{1,0:T(8,128)(2,1)S(1)}, u32[]{:S(2)}, u32[]{:S(2)}) collective-permute-start(bf16[512,256]{1,0:T(8,128)(2,1)S(1)} %collective-permute-done.4.refs_13_), channel_id=1, source_target_pairs={{0,7},{1,0},{2,1},{3,2},{4,3},{5,4},{6,5},{7,6},{8,15},{9,8},{10,9... | collective-permute-start | bytes 786440 | tf_op jit(solution)/shard_map/keys_values_ring/ppermute | solution.py:56
  35.2 10.6 %collective-permute-start.14 = (bf16[512,256]{1,0:T(8,128)(2,1)S(1)}, bf16[512,256]{1,0:T(8,128)(2,1)S(1)}, u32[]{:S(2)}, u32[]{:S(2)}) collective-permute-start(bf16[512,256]{1,0:T(8,128)(2,1)S(1)} %collective-permute-done.9.refs_10_), channel_id=1, source_target_pairs={{0,1},{1,2},{2,3},{3,4},{4,5},{5,6},{6,7},{7,0},{8,9},{9,10},{10,1... | collective-permute-start | bytes 786440 | tf_op jit(solution)/shard_map/keys_values_ring/ppermute | solution.py:56
  35.2 10.6 %collective-permute-start.15 = (bf16[512,256]{1,0:T(8,128)(2,1)S(1)}, bf16[512,256]{1,0:T(8,128)(2,1)S(1)}, u32[]{:S(2)}, u32[]{:S(2)}) collective-permute-start(bf16[512,256]{1,0:T(8,128)(2,1)S(1)} %collective-permute-done.10.refs_14_), channel_id=1, source_target_pairs={{0,7},{1,0},{2,1},{3,2},{4,3},{5,4},{6,5},{7,6},{8,15},{9,8},{10,9... | collective-permute-start | bytes 786440 | tf_op jit(solution)/shard_map/keys_values_ring/ppermute | solution.py:56
  38.9 10.0 %collective-permute-start.11 = (bf16[1152,128]{1,0:T(8,128)(2,1)S(1)}, bf16[1152,128]{1,0:T(8,128)(2,1)S(1)}, u32[]{:S(2)}, u32[]{:S(2)}) collective-permute-start(bf16[1152,128]{1,0:T(8,128)(2,1)S(1)} %get-tuple-element.100), channel_id=1, source_target_pairs={{0,8},{1,9},{2,10},{3,11},{4,12},{5,13},{6,14},{7,15},{8,16},{9,17... | collective-permute-start | bytes 884744 | tf_op jit(solution)/shard_map/grads_in/ppermute | solution.py:50
  40.5 13.8 %collective-permute-start.12 = (bf16[1152,128]{1,0:T(8,128)(2,1)S(1)}, bf16[1152,128]{1,0:T(8,128)(2,1)S(1)}, u32[]{:S(2)}, u32[]{:S(2)}) collective-permute-start(bf16[1152,128]{1,0:T(8,128)(2,1)S(1)} %get-tuple-element.101), channel_id=1, source_target_pairs={{0,16},{1,17},{2,18},{3,19},{4,20},{5,21},{6,22},{7,23},{8,24},{9,... | collective-permute-start | bytes 884744 | tf_op jit(solution)/shard_map/grads_in/ppermute | solution.py:50
  43.2 11.1 %collective-permute-start.13 = (bf16[1152,128]{1,0:T(8,128)(2,1)S(1)}, bf16[1152,128]{1,0:T(8,128)(2,1)S(1)}, u32[]{:S(2)}, u32[]{:S(2)}) collective-permute-start(bf16[1152,128]{1,0:T(8,128)(2,1)S(1)} %get-tuple-element.102), channel_id=1, source_target_pairs={{0,24},{1,25},{2,26},{3,27},{4,28},{5,29},{6,30},{7,31},{8,0},{9,1... | collective-permute-start | bytes 884744 | tf_op jit(solution)/shard_map/grads_in/ppermute | solution.py:50
  45.8 8.5 %collective-permute-start.16 = (bf16[512,256]{1,0:T(8,128)(2,1)S(1)}, bf16[512,256]{1,0:T(8,128)(2,1)S(1)}, u32[]{:S(2)}, u32[]{:S(2)}) collective-permute-start(bf16[512,256]{1,0:T(8,128)(2,1)S(1)} %collective-permute-done.14.refs_9_), channel_id=1, source_target_pairs={{0,1},{1,2},{2,3},{3,4},{4,5},{5,6},{6,7},{7,0},{8,9},{9,10},{10,1... | collective-permute-start | bytes 786440 | tf_op jit(solution)/shard_map/keys_values_ring/ppermute | solution.py:56
  68.1 6.5 %collective-permute-start.17 = (bf16[512,256]{1,0:T(8,128)(2,1)S(1)}, bf16[512,256]{1,0:T(8,128)(2,1)S(1)}, u32[]{:S(2)}, u32[]{:S(2)}) collective-permute-start(bf16[512,256]{1,0:T(8,128)(2,1)S(1)} %get-tuple-element.107), channel_id=1, source_target_pairs={{0,7},{1,0},{2,1},{3,2},{4,3},{5,4},{6,5},{7,6},{8,15},{9,8},{10,9... | collective-permute-start | bytes 786440 | tf_op jit(solution)/shard_map/key_value_grads_ring/ppermute | solution.py:56
  68.2 8.9 %collective-permute-start.18 = (bf16[512,256]{1,0:T(8,128)(2,1)S(1)}, bf16[512,256]{1,0:T(8,128)(2,1)S(1)}, u32[]{:S(2)}, u32[]{:S(2)}) collective-permute-start(bf16[512,256]{1,0:T(8,128)(2,1)S(1)} %get-tuple-element.108), channel_id=1, source_target_pairs={{0,1},{1,2},{2,3},{3,4},{4,5},{5,6},{6,7},{7,0},{8,9},{9,10},{10,1... | collective-permute-start | bytes 786440 | tf_op jit(solution)/shard_map/key_value_grads_ring/ppermute | solution.py:56
  77.1 7.4 %collective-permute-start.19 = (bf16[512,256]{1,0:T(8,128)(2,1)S(1)}, bf16[512,256]{1,0:T(8,128)(2,1)S(1)}, u32[]{:S(2)}, u32[]{:S(2)}) collective-permute-start(bf16[512,256]{1,0:T(8,128)(2,1)S(1)} %add_convert_fusion.5), channel_id=1, source_target_pairs={{0,7},{1,0},{2,1},{3,2},{4,3},{5,4},{6,5},{7,6},{8,15},{9,8},{10,9... | collective-permute-start | bytes 786440 | tf_op jit(solution)/shard_map/key_value_grads_ring/ppermute | solution.py:56
  77.5 8.0 %collective-permute-start.20 = (bf16[512,256]{1,0:T(8,128)(2,1)S(1)}, bf16[512,256]{1,0:T(8,128)(2,1)S(1)}, u32[]{:S(2)}, u32[]{:S(2)}) collective-permute-start(bf16[512,256]{1,0:T(8,128)(2,1)S(1)} %add_convert_fusion.4), channel_id=1, source_target_pairs={{0,1},{1,2},{2,3},{3,4},{4,5},{5,6},{6,7},{7,0},{8,9},{9,10},{10,1... | collective-permute-start | bytes 786440 | tf_op jit(solution)/shard_map/key_value_grads_ring/ppermute | solution.py:56
  79.3 14.0 %collective-permute-start.23 = (bf16[1024,128]{1,0:T(8,128)(2,1)S(1)}, bf16[1024,128]{1,0:T(8,128)(2,1)S(1)}, u32[]{:S(2)}, u32[]{:S(2)}) collective-permute-start(bf16[1024,128]{1,0:T(8,128)(2,1)S(1)} %get-tuple-element.118), channel_id=1, source_target_pairs={{0,24},{1,25},{2,26},{3,27},{4,28},{5,29},{6,30},{7,31},{8,0},{9,1... | collective-permute-start | bytes 786440 | tf_op jit(solution)/shard_map/query_grads_out/ppermute | solution.py:50
  82.7 10.8 %collective-permute-start.24 = (bf16[1024,128]{1,0:T(8,128)(2,1)S(1)}, bf16[1024,128]{1,0:T(8,128)(2,1)S(1)}, u32[]{:S(2)}, u32[]{:S(2)}) collective-permute-start(bf16[1024,128]{1,0:T(8,128)(2,1)S(1)} %get-tuple-element.119), channel_id=1, source_target_pairs={{0,16},{1,17},{2,18},{3,19},{4,20},{5,21},{6,22},{7,23},{8,24},{9,... | collective-permute-start | bytes 786440 | tf_op jit(solution)/shard_map/query_grads_out/ppermute | solution.py:50
  83.1 13.9 %collective-permute-start.25 = (bf16[1024,128]{1,0:T(8,128)(2,1)S(1)}, bf16[1024,128]{1,0:T(8,128)(2,1)S(1)}, u32[]{:S(2)}, u32[]{:S(2)}) collective-permute-start(bf16[1024,128]{1,0:T(8,128)(2,1)S(1)} %get-tuple-element.120), channel_id=1, source_target_pairs={{0,8},{1,9},{2,10},{3,11},{4,12},{5,13},{6,14},{7,15},{8,16},{9,17... | collective-permute-start | bytes 786440 | tf_op jit(solution)/shard_map/query_grads_out/ppermute | solution.py:50
  85.6 11.4 %collective-permute-start.21 = (bf16[512,256]{1,0:T(8,128)(2,1)S(1)}, bf16[512,256]{1,0:T(8,128)(2,1)S(1)}, u32[]{:S(2)}, u32[]{:S(2)}) collective-permute-start(bf16[512,256]{1,0:T(8,128)(2,1)S(1)} %add_convert_fusion.3), channel_id=1, source_target_pairs={{0,7},{1,0},{2,1},{3,2},{4,3},{5,4},{6,5},{7,6},{8,15},{9,8},{10,9... | collective-permute-start | bytes 786440 | tf_op jit(solution)/shard_map/key_value_grads_ring/ppermute | solution.py:56
  86.3 10.7 %collective-permute-start.22 = (bf16[512,256]{1,0:T(8,128)(2,1)S(1)}, bf16[512,256]{1,0:T(8,128)(2,1)S(1)}, u32[]{:S(2)}, u32[]{:S(2)}) collective-permute-start(bf16[512,256]{1,0:T(8,128)(2,1)S(1)} %add_convert_fusion.2), channel_id=1, source_target_pairs={{0,1},{1,2},{2,3},{3,4},{4,5},{5,6},{6,7},{7,0},{8,9},{9,10},{10,1... | collective-permute-start | bytes 786440 | tf_op jit(solution)/shard_map/key_value_grads_ring/ppermute | solution.py:56
  97.0 8.5 %collective-permute-start.26 = (bf16[512,256]{1,0:T(8,128)(2,1)S(1)}, bf16[512,256]{1,0:T(8,128)(2,1)S(1)}, u32[]{:S(2)}, u32[]{:S(2)}) collective-permute-start(bf16[512,256]{1,0:T(8,128)(2,1)S(1)} %add_convert_fusion.1), channel_id=1, source_target_pairs={{0,7},{1,0},{2,1},{3,2},{4,3},{5,4},{6,5},{7,6},{8,15},{9,8},{10,9... | collective-permute-start | bytes 786440 | tf_op jit(solution)/shard_map/key_value_grads_ring/ppermute | solution.py:56
  105.7 6.3 %collective-permute-start.29 = (bf16[128,256]{1,0:T(8,128)(2,1)S(1)}, bf16[128,256]{1,0:T(8,128)(2,1)S(1)}, u32[]{:S(2)}, u32[]{:S(2)}) collective-permute-start(bf16[128,256]{1,0:T(8,128)(2,1)S(1)} %get-tuple-element.133), channel_id=1, source_target_pairs={{0,8},{1,9},{2,10},{3,11},{4,12},{5,13},{6,14},{7,15},{8,16},{9,17... | collective-permute-start | bytes 196616 | tf_op jit(solution)/shard_map/key_value_grads_out/ppermute | solution.py:50
  105.8 6.2 %collective-permute-start.28 = (bf16[128,256]{1,0:T(8,128)(2,1)S(1)}, bf16[128,256]{1,0:T(8,128)(2,1)S(1)}, u32[]{:S(2)}, u32[]{:S(2)}) collective-permute-start(bf16[128,256]{1,0:T(8,128)(2,1)S(1)} %get-tuple-element.134), channel_id=1, source_target_pairs={{0,16},{1,17},{2,18},{3,19},{4,20},{5,21},{6,22},{7,23},{8,24},{9,... | collective-permute-start | bytes 196616 | tf_op jit(solution)/shard_map/key_value_grads_out/ppermute | solution.py:50
  107.4 5.4 %collective-permute-start.27 = (bf16[128,256]{1,0:T(8,128)(2,1)S(1)}, bf16[128,256]{1,0:T(8,128)(2,1)S(1)}, u32[]{:S(2)}, u32[]{:S(2)}) collective-permute-start(bf16[128,256]{1,0:T(8,128)(2,1)S(1)} %get-tuple-element.135), channel_id=1, source_target_pairs={{0,24},{1,25},{2,26},{3,27},{4,28},{5,29},{6,30},{7,31},{8,0},{9,1... | collective-permute-start | bytes 196616 | tf_op jit(solution)/shard_map/key_value_grads_out/ppermute | solution.py:50

commit v4 on v3

--- a/solution.py
+++ b/solution.py
@@ -22,8 +22,8 @@
 BLOCKS = 2 * NY
 TILE = 256
 PACE = 4
-PACK_STEP = 2
-PLAN_STEP = 1
+PACK_STEP = 1
+QUERY_STEP = 2
 BACK_STEP = 3
 WINDOW = 1024
 MAX_TILES = 5
@@ -62,20 +62,20 @@
     return lax.optimization_barrier(arrays)
 
 
-def gather_z(x, plan, packed):
+def gather_z(x, query_pieces, packed):
     right = left = x
     pieces = {0: x}
     for step in range(1, NZ // 2):
         right, left = along_z(right, 1), along_z(left, -1)
-        if step == PLAN_STEP:
-            right, left, *plan = together(right, left, *plan)
-        elif step == PACK_STEP:
+        if step == PACK_STEP:
             right, left, *packed = together(right, left, *packed)
-        else:
+        if step == QUERY_STEP:
+            right, left, *query_pieces = together(right, left, *query_pieces)
+        if step not in (PACK_STEP, QUERY_STEP):
             right, left = together(right, left)
         pieces[-step], pieces[step] = right, left
     pieces[-(NZ // 2)] = along_z(right, 1)
-    return [pieces[off] for off in OFFSETS], plan, packed
+    return [pieces[off] for off in OFFSETS], query_pieces, packed
 
 
 def add_low(moving, own):
@@ -490,10 +490,10 @@
     with jax.named_scope("plan"):
         plan = make_plan(pair_of, doc_lengths)
     with jax.named_scope("grads_pack"):
-        out_grad, *query_pieces = together(out_grad, *query_pieces)
         packed_grads = pack_grads(out_grad, forward_out[0])
     with jax.named_scope("keys_values_ring"):
-        gathered, plan, packed_grads = gather_z(kv, plan, packed_grads)
+        gathered, query_pieces, packed = gather_z(kv, query_pieces, [*plan, *packed_grads])
+        plan, packed_grads = packed[:2], packed[2:]
     with jax.named_scope("grads_in"):
         grad_pieces = to_heads(packed_grads, along_y)
     parts = attention_grads(plan, query_pieces, grad_pieces, gathered)

time: 114 us -> 114 us (level)
  starting transfers between devices: 49 us -> 43.6 us
  waiting for transfers between devices: 41.9 us -> 47 us
    ppermute x14, waiting for transfers between devices: 15.2 us -> 26.2 us  [along_z(): lax.ppermute(x, 'ctx', [(c, c // NZ * NZ + (c % NZ + by) % NZ) for c in r...]
    ppermute x15, waiting for transfers between devices: 26.7 us -> 20.8 us  [along_y(): lax.ppermute(x, 'ctx', [(c, (c // NZ + by) % NY * NZ + c % NZ) for c in r...]
    ppermute x15, starting transfers between devices: 27.6 us -> 22.9 us  [along_y(): lax.ppermute(x, 'ctx', [(c, (c // NZ + by) % NY * NZ + c % NZ) for c in r...]
  transfers between devices with their start and end apart: 30 -> 30, of which waited for: 18 -> 17; matrix products, arithmetic and copies ran while one was open for 0% -> 0% of each run, Pallas kernels for 3% -> 3%
where the time goes in v4:
time: 114 us; the launch traced here: 113 us
  waiting for transfers between devices  47 us (41%)
  starting transfers between devices  43.6 us (38%)
  Pallas kernels  18.4 us (16%)
  local copies, waits for them, and re-layouts  3.09 us (3%)
    ppermute x14, waiting for transfers between devices, along_z(): lax.ppermute(x, 'ctx', [(c, c // NZ * NZ + (c % NZ + by) % NZ) for c in r...  26.2 us
    ppermute x15, starting transfers between devices, along_y(): lax.ppermute(x, 'ctx', [(c, (c // NZ + by) % NY * NZ + c % NZ) for c in r...  22.9 us
    ppermute x15, waiting for transfers between devices, along_y(): lax.ppermute(x, 'ctx', [(c, (c // NZ + by) % NY * NZ + c % NZ) for c in r...  20.8 us
    ppermute x14, starting transfers between devices, along_z(): lax.ppermute(x, 'ctx', [(c, c // NZ * NZ + (c % NZ + by) % NZ) for c in r...  20.6 us
    pallas_call x1, Pallas kernels, attention_grads(): pl.pallas_call(main_body, out_shape=[jax.ShapeDtypeStruct((2 * ROWS, DIM)...  13.8 us
    unnamed x15, local copies, waits for them, and re-layouts  3.06 us
  transfers between devices with their start and end apart: 30, of which 17 were waited for; matrix products, arithmetic and copies ran while one was open for 0% of the time, Pallas kernels for 3%

profile of v4, /device:TPU:2, one launch (start us, length us, event | category | flops | bytes accessed | tf_op | source)
XLA Modules:
  0.0 113.3 jit_solution(5120027167872212488)
XLA Ops:
  0.7 0.9 copy-done.2
  1.6 0.9 copy-done.3
  2.5 1.7 %collective-permute-start = (bf16[128,256]{1,0:T(8,128)(2,1)S(1)}, bf16[128,256]{1,0:T(8,128)(2,1)S(1)}, u32[]{:S(2)}, u32[]{:S(2)}) collective-permute-start(bf16[128,256]{1,0:T(8,128)(2,1)S(1)} %get-tuple-element.68), channel_id=1, source_target_pairs={{0,8},{1,9},{2,10},{3,11},{4,12},{5,13},{6,14},{7,15},{8,16},{9,17... | collective-permute-start | bytes 196616 | tf_op jit(solution)/shard_map/keys_values_in/ppermute | solution.py:50
  4.2 2.9 %collective-permute-start.1 = (bf16[128,256]{1,0:T(8,128)(2,1)S(1)}, bf16[128,256]{1,0:T(8,128)(2,1)S(1)}, u32[]{:S(2)}, u32[]{:S(2)}) collective-permute-start(bf16[128,256]{1,0:T(8,128)(2,1)S(1)} %get-tuple-element.69), channel_id=1, source_target_pairs={{0,16},{1,17},{2,18},{3,19},{4,20},{5,21},{6,22},{7,23},{8,24},{9,... | collective-permute-start | bytes 196616 | tf_op jit(solution)/shard_map/keys_values_in/ppermute | solution.py:50
  7.1 1.3 %collective-permute-start.2 = (bf16[128,256]{1,0:T(8,128)(2,1)S(1)}, bf16[128,256]{1,0:T(8,128)(2,1)S(1)}, u32[]{:S(2)}, u32[]{:S(2)}) collective-permute-start(bf16[128,256]{1,0:T(8,128)(2,1)S(1)} %get-tuple-element.70), channel_id=1, source_target_pairs={{0,24},{1,25},{2,26},{3,27},{4,28},{5,29},{6,30},{7,31},{8,0},{9,1... | collective-permute-start | bytes 196616 | tf_op jit(solution)/shard_map/keys_values_in/ppermute | solution.py:50
  8.4 1.2 %copy-done = bf16[1,128,4096]{2,1,0:T(8,128)(2,1)S(1)} copy-done((bf16[1,128,4096]{2,1,0:T(8,128)(2,1)S(1)}, bf16[1,128,4096]{2,1,0:T(8,128)(2,1)}, u32[]{:S(2)}) %copy-start) | copy-done | bytes 1048600
  9.8 1.1 %collective-permute-done.1 = bf16[128,256]{1,0:T(8,128)(2,1)S(1)} collective-permute-done((bf16[128,256]{1,0:T(8,128)(2,1)S(1)}, bf16[128,256]{1,0:T(8,128)(2,1)S(1)}, u32[]{:S(2)}, u32[]{:S(2)}) %collective-permute-start.1) | collective-permute-done | bytes 65568 | tf_op jit(solution)/shard_map/keys_values_in/ppermute | solution.py:50
  10.9 0.4 collective-permute-done.2
  11.4 5.9 %collective-permute-start.4 = (bf16[512,256]{1,0:T(8,128)(2,1)S(1)}, bf16[512,256]{1,0:T(8,128)(2,1)S(1)}, u32[]{:S(2)}, u32[]{:S(2)}) collective-permute-start(bf16[512,256]{1,0:T(8,128)(2,1)S(1)} %constant_dynamic-update-slice_fusion.refs_12_), channel_id=1, source_target_pairs={{0,7},{1,0},{2,1},{3,2},{4,3},{5,4},{6,5},{7,6},{8,15},{9,8},{10,9... | collective-permute-start | bytes 786440 | tf_op jit(solution)/shard_map/keys_values_ring/ppermute | solution.py:56
  17.4 1.7 %make_plan.1 = (s32[272]{0:T(512)S(1)}, s32[8,512]{1,0:T(8,128)S(1)}) custom-call(s32[1,32]{1,0:T(1,128)S(1)} %copy-done.4, s32[1,16]{1,0:T(1,128)S(1)} %copy-done.5), custom_call_target="tpu_custom_call" | custom-call | tf_op jit(solution)/shard_map/plan/make_plan/pallas_call | solution.py:257
  19.0 0.9 collective-permute-start.8
  19.9 3.2 %collective-permute-start.9 = (bf16[1024,128]{1,0:T(8,128)(2,1)S(1)}, bf16[1024,128]{1,0:T(8,128)(2,1)S(1)}, u32[]{:S(2)}, u32[]{:S(2)}) collective-permute-start(bf16[1024,128]{1,0:T(8,128)(2,1)S(1)} %get-tuple-element.91), channel_id=1, source_target_pairs={{0,16},{1,17},{2,18},{3,19},{4,20},{5,21},{6,22},{7,23},{8,24},{9,... | collective-permute-start | bytes 786440 | tf_op jit(solution)/shard_map/queries_in/ppermute | solution.py:50
  23.1 0.7 collective-permute-start.10
  23.9 0.7 pack_grads.1
  24.6 1.2 %collective-permute-done.3.refs_11_ = bf16[512,256]{1,0:T(8,128)(2,1)S(1)} collective-permute-done((bf16[512,256]{1,0:T(8,128)(2,1)S(1)}, bf16[512,256]{1,0:T(8,128)(2,1)S(1)}, u32[]{:S(2)}, u32[]{:S(2)}) %collective-permute-start.3) | collective-permute-done | bytes 262176 | tf_op jit(solution)/shard_map/keys_values_ring/ppermute | solution.py:56
  25.8 3.2 %collective-permute-start.7 = (bf16[512,256]{1,0:T(8,128)(2,1)S(1)}, bf16[512,256]{1,0:T(8,128)(2,1)S(1)}, u32[]{:S(2)}, u32[]{:S(2)}) collective-permute-start(bf16[512,256]{1,0:T(8,128)(2,1)S(1)} %collective-permute-done.4.refs_13_), channel_id=1, source_target_pairs={{0,7},{1,0},{2,1},{3,2},{4,3},{5,4},{6,5},{7,6},{8,15},{9,8},{10,9... | collective-permute-start | bytes 786440 | tf_op jit(solution)/shard_map/keys_values_ring/ppermute | solution.py:56
  29.1 0.8 collective-permute-done.8.refs_1_
  29.9 3.6 %collective-permute-done.9.refs_2_ = bf16[1024,128]{1,0:T(8,128)(2,1)S(1)} collective-permute-done((bf16[1024,128]{1,0:T(8,128)(2,1)S(1)}, bf16[1024,128]{1,0:T(8,128)(2,1)S(1)}, u32[]{:S(2)}, u32[]{:S(2)}) %collective-permute-start.9) | collective-permute-done | bytes 262176 | tf_op jit(solution)/shard_map/queries_in/ppermute | solution.py:50
  33.4 0.4 collective-permute-done.10.refs_3_
  33.8 3.2 %collective-permute-start.15 = (bf16[512,256]{1,0:T(8,128)(2,1)S(1)}, bf16[512,256]{1,0:T(8,128)(2,1)S(1)}, u32[]{:S(2)}, u32[]{:S(2)}) collective-permute-start(bf16[512,256]{1,0:T(8,128)(2,1)S(1)} %collective-permute-done.7.refs_14_), channel_id=1, source_target_pairs={{0,7},{1,0},{2,1},{3,2},{4,3},{5,4},{6,5},{7,6},{8,15},{9,8},{10,9... | collective-permute-start | bytes 786440 | tf_op jit(solution)/shard_map/keys_values_ring/ppermute | solution.py:56
  37.0 1.6 %collective-permute-start.11 = (bf16[1152,128]{1,0:T(8,128)(2,1)S(1)}, bf16[1152,128]{1,0:T(8,128)(2,1)S(1)}, u32[]{:S(2)}, u32[]{:S(2)}) collective-permute-start(bf16[1152,128]{1,0:T(8,128)(2,1)S(1)} %get-tuple-element.98), channel_id=1, source_target_pairs={{0,8},{1,9},{2,10},{3,11},{4,12},{5,13},{6,14},{7,15},{8,16},{9,17... | collective-permute-start | bytes 884744 | tf_op jit(solution)/shard_map/grads_in/ppermute | solution.py:50
  38.6 2.5 %collective-permute-start.12 = (bf16[1152,128]{1,0:T(8,128)(2,1)S(1)}, bf16[1152,128]{1,0:T(8,128)(2,1)S(1)}, u32[]{:S(2)}, u32[]{:S(2)}) collective-permute-start(bf16[1152,128]{1,0:T(8,128)(2,1)S(1)} %get-tuple-element.99), channel_id=1, source_target_pairs={{0,16},{1,17},{2,18},{3,19},{4,20},{5,21},{6,22},{7,23},{8,24},{9,... | collective-permute-start | bytes 884744 | tf_op jit(solution)/shard_map/grads_in/ppermute | solution.py:50
  41.1 0.7 collective-permute-start.13
  41.9 0.3 collective-permute-done.14.refs_9_
  42.2 4.5 %collective-permute-done.11.refs_5_ = bf16[1152,128]{1,0:T(8,128)(2,1)S(1)} collective-permute-done((bf16[1152,128]{1,0:T(8,128)(2,1)S(1)}, bf16[1152,128]{1,0:T(8,128)(2,1)S(1)}, u32[]{:S(2)}, u32[]{:S(2)}) %collective-permute-start.11) | collective-permute-done | bytes 294944 | tf_op jit(solution)/shard_map/grads_in/ppermute | solution.py:50
  46.7 7.1 %collective-permute-done.12.refs_6_ = bf16[1152,128]{1,0:T(8,128)(2,1)S(1)} collective-permute-done((bf16[1152,128]{1,0:T(8,128)(2,1)S(1)}, bf16[1152,128]{1,0:T(8,128)(2,1)S(1)}, u32[]{:S(2)}, u32[]{:S(2)}) %collective-permute-start.12) | collective-permute-done | bytes 294944 | tf_op jit(solution)/shard_map/grads_in/ppermute | solution.py:50
  53.8 13.8 %attention_grads.1 = (bf16[1024,128]{1,0:T(8,128)(2,1)S(1)}, bf16[1024,128]{1,0:T(8,128)(2,1)S(1)}, bf16[1024,128]{1,0:T(8,128)(2,1)S(1)}, bf16[1024,128]{1,0:T(...) custom-call(s32[272]{0:T(512)S(1)} %get-tuple-element.85.plan, ...), custom_call_target="tpu_custom_call" | custom-call | tf_op jit(solution)/shard_map/attention_grads/pallas_call | solution.py:400
  67.6 1.5 %collective-permute-start.17 = (bf16[512,256]{1,0:T(8,128)(2,1)S(1)}, bf16[512,256]{1,0:T(8,128)(2,1)S(1)}, u32[]{:S(2)}, u32[]{:S(2)}) collective-permute-start(bf16[512,256]{1,0:T(8,128)(2,1)S(1)} %get-tuple-element.105), channel_id=1, source_target_pairs={{0,7},{1,0},{2,1},{3,2},{4,3},{5,4},{6,5},{7,6},{8,15},{9,8},{10,9... | collective-permute-start | bytes 786440 | tf_op jit(solution)/shard_map/key_value_grads_ring/ppermute | solution.py:56
  69.1 0.6 collective-permute-start.18
  69.7 4.3 %collective-permute-done.17 = bf16[512,256]{1,0:T(8,128)(2,1)S(1)} collective-permute-done((bf16[512,256]{1,0:T(8,128)(2,1)S(1)}, bf16[512,256]{1,0:T(8,128)(2,1)S(1)}, u32[]{:S(2)}, u32[]{:S(2)}) %collective-permute-start.17) | collective-permute-done | bytes 262176 | tf_op jit(solution)/shard_map/key_value_grads_ring/ppermute | solution.py:56
  74.1 3.7 %collective-permute-done.18 = bf16[512,256]{1,0:T(8,128)(2,1)S(1)} collective-permute-done((bf16[512,256]{1,0:T(8,128)(2,1)S(1)}, bf16[512,256]{1,0:T(8,128)(2,1)S(1)}, u32[]{:S(2)}, u32[]{:S(2)}) %collective-permute-start.18) | collective-permute-done | bytes 262176 | tf_op jit(solution)/shard_map/key_value_grads_ring/ppermute | solution.py:56
  77.8 1.5 %collective-permute-start.19 = (bf16[512,256]{1,0:T(8,128)(2,1)S(1)}, bf16[512,256]{1,0:T(8,128)(2,1)S(1)}, u32[]{:S(2)}, u32[]{:S(2)}) collective-permute-start(bf16[512,256]{1,0:T(8,128)(2,1)S(1)} %add_convert_fusion.5), channel_id=1, source_target_pairs={{0,7},{1,0},{2,1},{3,2},{4,3},{5,4},{6,5},{7,6},{8,15},{9,8},{10,9... | collective-permute-start | bytes 786440 | tf_op jit(solution)/shard_map/key_value_grads_ring/ppermute | solution.py:56
  79.4 0.6 collective-permute-start.20
  80.1 1.0 collective-permute-start.23
  81.1 1.1 %collective-permute-start.24 = (bf16[1024,128]{1,0:T(8,128)(2,1)S(1)}, bf16[1024,128]{1,0:T(8,128)(2,1)S(1)}, u32[]{:S(2)}, u32[]{:S(2)}) collective-permute-start(bf16[1024,128]{1,0:T(8,128)(2,1)S(1)} %get-tuple-element.117), channel_id=1, source_target_pairs={{0,16},{1,17},{2,18},{3,19},{4,20},{5,21},{6,22},{7,23},{8,24},{9,... | collective-permute-start | bytes 786440 | tf_op jit(solution)/shard_map/query_grads_out/ppermute | solution.py:50
  82.2 1.0 collective-permute-start.25
  83.3 3.3 %collective-permute-done.19 = bf16[512,256]{1,0:T(8,128)(2,1)S(1)} collective-permute-done((bf16[512,256]{1,0:T(8,128)(2,1)S(1)}, bf16[512,256]{1,0:T(8,128)(2,1)S(1)}, u32[]{:S(2)}, u32[]{:S(2)}) %collective-permute-start.19) | collective-permute-done | bytes 262176 | tf_op jit(solution)/shard_map/key_value_grads_ring/ppermute | solution.py:56
  86.6 3.2 %collective-permute-done.20 = bf16[512,256]{1,0:T(8,128)(2,1)S(1)} collective-permute-done((bf16[512,256]{1,0:T(8,128)(2,1)S(1)}, bf16[512,256]{1,0:T(8,128)(2,1)S(1)}, u32[]{:S(2)}, u32[]{:S(2)}) %collective-permute-start.20) | collective-permute-done | bytes 262176 | tf_op jit(solution)/shard_map/key_value_grads_ring/ppermute | solution.py:56
  90.0 2.1 %collective-permute-start.22 = (bf16[512,256]{1,0:T(8,128)(2,1)S(1)}, bf16[512,256]{1,0:T(8,128)(2,1)S(1)}, u32[]{:S(2)}, u32[]{:S(2)}) collective-permute-start(bf16[512,256]{1,0:T(8,128)(2,1)S(1)} %add_convert_fusion.2), channel_id=1, source_target_pairs={{0,1},{1,2},{2,3},{3,4},{4,5},{5,6},{6,7},{7,0},{8,9},{9,10},{10,1... | collective-permute-start | bytes 786440 | tf_op jit(solution)/shard_map/key_value_grads_ring/ppermute | solution.py:56
  92.1 6.5 %collective-permute-done.21 = bf16[512,256]{1,0:T(8,128)(2,1)S(1)} collective-permute-done((bf16[512,256]{1,0:T(8,128)(2,1)S(1)}, bf16[512,256]{1,0:T(8,128)(2,1)S(1)}, u32[]{:S(2)}, u32[]{:S(2)}) %collective-permute-start.21) | collective-permute-done | bytes 262176 | tf_op jit(solution)/shard_map/key_value_grads_ring/ppermute | solution.py:56
  98.6 1.8 %collective-permute-start.26 = (bf16[512,256]{1,0:T(8,128)(2,1)S(1)}, bf16[512,256]{1,0:T(8,128)(2,1)S(1)}, u32[]{:S(2)}, u32[]{:S(2)}) collective-permute-start(bf16[512,256]{1,0:T(8,128)(2,1)S(1)} %add_convert_fusion.1), channel_id=1, source_target_pairs={{0,7},{1,0},{2,1},{3,2},{4,3},{5,4},{6,5},{7,6},{8,15},{9,8},{10,9... | collective-permute-start | bytes 786440 | tf_op jit(solution)/shard_map/key_value_grads_ring/ppermute | solution.py:56
  100.4 1.3 %place_wide.1 = bf16[128,4096]{1,0:T(8,128)(2,1)} custom-call(bf16[1024,128]{1,0:T(8,128)(2,1)S(1)} %get-tuple-element.121.refs_0_, bf16[1024,128]{1,0:T(8,128)(2,1)S(1)} %collective-permute-done.23.refs_1_, bf16[1024,128]{1,0:T(8,128)(2,1)S(1)} %collective-permute-done.24.refs_2_, bf16[1024,128]{1,0:T(8,128)(2,1)S(1)} %collective-permute-done.25.refs_3_), custom_call_target="tpu_custom_call" | custom-call | tf_op jit(solution)/shard_map/key_value_grads_ring/place_wide/pallas_call | solution.py:444
  101.7 3.6 %collective-permute-done.26 = bf16[512,256]{1,0:T(8,128)(2,1)S(1)} collective-permute-done((bf16[512,256]{1,0:T(8,128)(2,1)S(1)}, bf16[512,256]{1,0:T(8,128)(2,1)S(1)}, u32[]{:S(2)}, u32[]{:S(2)}) %collective-permute-start.26) | collective-permute-done | bytes 262176 | tf_op jit(solution)/shard_map/key_value_grads_ring/ppermute | solution.py:56
  105.5 1.6 %collective-permute-start.28 = (bf16[128,256]{1,0:T(8,128)(2,1)S(1)}, bf16[128,256]{1,0:T(8,128)(2,1)S(1)}, u32[]{:S(2)}, u32[]{:S(2)}) collective-permute-start(bf16[128,256]{1,0:T(8,128)(2,1)S(1)} %get-tuple-element.132), channel_id=1, source_target_pairs={{0,16},{1,17},{2,18},{3,19},{4,20},{5,21},{6,22},{7,23},{8,24},{9,... | collective-permute-start | bytes 196616 | tf_op jit(solution)/shard_map/key_value_grads_out/ppermute | solution.py:50
  107.1 2.5 %collective-permute-start.27 = (bf16[128,256]{1,0:T(8,128)(2,1)S(1)}, bf16[128,256]{1,0:T(8,128)(2,1)S(1)}, u32[]{:S(2)}, u32[]{:S(2)}) collective-permute-start(bf16[128,256]{1,0:T(8,128)(2,1)S(1)} %get-tuple-element.133), channel_id=1, source_target_pairs={{0,24},{1,25},{2,26},{3,27},{4,28},{5,29},{6,30},{7,31},{8,0},{9,1... | collective-permute-start | bytes 196616 | tf_op jit(solution)/shard_map/key_value_grads_out/ppermute | solution.py:50
  109.6 2.1 %collective-permute-done.29.refs_3_ = bf16[128,256]{1,0:T(8,128)(2,1)S(1)} collective-permute-done((bf16[128,256]{1,0:T(8,128)(2,1)S(1)}, bf16[128,256]{1,0:T(8,128)(2,1)S(1)}, u32[]{:S(2)}, u32[]{:S(2)}) %collective-permute-start.29) | collective-permute-done | bytes 65568 | tf_op jit(solution)/shard_map/key_value_grads_out/ppermute | solution.py:50
  111.7 0.9 collective-permute-done.27.refs_1_
  112.5 0.8 place_kv.1
  (42 shorter events, 0.8 us)
Async XLA Ops:
  0.6 22.5 %collective-permute-start.5 = (bf16[128,4096]{1,0:T(8,128)(2,1)}, bf16[128,4096]{1,0:T(8,128)(2,1)S(1)}, u32[]{:S(2)}, u32[]{:S(2)}) collective-permute-start(bf16[128,4096]{1,0:T(8,128)(2,1)} %bitcast.13), channel_id=1, source_target_pairs={{0,224},{32,0},{64,32},{96,64},{128,96},{160,128},{192,160},{224,1... | collective-permute-start | bytes 3145736 | tf_op jit(solution)/shard_map/grads_shift/ppermute | solution.py:479
  0.7 0.9 copy-start.2
  1.6 0.9 copy-start.3
  2.5 7.3 %collective-permute-start = (bf16[128,256]{1,0:T(8,128)(2,1)S(1)}, bf16[128,256]{1,0:T(8,128)(2,1)S(1)}, u32[]{:S(2)}, u32[]{:S(2)}) collective-permute-start(bf16[128,256]{1,0:T(8,128)(2,1)S(1)} %get-tuple-element.68), channel_id=1, source_target_pairs={{0,8},{1,9},{2,10},{3,11},{4,12},{5,13},{6,14},{7,15},{8,16},{9,17... | collective-permute-start | bytes 196616 | tf_op jit(solution)/shard_map/keys_values_in/ppermute | solution.py:50
  4.2 6.8 %collective-permute-start.1 = (bf16[128,256]{1,0:T(8,128)(2,1)S(1)}, bf16[128,256]{1,0:T(8,128)(2,1)S(1)}, u32[]{:S(2)}, u32[]{:S(2)}) collective-permute-start(bf16[128,256]{1,0:T(8,128)(2,1)S(1)} %get-tuple-element.69), channel_id=1, source_target_pairs={{0,16},{1,17},{2,18},{3,19},{4,20},{5,21},{6,22},{7,23},{8,24},{9,... | collective-permute-start | bytes 196616 | tf_op jit(solution)/shard_map/keys_values_in/ppermute | solution.py:50
  7.1 4.3 %collective-permute-start.2 = (bf16[128,256]{1,0:T(8,128)(2,1)S(1)}, bf16[128,256]{1,0:T(8,128)(2,1)S(1)}, u32[]{:S(2)}, u32[]{:S(2)}) collective-permute-start(bf16[128,256]{1,0:T(8,128)(2,1)S(1)} %get-tuple-element.70), channel_id=1, source_target_pairs={{0,24},{1,25},{2,26},{3,27},{4,28},{5,29},{6,30},{7,31},{8,0},{9,1... | collective-permute-start | bytes 196616 | tf_op jit(solution)/shard_map/keys_values_in/ppermute | solution.py:50
  8.4 1.2 %copy-start = (bf16[1,128,4096]{2,1,0:T(8,128)(2,1)S(1)}, bf16[1,128,4096]{2,1,0:T(8,128)(2,1)}, u32[]{:S(2)}) copy-start(bf16[1,128,4096]{2,1,0:T(8,128)(2,1)} %param.7) | copy-start | bytes 3145732
  9.6 14.2 %copy-start.1 = (bf16[1,128,4096]{2,1,0:T(8,128)(2,1)S(1)}, bf16[1,128,4096]{2,1,0:T(8,128)(2,1)}, u32[]{:S(2)}) copy-start(bf16[1,128,4096]{2,1,0:T(8,128)(2,1)} %param.10) | copy-start | bytes 3145732
  11.4 6.0 %copy-start.4 = (s32[1,32]{1,0:T(1,128)S(1)}, s32[1,32]{1,0:T(1,128)}, u32[]{:S(2)}) copy-start(s32[1,32]{1,0:T(1,128)} %pairs.1) | copy-start | bytes 388
  11.4 6.0 %copy-start.5 = (s32[1,16]{1,0:T(1,128)S(1)}, s32[1,16]{1,0:T(1,128)}, u32[]{:S(2)}) copy-start(s32[1,16]{1,0:T(1,128)} %lengths.1) | copy-start | bytes 196
  11.4 13.2 %collective-permute-start.4 = (bf16[512,256]{1,0:T(8,128)(2,1)S(1)}, bf16[512,256]{1,0:T(8,128)(2,1)S(1)}, u32[]{:S(2)}, u32[]{:S(2)}) collective-permute-start(bf16[512,256]{1,0:T(8,128)(2,1)S(1)} %constant_dynamic-update-slice_fusion.refs_12_), channel_id=1, source_target_pairs={{0,7},{1,0},{2,1},{3,2},{4,3},{5,4},{6,5},{7,6},{8,15},{9,8},{10,9... | collective-permute-start | bytes 786440 | tf_op jit(solution)/shard_map/keys_values_ring/ppermute | solution.py:56
  17.3 8.5 %collective-permute-start.3 = (bf16[512,256]{1,0:T(8,128)(2,1)S(1)}, bf16[512,256]{1,0:T(8,128)(2,1)S(1)}, u32[]{:S(2)}, u32[]{:S(2)}) collective-permute-start(bf16[512,256]{1,0:T(8,128)(2,1)S(1)} %constant_dynamic-update-slice_fusion.refs_12_), channel_id=1, source_target_pairs={{0,1},{1,2},{2,3},{3,4},{4,5},{5,6},{6,7},{7,0},{8,9},{9,10},{10,1... | collective-permute-start | bytes 786440 | tf_op jit(solution)/shard_map/keys_values_ring/ppermute | solution.py:56
  19.0 10.8 %collective-permute-start.8 = (bf16[1024,128]{1,0:T(8,128)(2,1)S(1)}, bf16[1024,128]{1,0:T(8,128)(2,1)S(1)}, u32[]{:S(2)}, u32[]{:S(2)}) collective-permute-start(bf16[1024,128]{1,0:T(8,128)(2,1)S(1)} %get-tuple-element.90), channel_id=1, source_target_pairs={{0,8},{1,9},{2,10},{3,11},{4,12},{5,13},{6,14},{7,15},{8,16},{9,17... | collective-permute-start | bytes 786440 | tf_op jit(solution)/shard_map/queries_in/ppermute | solution.py:50
  19.9 13.5 %collective-permute-start.9 = (bf16[1024,128]{1,0:T(8,128)(2,1)S(1)}, bf16[1024,128]{1,0:T(8,128)(2,1)S(1)}, u32[]{:S(2)}, u32[]{:S(2)}) collective-permute-start(bf16[1024,128]{1,0:T(8,128)(2,1)S(1)} %get-tuple-element.91), channel_id=1, source_target_pairs={{0,16},{1,17},{2,18},{3,19},{4,20},{5,21},{6,22},{7,23},{8,24},{9,... | collective-permute-start | bytes 786440 | tf_op jit(solution)/shard_map/queries_in/ppermute | solution.py:50
  23.1 10.7 %collective-permute-start.10 = (bf16[1024,128]{1,0:T(8,128)(2,1)S(1)}, bf16[1024,128]{1,0:T(8,128)(2,1)S(1)}, u32[]{:S(2)}, u32[]{:S(2)}) collective-permute-start(bf16[1024,128]{1,0:T(8,128)(2,1)S(1)} %get-tuple-element.92), channel_id=1, source_target_pairs={{0,24},{1,25},{2,26},{3,27},{4,28},{5,29},{6,30},{7,31},{8,0},{9,1... | collective-permute-start | bytes 786440 | tf_op jit(solution)/shard_map/queries_in/ppermute | solution.py:50
  25.8 8.0 %collective-permute-start.6 = (bf16[512,256]{1,0:T(8,128)(2,1)S(1)}, bf16[512,256]{1,0:T(8,128)(2,1)S(1)}, u32[]{:S(2)}, u32[]{:S(2)}) collective-permute-start(bf16[512,256]{1,0:T(8,128)(2,1)S(1)} %collective-permute-done.3.refs_11_), channel_id=1, source_target_pairs={{0,1},{1,2},{2,3},{3,4},{4,5},{5,6},{6,7},{7,0},{8,9},{9,10},{10,1... | collective-permute-start | bytes 786440 | tf_op jit(solution)/shard_map/keys_values_ring/ppermute | solution.py:56
  25.8 8.0 %collective-permute-start.7 = (bf16[512,256]{1,0:T(8,128)(2,1)S(1)}, bf16[512,256]{1,0:T(8,128)(2,1)S(1)}, u32[]{:S(2)}, u32[]{:S(2)}) collective-permute-start(bf16[512,256]{1,0:T(8,128)(2,1)S(1)} %collective-permute-done.4.refs_13_), channel_id=1, source_target_pairs={{0,7},{1,0},{2,1},{3,2},{4,3},{5,4},{6,5},{7,6},{8,15},{9,8},{10,9... | collective-permute-start | bytes 786440 | tf_op jit(solution)/shard_map/keys_values_ring/ppermute | solution.py:56
  33.8 8.4 %collective-permute-start.14 = (bf16[512,256]{1,0:T(8,128)(2,1)S(1)}, bf16[512,256]{1,0:T(8,128)(2,1)S(1)}, u32[]{:S(2)}, u32[]{:S(2)}) collective-permute-start(bf16[512,256]{1,0:T(8,128)(2,1)S(1)} %collective-permute-done.6.refs_10_), channel_id=1, source_target_pairs={{0,1},{1,2},{2,3},{3,4},{4,5},{5,6},{6,7},{7,0},{8,9},{9,10},{10,1... | collective-permute-start | bytes 786440 | tf_op jit(solution)/shard_map/keys_values_ring/ppermute | solution.py:56
  33.8 8.4 %collective-permute-start.15 = (bf16[512,256]{1,0:T(8,128)(2,1)S(1)}, bf16[512,256]{1,0:T(8,128)(2,1)S(1)}, u32[]{:S(2)}, u32[]{:S(2)}) collective-permute-start(bf16[512,256]{1,0:T(8,128)(2,1)S(1)} %collective-permute-done.7.refs_14_), channel_id=1, source_target_pairs={{0,7},{1,0},{2,1},{3,2},{4,3},{5,4},{6,5},{7,6},{8,15},{9,8},{10,9... | collective-permute-start | bytes 786440 | tf_op jit(solution)/shard_map/keys_values_ring/ppermute | solution.py:56
  37.0 9.6 %collective-permute-start.11 = (bf16[1152,128]{1,0:T(8,128)(2,1)S(1)}, bf16[1152,128]{1,0:T(8,128)(2,1)S(1)}, u32[]{:S(2)}, u32[]{:S(2)}) collective-permute-start(bf16[1152,128]{1,0:T(8,128)(2,1)S(1)} %get-tuple-element.98), channel_id=1, source_target_pairs={{0,8},{1,9},{2,10},{3,11},{4,12},{5,13},{6,14},{7,15},{8,16},{9,17... | collective-permute-start | bytes 884744 | tf_op jit(solution)/shard_map/grads_in/ppermute | solution.py:50
  38.6 15.2 %collective-permute-start.12 = (bf16[1152,128]{1,0:T(8,128)(2,1)S(1)}, bf16[1152,128]{1,0:T(8,128)(2,1)S(1)}, u32[]{:S(2)}, u32[]{:S(2)}) collective-permute-start(bf16[1152,128]{1,0:T(8,128)(2,1)S(1)} %get-tuple-element.99), channel_id=1, source_target_pairs={{0,16},{1,17},{2,18},{3,19},{4,20},{5,21},{6,22},{7,23},{8,24},{9,... | collective-permute-start | bytes 884744 | tf_op jit(solution)/shard_map/grads_in/ppermute | solution.py:50
  41.1 12.7 %collective-permute-start.13 = (bf16[1152,128]{1,0:T(8,128)(2,1)S(1)}, bf16[1152,128]{1,0:T(8,128)(2,1)S(1)}, u32[]{:S(2)}, u32[]{:S(2)}) collective-permute-start(bf16[1152,128]{1,0:T(8,128)(2,1)S(1)} %get-tuple-element.100), channel_id=1, source_target_pairs={{0,24},{1,25},{2,26},{3,27},{4,28},{5,29},{6,30},{7,31},{8,0},{9,1... | collective-permute-start | bytes 884744 | tf_op jit(solution)/shard_map/grads_in/ppermute | solution.py:50
  42.2 11.6 %collective-permute-start.16 = (bf16[512,256]{1,0:T(8,128)(2,1)S(1)}, bf16[512,256]{1,0:T(8,128)(2,1)S(1)}, u32[]{:S(2)}, u32[]{:S(2)}) collective-permute-start(bf16[512,256]{1,0:T(8,128)(2,1)S(1)} %collective-permute-done.14.refs_9_), channel_id=1, source_target_pairs={{0,1},{1,2},{2,3},{3,4},{4,5},{5,6},{6,7},{7,0},{8,9},{9,10},{10,1... | collective-permute-start | bytes 786440 | tf_op jit(solution)/shard_map/keys_values_ring/ppermute | solution.py:56
  67.6 6.5 %collective-permute-start.17 = (bf16[512,256]{1,0:T(8,128)(2,1)S(1)}, bf16[512,256]{1,0:T(8,128)(2,1)S(1)}, u32[]{:S(2)}, u32[]{:S(2)}) collective-permute-start(bf16[512,256]{1,0:T(8,128)(2,1)S(1)} %get-tuple-element.105), channel_id=1, source_target_pairs={{0,7},{1,0},{2,1},{3,2},{4,3},{5,4},{6,5},{7,6},{8,15},{9,8},{10,9... | collective-permute-start | bytes 786440 | tf_op jit(solution)/shard_map/key_value_grads_ring/ppermute | solution.py:56
  69.1 8.7 %collective-permute-start.18 = (bf16[512,256]{1,0:T(8,128)(2,1)S(1)}, bf16[512,256]{1,0:T(8,128)(2,1)S(1)}, u32[]{:S(2)}, u32[]{:S(2)}) collective-permute-start(bf16[512,256]{1,0:T(8,128)(2,1)S(1)} %get-tuple-element.106), channel_id=1, source_target_pairs={{0,1},{1,2},{2,3},{3,4},{4,5},{5,6},{6,7},{7,0},{8,9},{9,10},{10,1... | collective-permute-start | bytes 786440 | tf_op jit(solution)/shard_map/key_value_grads_ring/ppermute | solution.py:56
  77.8 8.7 %collective-permute-start.19 = (bf16[512,256]{1,0:T(8,128)(2,1)S(1)}, bf16[512,256]{1,0:T(8,128)(2,1)S(1)}, u32[]{:S(2)}, u32[]{:S(2)}) collective-permute-start(bf16[512,256]{1,0:T(8,128)(2,1)S(1)} %add_convert_fusion.5), channel_id=1, source_target_pairs={{0,7},{1,0},{2,1},{3,2},{4,3},{5,4},{6,5},{7,6},{8,15},{9,8},{10,9... | collective-permute-start | bytes 786440 | tf_op jit(solution)/shard_map/key_value_grads_ring/ppermute | solution.py:56
  79.4 10.3 %collective-permute-start.20 = (bf16[512,256]{1,0:T(8,128)(2,1)S(1)}, bf16[512,256]{1,0:T(8,128)(2,1)S(1)}, u32[]{:S(2)}, u32[]{:S(2)}) collective-permute-start(bf16[512,256]{1,0:T(8,128)(2,1)S(1)} %add_convert_fusion.4), channel_id=1, source_target_pairs={{0,1},{1,2},{2,3},{3,4},{4,5},{5,6},{6,7},{7,0},{8,9},{9,10},{10,1... | collective-permute-start | bytes 786440 | tf_op jit(solution)/shard_map/key_value_grads_ring/ppermute | solution.py:56
  80.1 12.0 %collective-permute-start.23 = (bf16[1024,128]{1,0:T(8,128)(2,1)S(1)}, bf16[1024,128]{1,0:T(8,128)(2,1)S(1)}, u32[]{:S(2)}, u32[]{:S(2)}) collective-permute-start(bf16[1024,128]{1,0:T(8,128)(2,1)S(1)} %get-tuple-element.116), channel_id=1, source_target_pairs={{0,24},{1,25},{2,26},{3,27},{4,28},{5,29},{6,30},{7,31},{8,0},{9,1... | collective-permute-start | bytes 786440 | tf_op jit(solution)/shard_map/query_grads_out/ppermute | solution.py:50
  81.1 11.0 %collective-permute-start.24 = (bf16[1024,128]{1,0:T(8,128)(2,1)S(1)}, bf16[1024,128]{1,0:T(8,128)(2,1)S(1)}, u32[]{:S(2)}, u32[]{:S(2)}) collective-permute-start(bf16[1024,128]{1,0:T(8,128)(2,1)S(1)} %get-tuple-element.117), channel_id=1, source_target_pairs={{0,16},{1,17},{2,18},{3,19},{4,20},{5,21},{6,22},{7,23},{8,24},{9,... | collective-permute-start | bytes 786440 | tf_op jit(solution)/shard_map/query_grads_out/ppermute | solution.py:50
  82.2 9.9 %collective-permute-start.25 = (bf16[1024,128]{1,0:T(8,128)(2,1)S(1)}, bf16[1024,128]{1,0:T(8,128)(2,1)S(1)}, u32[]{:S(2)}, u32[]{:S(2)}) collective-permute-start(bf16[1024,128]{1,0:T(8,128)(2,1)S(1)} %get-tuple-element.118), channel_id=1, source_target_pairs={{0,8},{1,9},{2,10},{3,11},{4,12},{5,13},{6,14},{7,15},{8,16},{9,17... | collective-permute-start | bytes 786440 | tf_op jit(solution)/shard_map/query_grads_out/ppermute | solution.py:50
  89.8 8.8 %collective-permute-start.21 = (bf16[512,256]{1,0:T(8,128)(2,1)S(1)}, bf16[512,256]{1,0:T(8,128)(2,1)S(1)}, u32[]{:S(2)}, u32[]{:S(2)}) collective-permute-start(bf16[512,256]{1,0:T(8,128)(2,1)S(1)} %add_convert_fusion.3), channel_id=1, source_target_pairs={{0,7},{1,0},{2,1},{3,2},{4,3},{5,4},{6,5},{7,6},{8,15},{9,8},{10,9... | collective-permute-start | bytes 786440 | tf_op jit(solution)/shard_map/key_value_grads_ring/ppermute | solution.py:56
  90.0 8.6 %collective-permute-start.22 = (bf16[512,256]{1,0:T(8,128)(2,1)S(1)}, bf16[512,256]{1,0:T(8,128)(2,1)S(1)}, u32[]{:S(2)}, u32[]{:S(2)}) collective-permute-start(bf16[512,256]{1,0:T(8,128)(2,1)S(1)} %add_convert_fusion.2), channel_id=1, source_target_pairs={{0,1},{1,2},{2,3},{3,4},{4,5},{5,6},{6,7},{7,0},{8,9},{9,10},{10,1... | collective-permute-start | bytes 786440 | tf_op jit(solution)/shard_map/key_value_grads_ring/ppermute | solution.py:56
  98.6 6.7 %collective-permute-start.26 = (bf16[512,256]{1,0:T(8,128)(2,1)S(1)}, bf16[512,256]{1,0:T(8,128)(2,1)S(1)}, u32[]{:S(2)}, u32[]{:S(2)}) collective-permute-start(bf16[512,256]{1,0:T(8,128)(2,1)S(1)} %add_convert_fusion.1), channel_id=1, source_target_pairs={{0,7},{1,0},{2,1},{3,2},{4,3},{5,4},{6,5},{7,6},{8,15},{9,8},{10,9... | collective-permute-start | bytes 786440 | tf_op jit(solution)/shard_map/key_value_grads_ring/ppermute | solution.py:56
  105.4 6.3 %collective-permute-start.29 = (bf16[128,256]{1,0:T(8,128)(2,1)S(1)}, bf16[128,256]{1,0:T(8,128)(2,1)S(1)}, u32[]{:S(2)}, u32[]{:S(2)}) collective-permute-start(bf16[128,256]{1,0:T(8,128)(2,1)S(1)} %get-tuple-element.131), channel_id=1, source_target_pairs={{0,8},{1,9},{2,10},{3,11},{4,12},{5,13},{6,14},{7,15},{8,16},{9,17... | collective-permute-start | bytes 196616 | tf_op jit(solution)/shard_map/key_value_grads_out/ppermute | solution.py:50
  105.5 6.2 %collective-permute-start.28 = (bf16[128,256]{1,0:T(8,128)(2,1)S(1)}, bf16[128,256]{1,0:T(8,128)(2,1)S(1)}, u32[]{:S(2)}, u32[]{:S(2)}) collective-permute-start(bf16[128,256]{1,0:T(8,128)(2,1)S(1)} %get-tuple-element.132), channel_id=1, source_target_pairs={{0,16},{1,17},{2,18},{3,19},{4,20},{5,21},{6,22},{7,23},{8,24},{9,... | collective-permute-start | bytes 196616 | tf_op jit(solution)/shard_map/key_value_grads_out/ppermute | solution.py:50
  107.1 5.5 %collective-permute-start.27 = (bf16[128,256]{1,0:T(8,128)(2,1)S(1)}, bf16[128,256]{1,0:T(8,128)(2,1)S(1)}, u32[]{:S(2)}, u32[]{:S(2)}) collective-permute-start(bf16[128,256]{1,0:T(8,128)(2,1)S(1)} %get-tuple-element.133), channel_id=1, source_target_pairs={{0,24},{1,25},{2,26},{3,27},{4,28},{5,29},{6,30},{7,31},{8,0},{9,1... | collective-permute-start | bytes 196616 | tf_op jit(solution)/shard_map/key_value_grads_out/ppermute | solution.py:50

commit v5 on v4

--- a/solution.py
+++ b/solution.py
@@ -24,7 +24,7 @@
 PACE = 4
 PACK_STEP = 1
 QUERY_STEP = 2
-BACK_STEP = 3
+BACK_STEP = 2
 WINDOW = 1024
 MAX_TILES = 5
 MAX_VISITS = 48

time: 114 us -> 115 us (level)
  Pallas kernels: 18.4 us -> 14 us
  waiting for transfers between devices: 47 us -> 50.3 us
  starting transfers between devices: 43.6 us -> 46.5 us
    ppermute x15, waiting for transfers between devices: 20.8 us -> 28.4 us  [along_y(): lax.ppermute(x, 'ctx', [(c, (c // NZ + by) % NY * NZ + c % NZ) for c in r...]
    pallas_call x1, Pallas kernels: 13.8 us -> 9.43 us  [attention_grads(): pl.pallas_call(main_body, out_shape=[jax.ShapeDtypeStruct((2 * ROWS, DIM)...]
    ppermute x14, waiting for transfers between devices: 26.2 us -> 21.9 us  [along_z(): lax.ppermute(x, 'ctx', [(c, c // NZ * NZ + (c % NZ + by) % NZ) for c in r...]
    ppermute x14, starting transfers between devices: 20.6 us -> 23.8 us  [along_z(): lax.ppermute(x, 'ctx', [(c, c // NZ * NZ + (c % NZ + by) % NZ) for c in r...]
  transfers between devices with their start and end apart: 30 -> 30, of which waited for: 17 -> 18; matrix products, arithmetic and copies ran while one was open for 0% -> 0% of each run, Pallas kernels for 3% -> 3%
where the time goes in v5:
time: 115 us
  waiting for transfers between devices  50.3 us (44%)
  starting transfers between devices  46.5 us (40%)
  Pallas kernels  14 us (12%)
  local copies, waits for them, and re-layouts  3.09 us (3%)
    ppermute x15, waiting for transfers between devices, along_y(): lax.ppermute(x, 'ctx', [(c, (c // NZ + by) % NY * NZ + c % NZ) for c in r...  28.4 us
    ppermute x14, starting transfers between devices, along_z(): lax.ppermute(x, 'ctx', [(c, c // NZ * NZ + (c % NZ + by) % NZ) for c in r...  23.8 us
    ppermute x15, starting transfers between devices, along_y(): lax.ppermute(x, 'ctx', [(c, (c // NZ + by) % NY * NZ + c % NZ) for c in r...  22.7 us
    ppermute x14, waiting for transfers between devices, along_z(): lax.ppermute(x, 'ctx', [(c, c // NZ * NZ + (c % NZ + by) % NZ) for c in r...  21.9 us
    pallas_call x1, Pallas kernels, attention_grads(): pl.pallas_call(main_body, out_shape=[jax.ShapeDtypeStruct((2 * ROWS, DIM)...  9.43 us
    unnamed x15, local copies, waits for them, and re-layouts  3.06 us
  transfers between devices with their start and end apart: 30, of which 18 were waited for; matrix products, arithmetic and copies ran while one was open for 0% of the time, Pallas kernels for 3%

profile of v5, /device:TPU:2, one launch (start us, length us, event | category | flops | bytes accessed | tf_op | source)
XLA Modules:
  0.0 115.0 jit_solution(5602864780267401670)
XLA Ops:
  0.7 0.9 copy-done.2
  1.6 0.9 copy-done.3
  2.5 1.7 %collective-permute-start = (bf16[128,256]{1,0:T(8,128)(2,1)S(1)}, bf16[128,256]{1,0:T(8,128)(2,1)S(1)}, u32[]{:S(2)}, u32[]{:S(2)}) collective-permute-start(bf16[128,256]{1,0:T(8,128)(2,1)S(1)} %get-tuple-element.68), channel_id=1, source_target_pairs={{0,8},{1,9},{2,10},{3,11},{4,12},{5,13},{6,14},{7,15},{8,16},{9,17... | collective-permute-start | bytes 196616 | tf_op jit(solution)/shard_map/keys_values_in/ppermute | solution.py:50
  4.2 2.9 %collective-permute-start.1 = (bf16[128,256]{1,0:T(8,128)(2,1)S(1)}, bf16[128,256]{1,0:T(8,128)(2,1)S(1)}, u32[]{:S(2)}, u32[]{:S(2)}) collective-permute-start(bf16[128,256]{1,0:T(8,128)(2,1)S(1)} %get-tuple-element.69), channel_id=1, source_target_pairs={{0,16},{1,17},{2,18},{3,19},{4,20},{5,21},{6,22},{7,23},{8,24},{9,... | collective-permute-start | bytes 196616 | tf_op jit(solution)/shard_map/keys_values_in/ppermute | solution.py:50
  7.1 1.3 %collective-permute-start.2 = (bf16[128,256]{1,0:T(8,128)(2,1)S(1)}, bf16[128,256]{1,0:T(8,128)(2,1)S(1)}, u32[]{:S(2)}, u32[]{:S(2)}) collective-permute-start(bf16[128,256]{1,0:T(8,128)(2,1)S(1)} %get-tuple-element.70), channel_id=1, source_target_pairs={{0,24},{1,25},{2,26},{3,27},{4,28},{5,29},{6,30},{7,31},{8,0},{9,1... | collective-permute-start | bytes 196616 | tf_op jit(solution)/shard_map/keys_values_in/ppermute | solution.py:50
  8.4 1.2 %copy-done = bf16[1,128,4096]{2,1,0:T(8,128)(2,1)S(1)} copy-done((bf16[1,128,4096]{2,1,0:T(8,128)(2,1)S(1)}, bf16[1,128,4096]{2,1,0:T(8,128)(2,1)}, u32[]{:S(2)}) %copy-start) | copy-done | bytes 1048600
  9.8 1.1 collective-permute-done.1
  10.9 0.4 collective-permute-done.2
  11.4 5.9 %collective-permute-start.4 = (bf16[512,256]{1,0:T(8,128)(2,1)S(1)}, bf16[512,256]{1,0:T(8,128)(2,1)S(1)}, u32[]{:S(2)}, u32[]{:S(2)}) collective-permute-start(bf16[512,256]{1,0:T(8,128)(2,1)S(1)} %constant_dynamic-update-slice_fusion.refs_12_), channel_id=1, source_target_pairs={{0,7},{1,0},{2,1},{3,2},{4,3},{5,4},{6,5},{7,6},{8,15},{9,8},{10,9... | collective-permute-start | bytes 786440 | tf_op jit(solution)/shard_map/keys_values_ring/ppermute | solution.py:56
  17.4 1.6 %make_plan.1 = (s32[272]{0:T(512)S(1)}, s32[8,512]{1,0:T(8,128)S(1)}) custom-call(s32[1,32]{1,0:T(1,128)S(1)} %copy-done.4, s32[1,16]{1,0:T(1,128)S(1)} %copy-done.5), custom_call_target="tpu_custom_call" | custom-call | tf_op jit(solution)/shard_map/plan/make_plan/pallas_call | solution.py:257
  19.0 0.9 collective-permute-start.8
  19.9 3.2 %collective-permute-start.9 = (bf16[1024,128]{1,0:T(8,128)(2,1)S(1)}, bf16[1024,128]{1,0:T(8,128)(2,1)S(1)}, u32[]{:S(2)}, u32[]{:S(2)}) collective-permute-start(bf16[1024,128]{1,0:T(8,128)(2,1)S(1)} %get-tuple-element.91), channel_id=1, source_target_pairs={{0,16},{1,17},{2,18},{3,19},{4,20},{5,21},{6,22},{7,23},{8,24},{9,... | collective-permute-start | bytes 786440 | tf_op jit(solution)/shard_map/queries_in/ppermute | solution.py:50
  23.1 0.7 collective-permute-start.10
  23.8 0.7 pack_grads.1
  24.6 1.2 %collective-permute-done.3.refs_11_ = bf16[512,256]{1,0:T(8,128)(2,1)S(1)} collective-permute-done((bf16[512,256]{1,0:T(8,128)(2,1)S(1)}, bf16[512,256]{1,0:T(8,128)(2,1)S(1)}, u32[]{:S(2)}, u32[]{:S(2)}) %collective-permute-start.3) | collective-permute-done | bytes 262176 | tf_op jit(solution)/shard_map/keys_values_ring/ppermute | solution.py:56
  25.8 3.2 %collective-permute-start.7 = (bf16[512,256]{1,0:T(8,128)(2,1)S(1)}, bf16[512,256]{1,0:T(8,128)(2,1)S(1)}, u32[]{:S(2)}, u32[]{:S(2)}) collective-permute-start(bf16[512,256]{1,0:T(8,128)(2,1)S(1)} %collective-permute-done.4.refs_13_), channel_id=1, source_target_pairs={{0,7},{1,0},{2,1},{3,2},{4,3},{5,4},{6,5},{7,6},{8,15},{9,8},{10,9... | collective-permute-start | bytes 786440 | tf_op jit(solution)/shard_map/keys_values_ring/ppermute | solution.py:56
  29.1 0.7 collective-permute-done.8.refs_1_
  29.8 3.7 %collective-permute-done.9.refs_2_ = bf16[1024,128]{1,0:T(8,128)(2,1)S(1)} collective-permute-done((bf16[1024,128]{1,0:T(8,128)(2,1)S(1)}, bf16[1024,128]{1,0:T(8,128)(2,1)S(1)}, u32[]{:S(2)}, u32[]{:S(2)}) %collective-permute-start.9) | collective-permute-done | bytes 262176 | tf_op jit(solution)/shard_map/queries_in/ppermute | solution.py:50
  33.5 0.4 collective-permute-done.10.refs_3_
  33.9 3.2 %collective-permute-start.15 = (bf16[512,256]{1,0:T(8,128)(2,1)S(1)}, bf16[512,256]{1,0:T(8,128)(2,1)S(1)}, u32[]{:S(2)}, u32[]{:S(2)}) collective-permute-start(bf16[512,256]{1,0:T(8,128)(2,1)S(1)} %collective-permute-done.7.refs_14_), channel_id=1, source_target_pairs={{0,7},{1,0},{2,1},{3,2},{4,3},{5,4},{6,5},{7,6},{8,15},{9,8},{10,9... | collective-permute-start | bytes 786440 | tf_op jit(solution)/shard_map/keys_values_ring/ppermute | solution.py:56
  37.1 1.6 %collective-permute-start.11 = (bf16[1152,128]{1,0:T(8,128)(2,1)S(1)}, bf16[1152,128]{1,0:T(8,128)(2,1)S(1)}, u32[]{:S(2)}, u32[]{:S(2)}) collective-permute-start(bf16[1152,128]{1,0:T(8,128)(2,1)S(1)} %get-tuple-element.98), channel_id=1, source_target_pairs={{0,8},{1,9},{2,10},{3,11},{4,12},{5,13},{6,14},{7,15},{8,16},{9,17... | collective-permute-start | bytes 884744 | tf_op jit(solution)/shard_map/grads_in/ppermute | solution.py:50
  38.6 2.5 %collective-permute-start.12 = (bf16[1152,128]{1,0:T(8,128)(2,1)S(1)}, bf16[1152,128]{1,0:T(8,128)(2,1)S(1)}, u32[]{:S(2)}, u32[]{:S(2)}) collective-permute-start(bf16[1152,128]{1,0:T(8,128)(2,1)S(1)} %get-tuple-element.99), channel_id=1, source_target_pairs={{0,16},{1,17},{2,18},{3,19},{4,20},{5,21},{6,22},{7,23},{8,24},{9,... | collective-permute-start | bytes 884744 | tf_op jit(solution)/shard_map/grads_in/ppermute | solution.py:50
  41.2 0.7 collective-permute-start.13
  41.9 0.3 collective-permute-done.14.refs_9_
  42.2 4.5 %collective-permute-done.11.refs_5_ = bf16[1152,128]{1,0:T(8,128)(2,1)S(1)} collective-permute-done((bf16[1152,128]{1,0:T(8,128)(2,1)S(1)}, bf16[1152,128]{1,0:T(8,128)(2,1)S(1)}, u32[]{:S(2)}, u32[]{:S(2)}) %collective-permute-start.11) | collective-permute-done | bytes 294944 | tf_op jit(solution)/shard_map/grads_in/ppermute | solution.py:50
  46.7 7.1 %collective-permute-done.12.refs_6_ = bf16[1152,128]{1,0:T(8,128)(2,1)S(1)} collective-permute-done((bf16[1152,128]{1,0:T(8,128)(2,1)S(1)}, bf16[1152,128]{1,0:T(8,128)(2,1)S(1)}, u32[]{:S(2)}, u32[]{:S(2)}) %collective-permute-start.12) | collective-permute-done | bytes 294944 | tf_op jit(solution)/shard_map/grads_in/ppermute | solution.py:50
  53.9 9.4 %attention_grads.1 = (bf16[1024,128]{1,0:T(8,128)(2,1)S(1)}, bf16[1024,128]{1,0:T(8,128)(2,1)S(1)}, bf16[1024,128]{1,0:T(8,128)(2,1)S(1)}, bf16[1024,128]{1,0:T(...) custom-call(s32[272]{0:T(512)S(1)} %get-tuple-element.85.plan, ...), custom_call_target="tpu_custom_call" | custom-call | tf_op jit(solution)/shard_map/attention_grads/pallas_call | solution.py:400
  63.3 5.8 %collective-permute-start.17 = (bf16[512,256]{1,0:T(8,128)(2,1)S(1)}, bf16[512,256]{1,0:T(8,128)(2,1)S(1)}, u32[]{:S(2)}, u32[]{:S(2)}) collective-permute-start(bf16[512,256]{1,0:T(8,128)(2,1)S(1)} %get-tuple-element.105), channel_id=1, source_target_pairs={{0,7},{1,0},{2,1},{3,2},{4,3},{5,4},{6,5},{7,6},{8,15},{9,8},{10,9... | collective-permute-start | bytes 786440 | tf_op jit(solution)/shard_map/key_value_grads_ring/ppermute | solution.py:56
  69.1 2.1 %collective-permute-start.21 = (bf16[1024,128]{1,0:T(8,128)(2,1)S(1)}, bf16[1024,128]{1,0:T(8,128)(2,1)S(1)}, u32[]{:S(2)}, u32[]{:S(2)}) collective-permute-start(bf16[1024,128]{1,0:T(8,128)(2,1)S(1)} %get-tuple-element.112), channel_id=1, source_target_pairs={{0,24},{1,25},{2,26},{3,27},{4,28},{5,29},{6,30},{7,31},{8,0},{9,1... | collective-permute-start | bytes 786440 | tf_op jit(solution)/shard_map/query_grads_out/ppermute | solution.py:50
  71.2 1.1 collective-permute-start.22
  72.3 0.2 collective-permute-start.23
  72.5 2.0 %collective-permute-done.17 = bf16[512,256]{1,0:T(8,128)(2,1)S(1)} collective-permute-done((bf16[512,256]{1,0:T(8,128)(2,1)S(1)}, bf16[512,256]{1,0:T(8,128)(2,1)S(1)}, u32[]{:S(2)}, u32[]{:S(2)}) %collective-permute-start.17) | collective-permute-done | bytes 262176 | tf_op jit(solution)/shard_map/key_value_grads_ring/ppermute | solution.py:56
  74.5 3.5 %collective-permute-done.18 = bf16[512,256]{1,0:T(8,128)(2,1)S(1)} collective-permute-done((bf16[512,256]{1,0:T(8,128)(2,1)S(1)}, bf16[512,256]{1,0:T(8,128)(2,1)S(1)}, u32[]{:S(2)}, u32[]{:S(2)}) %collective-permute-start.18) | collective-permute-done | bytes 262176 | tf_op jit(solution)/shard_map/key_value_grads_ring/ppermute | solution.py:56
  78.1 0.3 collective-permute-start.19
  78.4 1.9 %collective-permute-start.20 = (bf16[512,256]{1,0:T(8,128)(2,1)S(1)}, bf16[512,256]{1,0:T(8,128)(2,1)S(1)}, u32[]{:S(2)}, u32[]{:S(2)}) collective-permute-start(bf16[512,256]{1,0:T(8,128)(2,1)S(1)} %add_convert_fusion.4), channel_id=1, source_target_pairs={{0,1},{1,2},{2,3},{3,4},{4,5},{5,6},{6,7},{7,0},{8,9},{9,10},{10,1... | collective-permute-start | bytes 786440 | tf_op jit(solution)/shard_map/key_value_grads_ring/ppermute | solution.py:56
  80.3 0.5 collective-permute-done.22.refs_2_
  80.9 6.6 %collective-permute-done.23.refs_3_ = bf16[1024,128]{1,0:T(8,128)(2,1)S(1)} collective-permute-done((bf16[1024,128]{1,0:T(8,128)(2,1)S(1)}, bf16[1024,128]{1,0:T(8,128)(2,1)S(1)}, u32[]{:S(2)}, u32[]{:S(2)}) %collective-permute-start.23) | collective-permute-done | bytes 262176 | tf_op jit(solution)/shard_map/query_grads_out/ppermute | solution.py:50
  87.5 2.8 %collective-permute-start.24 = (bf16[512,256]{1,0:T(8,128)(2,1)S(1)}, bf16[512,256]{1,0:T(8,128)(2,1)S(1)}, u32[]{:S(2)}, u32[]{:S(2)}) collective-permute-start(bf16[512,256]{1,0:T(8,128)(2,1)S(1)} %add_convert_fusion.3), channel_id=1, source_target_pairs={{0,7},{1,0},{2,1},{3,2},{4,3},{5,4},{6,5},{7,6},{8,15},{9,8},{10,9... | collective-permute-start | bytes 786440 | tf_op jit(solution)/shard_map/key_value_grads_ring/ppermute | solution.py:56
  90.5 5.6 %collective-permute-done.24 = bf16[512,256]{1,0:T(8,128)(2,1)S(1)} collective-permute-done((bf16[512,256]{1,0:T(8,128)(2,1)S(1)}, bf16[512,256]{1,0:T(8,128)(2,1)S(1)}, u32[]{:S(2)}, u32[]{:S(2)}) %collective-permute-start.24) | collective-permute-done | bytes 262176 | tf_op jit(solution)/shard_map/key_value_grads_ring/ppermute | solution.py:56
  96.1 3.5 %collective-permute-done.25 = bf16[512,256]{1,0:T(8,128)(2,1)S(1)} collective-permute-done((bf16[512,256]{1,0:T(8,128)(2,1)S(1)}, bf16[512,256]{1,0:T(8,128)(2,1)S(1)}, u32[]{:S(2)}, u32[]{:S(2)}) %collective-permute-start.25) | collective-permute-done | bytes 262176 | tf_op jit(solution)/shard_map/key_value_grads_ring/ppermute | solution.py:56
  99.7 0.4 collective-permute-start.26
  100.1 1.3 %place_wide.1 = bf16[128,4096]{1,0:T(8,128)(2,1)} custom-call(bf16[1024,128]{1,0:T(8,128)(2,1)S(1)} %get-tuple-element.121.refs_0_, bf16[1024,128]{1,0:T(8,128)(2,1)S(1)} %collective-permute-done.21.refs_1_, bf16[1024,128]{1,0:T(8,128)(2,1)S(1)} %collective-permute-done.22.refs_2_, bf16[1024,128]{1,0:T(8,128)(2,1)S(1)} %collective-permute-done.23.refs_3_), custom_call_target="tpu_custom_call" | custom-call | tf_op jit(solution)/shard_map/key_value_grads_ring/place_wide/pallas_call | solution.py:444
  101.4 5.7 %collective-permute-done.26 = bf16[512,256]{1,0:T(8,128)(2,1)S(1)} collective-permute-done((bf16[512,256]{1,0:T(8,128)(2,1)S(1)}, bf16[512,256]{1,0:T(8,128)(2,1)S(1)}, u32[]{:S(2)}, u32[]{:S(2)}) %collective-permute-start.26) | collective-permute-done | bytes 262176 | tf_op jit(solution)/shard_map/key_value_grads_ring/ppermute | solution.py:56
  107.3 1.9 %collective-permute-start.28 = (bf16[128,256]{1,0:T(8,128)(2,1)S(1)}, bf16[128,256]{1,0:T(8,128)(2,1)S(1)}, u32[]{:S(2)}, u32[]{:S(2)}) collective-permute-start(bf16[128,256]{1,0:T(8,128)(2,1)S(1)} %get-tuple-element.132), channel_id=1, source_target_pairs={{0,16},{1,17},{2,18},{3,19},{4,20},{5,21},{6,22},{7,23},{8,24},{9,... | collective-permute-start | bytes 196616 | tf_op jit(solution)/shard_map/key_value_grads_out/ppermute | solution.py:50
  109.1 1.7 %collective-permute-start.27 = (bf16[128,256]{1,0:T(8,128)(2,1)S(1)}, bf16[128,256]{1,0:T(8,128)(2,1)S(1)}, u32[]{:S(2)}, u32[]{:S(2)}) collective-permute-start(bf16[128,256]{1,0:T(8,128)(2,1)S(1)} %get-tuple-element.133), channel_id=1, source_target_pairs={{0,24},{1,25},{2,26},{3,27},{4,28},{5,29},{6,30},{7,31},{8,0},{9,1... | collective-permute-start | bytes 196616 | tf_op jit(solution)/shard_map/key_value_grads_out/ppermute | solution.py:50
  110.9 2.5 %collective-permute-done.29.refs_3_ = bf16[128,256]{1,0:T(8,128)(2,1)S(1)} collective-permute-done((bf16[128,256]{1,0:T(8,128)(2,1)S(1)}, bf16[128,256]{1,0:T(8,128)(2,1)S(1)}, u32[]{:S(2)}, u32[]{:S(2)}) %collective-permute-start.29) | collective-permute-done | bytes 65568 | tf_op jit(solution)/shard_map/key_value_grads_out/ppermute | solution.py:50
  113.4 0.9 collective-permute-done.27.refs_1_
  114.3 0.8 place_kv.1
  (42 shorter events, 0.8 us)
Async XLA Ops:
  0.6 22.4 %collective-permute-start.5 = (bf16[128,4096]{1,0:T(8,128)(2,1)}, bf16[128,4096]{1,0:T(8,128)(2,1)S(1)}, u32[]{:S(2)}, u32[]{:S(2)}) collective-permute-start(bf16[128,4096]{1,0:T(8,128)(2,1)} %bitcast.13), channel_id=1, source_target_pairs={{0,224},{32,0},{64,32},{96,64},{128,96},{160,128},{192,160},{224,1... | collective-permute-start | bytes 3145736 | tf_op jit(solution)/shard_map/grads_shift/ppermute | solution.py:479
  0.7 0.9 copy-start.2
  1.6 0.9 copy-start.3
  2.5 7.3 %collective-permute-start = (bf16[128,256]{1,0:T(8,128)(2,1)S(1)}, bf16[128,256]{1,0:T(8,128)(2,1)S(1)}, u32[]{:S(2)}, u32[]{:S(2)}) collective-permute-start(bf16[128,256]{1,0:T(8,128)(2,1)S(1)} %get-tuple-element.68), channel_id=1, source_target_pairs={{0,8},{1,9},{2,10},{3,11},{4,12},{5,13},{6,14},{7,15},{8,16},{9,17... | collective-permute-start | bytes 196616 | tf_op jit(solution)/shard_map/keys_values_in/ppermute | solution.py:50
  4.2 6.8 %collective-permute-start.1 = (bf16[128,256]{1,0:T(8,128)(2,1)S(1)}, bf16[128,256]{1,0:T(8,128)(2,1)S(1)}, u32[]{:S(2)}, u32[]{:S(2)}) collective-permute-start(bf16[128,256]{1,0:T(8,128)(2,1)S(1)} %get-tuple-element.69), channel_id=1, source_target_pairs={{0,16},{1,17},{2,18},{3,19},{4,20},{5,21},{6,22},{7,23},{8,24},{9,... | collective-permute-start | bytes 196616 | tf_op jit(solution)/shard_map/keys_values_in/ppermute | solution.py:50
  7.1 4.3 %collective-permute-start.2 = (bf16[128,256]{1,0:T(8,128)(2,1)S(1)}, bf16[128,256]{1,0:T(8,128)(2,1)S(1)}, u32[]{:S(2)}, u32[]{:S(2)}) collective-permute-start(bf16[128,256]{1,0:T(8,128)(2,1)S(1)} %get-tuple-element.70), channel_id=1, source_target_pairs={{0,24},{1,25},{2,26},{3,27},{4,28},{5,29},{6,30},{7,31},{8,0},{9,1... | collective-permute-start | bytes 196616 | tf_op jit(solution)/shard_map/keys_values_in/ppermute | solution.py:50
  8.4 1.2 %copy-start = (bf16[1,128,4096]{2,1,0:T(8,128)(2,1)S(1)}, bf16[1,128,4096]{2,1,0:T(8,128)(2,1)}, u32[]{:S(2)}) copy-start(bf16[1,128,4096]{2,1,0:T(8,128)(2,1)} %param.7) | copy-start | bytes 3145732
  9.6 14.2 %copy-start.1 = (bf16[1,128,4096]{2,1,0:T(8,128)(2,1)S(1)}, bf16[1,128,4096]{2,1,0:T(8,128)(2,1)}, u32[]{:S(2)}) copy-start(bf16[1,128,4096]{2,1,0:T(8,128)(2,1)} %param.10) | copy-start | bytes 3145732
  11.4 6.0 %copy-start.4 = (s32[1,32]{1,0:T(1,128)S(1)}, s32[1,32]{1,0:T(1,128)}, u32[]{:S(2)}) copy-start(s32[1,32]{1,0:T(1,128)} %pairs.1) | copy-start | bytes 388
  11.4 6.0 %copy-start.5 = (s32[1,16]{1,0:T(1,128)S(1)}, s32[1,16]{1,0:T(1,128)}, u32[]{:S(2)}) copy-start(s32[1,16]{1,0:T(1,128)} %lengths.1) | copy-start | bytes 196
  11.4 13.2 %collective-permute-start.4 = (bf16[512,256]{1,0:T(8,128)(2,1)S(1)}, bf16[512,256]{1,0:T(8,128)(2,1)S(1)}, u32[]{:S(2)}, u32[]{:S(2)}) collective-permute-start(bf16[512,256]{1,0:T(8,128)(2,1)S(1)} %constant_dynamic-update-slice_fusion.refs_12_), channel_id=1, source_target_pairs={{0,7},{1,0},{2,1},{3,2},{4,3},{5,4},{6,5},{7,6},{8,15},{9,8},{10,9... | collective-permute-start | bytes 786440 | tf_op jit(solution)/shard_map/keys_values_ring/ppermute | solution.py:56
  17.3 8.5 %collective-permute-start.3 = (bf16[512,256]{1,0:T(8,128)(2,1)S(1)}, bf16[512,256]{1,0:T(8,128)(2,1)S(1)}, u32[]{:S(2)}, u32[]{:S(2)}) collective-permute-start(bf16[512,256]{1,0:T(8,128)(2,1)S(1)} %constant_dynamic-update-slice_fusion.refs_12_), channel_id=1, source_target_pairs={{0,1},{1,2},{2,3},{3,4},{4,5},{5,6},{6,7},{7,0},{8,9},{9,10},{10,1... | collective-permute-start | bytes 786440 | tf_op jit(solution)/shard_map/keys_values_ring/ppermute | solution.py:56
  19.0 10.8 %collective-permute-start.8 = (bf16[1024,128]{1,0:T(8,128)(2,1)S(1)}, bf16[1024,128]{1,0:T(8,128)(2,1)S(1)}, u32[]{:S(2)}, u32[]{:S(2)}) collective-permute-start(bf16[1024,128]{1,0:T(8,128)(2,1)S(1)} %get-tuple-element.90), channel_id=1, source_target_pairs={{0,8},{1,9},{2,10},{3,11},{4,12},{5,13},{6,14},{7,15},{8,16},{9,17... | collective-permute-start | bytes 786440 | tf_op jit(solution)/shard_map/queries_in/ppermute | solution.py:50
  19.9 13.6 %collective-permute-start.9 = (bf16[1024,128]{1,0:T(8,128)(2,1)S(1)}, bf16[1024,128]{1,0:T(8,128)(2,1)S(1)}, u32[]{:S(2)}, u32[]{:S(2)}) collective-permute-start(bf16[1024,128]{1,0:T(8,128)(2,1)S(1)} %get-tuple-element.91), channel_id=1, source_target_pairs={{0,16},{1,17},{2,18},{3,19},{4,20},{5,21},{6,22},{7,23},{8,24},{9,... | collective-permute-start | bytes 786440 | tf_op jit(solution)/shard_map/queries_in/ppermute | solution.py:50
  23.1 10.8 %collective-permute-start.10 = (bf16[1024,128]{1,0:T(8,128)(2,1)S(1)}, bf16[1024,128]{1,0:T(8,128)(2,1)S(1)}, u32[]{:S(2)}, u32[]{:S(2)}) collective-permute-start(bf16[1024,128]{1,0:T(8,128)(2,1)S(1)} %get-tuple-element.92), channel_id=1, source_target_pairs={{0,24},{1,25},{2,26},{3,27},{4,28},{5,29},{6,30},{7,31},{8,0},{9,1... | collective-permute-start | bytes 786440 | tf_op jit(solution)/shard_map/queries_in/ppermute | solution.py:50
  25.8 8.0 %collective-permute-start.6 = (bf16[512,256]{1,0:T(8,128)(2,1)S(1)}, bf16[512,256]{1,0:T(8,128)(2,1)S(1)}, u32[]{:S(2)}, u32[]{:S(2)}) collective-permute-start(bf16[512,256]{1,0:T(8,128)(2,1)S(1)} %collective-permute-done.3.refs_11_), channel_id=1, source_target_pairs={{0,1},{1,2},{2,3},{3,4},{4,5},{5,6},{6,7},{7,0},{8,9},{9,10},{10,1... | collective-permute-start | bytes 786440 | tf_op jit(solution)/shard_map/keys_values_ring/ppermute | solution.py:56
  25.8 8.0 %collective-permute-start.7 = (bf16[512,256]{1,0:T(8,128)(2,1)S(1)}, bf16[512,256]{1,0:T(8,128)(2,1)S(1)}, u32[]{:S(2)}, u32[]{:S(2)}) collective-permute-start(bf16[512,256]{1,0:T(8,128)(2,1)S(1)} %collective-permute-done.4.refs_13_), channel_id=1, source_target_pairs={{0,7},{1,0},{2,1},{3,2},{4,3},{5,4},{6,5},{7,6},{8,15},{9,8},{10,9... | collective-permute-start | bytes 786440 | tf_op jit(solution)/shard_map/keys_values_ring/ppermute | solution.py:56
  33.9 8.4 %collective-permute-start.14 = (bf16[512,256]{1,0:T(8,128)(2,1)S(1)}, bf16[512,256]{1,0:T(8,128)(2,1)S(1)}, u32[]{:S(2)}, u32[]{:S(2)}) collective-permute-start(bf16[512,256]{1,0:T(8,128)(2,1)S(1)} %collective-permute-done.6.refs_10_), channel_id=1, source_target_pairs={{0,1},{1,2},{2,3},{3,4},{4,5},{5,6},{6,7},{7,0},{8,9},{9,10},{10,1... | collective-permute-start | bytes 786440 | tf_op jit(solution)/shard_map/keys_values_ring/ppermute | solution.py:56
  33.9 8.4 %collective-permute-start.15 = (bf16[512,256]{1,0:T(8,128)(2,1)S(1)}, bf16[512,256]{1,0:T(8,128)(2,1)S(1)}, u32[]{:S(2)}, u32[]{:S(2)}) collective-permute-start(bf16[512,256]{1,0:T(8,128)(2,1)S(1)} %collective-permute-done.7.refs_14_), channel_id=1, source_target_pairs={{0,7},{1,0},{2,1},{3,2},{4,3},{5,4},{6,5},{7,6},{8,15},{9,8},{10,9... | collective-permute-start | bytes 786440 | tf_op jit(solution)/shard_map/keys_values_ring/ppermute | solution.py:56
  37.1 9.6 %collective-permute-start.11 = (bf16[1152,128]{1,0:T(8,128)(2,1)S(1)}, bf16[1152,128]{1,0:T(8,128)(2,1)S(1)}, u32[]{:S(2)}, u32[]{:S(2)}) collective-permute-start(bf16[1152,128]{1,0:T(8,128)(2,1)S(1)} %get-tuple-element.98), channel_id=1, source_target_pairs={{0,8},{1,9},{2,10},{3,11},{4,12},{5,13},{6,14},{7,15},{8,16},{9,17... | collective-permute-start | bytes 884744 | tf_op jit(solution)/shard_map/grads_in/ppermute | solution.py:50
  38.6 15.2 %collective-permute-start.12 = (bf16[1152,128]{1,0:T(8,128)(2,1)S(1)}, bf16[1152,128]{1,0:T(8,128)(2,1)S(1)}, u32[]{:S(2)}, u32[]{:S(2)}) collective-permute-start(bf16[1152,128]{1,0:T(8,128)(2,1)S(1)} %get-tuple-element.99), channel_id=1, source_target_pairs={{0,16},{1,17},{2,18},{3,19},{4,20},{5,21},{6,22},{7,23},{8,24},{9,... | collective-permute-start | bytes 884744 | tf_op jit(solution)/shard_map/grads_in/ppermute | solution.py:50
  41.2 12.7 %collective-permute-start.13 = (bf16[1152,128]{1,0:T(8,128)(2,1)S(1)}, bf16[1152,128]{1,0:T(8,128)(2,1)S(1)}, u32[]{:S(2)}, u32[]{:S(2)}) collective-permute-start(bf16[1152,128]{1,0:T(8,128)(2,1)S(1)} %get-tuple-element.100), channel_id=1, source_target_pairs={{0,24},{1,25},{2,26},{3,27},{4,28},{5,29},{6,30},{7,31},{8,0},{9,1... | collective-permute-start | bytes 884744 | tf_op jit(solution)/shard_map/grads_in/ppermute | solution.py:50
  42.2 11.6 %collective-permute-start.16 = (bf16[512,256]{1,0:T(8,128)(2,1)S(1)}, bf16[512,256]{1,0:T(8,128)(2,1)S(1)}, u32[]{:S(2)}, u32[]{:S(2)}) collective-permute-start(bf16[512,256]{1,0:T(8,128)(2,1)S(1)} %collective-permute-done.14.refs_9_), channel_id=1, source_target_pairs={{0,1},{1,2},{2,3},{3,4},{4,5},{5,6},{6,7},{7,0},{8,9},{9,10},{10,1... | collective-permute-start | bytes 786440 | tf_op jit(solution)/shard_map/keys_values_ring/ppermute | solution.py:56
  63.3 11.2 %collective-permute-start.17 = (bf16[512,256]{1,0:T(8,128)(2,1)S(1)}, bf16[512,256]{1,0:T(8,128)(2,1)S(1)}, u32[]{:S(2)}, u32[]{:S(2)}) collective-permute-start(bf16[512,256]{1,0:T(8,128)(2,1)S(1)} %get-tuple-element.105), channel_id=1, source_target_pairs={{0,7},{1,0},{2,1},{3,2},{4,3},{5,4},{6,5},{7,6},{8,15},{9,8},{10,9... | collective-permute-start | bytes 786440 | tf_op jit(solution)/shard_map/key_value_grads_ring/ppermute | solution.py:56
  69.1 8.9 %collective-permute-start.18 = (bf16[512,256]{1,0:T(8,128)(2,1)S(1)}, bf16[512,256]{1,0:T(8,128)(2,1)S(1)}, u32[]{:S(2)}, u32[]{:S(2)}) collective-permute-start(bf16[512,256]{1,0:T(8,128)(2,1)S(1)} %get-tuple-element.106), channel_id=1, source_target_pairs={{0,1},{1,2},{2,3},{3,4},{4,5},{5,6},{6,7},{7,0},{8,9},{9,10},{10,1... | collective-permute-start | bytes 786440 | tf_op jit(solution)/shard_map/key_value_grads_ring/ppermute | solution.py:56
  69.1 11.2 %collective-permute-start.21 = (bf16[1024,128]{1,0:T(8,128)(2,1)S(1)}, bf16[1024,128]{1,0:T(8,128)(2,1)S(1)}, u32[]{:S(2)}, u32[]{:S(2)}) collective-permute-start(bf16[1024,128]{1,0:T(8,128)(2,1)S(1)} %get-tuple-element.112), channel_id=1, source_target_pairs={{0,24},{1,25},{2,26},{3,27},{4,28},{5,29},{6,30},{7,31},{8,0},{9,1... | collective-permute-start | bytes 786440 | tf_op jit(solution)/shard_map/query_grads_out/ppermute | solution.py:50
  71.2 9.7 %collective-permute-start.22 = (bf16[1024,128]{1,0:T(8,128)(2,1)S(1)}, bf16[1024,128]{1,0:T(8,128)(2,1)S(1)}, u32[]{:S(2)}, u32[]{:S(2)}) collective-permute-start(bf16[1024,128]{1,0:T(8,128)(2,1)S(1)} %get-tuple-element.113), channel_id=1, source_target_pairs={{0,16},{1,17},{2,18},{3,19},{4,20},{5,21},{6,22},{7,23},{8,24},{9,... | collective-permute-start | bytes 786440 | tf_op jit(solution)/shard_map/query_grads_out/ppermute | solution.py:50
  72.3 15.1 %collective-permute-start.23 = (bf16[1024,128]{1,0:T(8,128)(2,1)S(1)}, bf16[1024,128]{1,0:T(8,128)(2,1)S(1)}, u32[]{:S(2)}, u32[]{:S(2)}) collective-permute-start(bf16[1024,128]{1,0:T(8,128)(2,1)S(1)} %get-tuple-element.114), channel_id=1, source_target_pairs={{0,8},{1,9},{2,10},{3,11},{4,12},{5,13},{6,14},{7,15},{8,16},{9,17... | collective-permute-start | bytes 786440 | tf_op jit(solution)/shard_map/query_grads_out/ppermute | solution.py:50
  78.1 9.3 %collective-permute-start.19 = (bf16[512,256]{1,0:T(8,128)(2,1)S(1)}, bf16[512,256]{1,0:T(8,128)(2,1)S(1)}, u32[]{:S(2)}, u32[]{:S(2)}) collective-permute-start(bf16[512,256]{1,0:T(8,128)(2,1)S(1)} %add_convert_fusion.5), channel_id=1, source_target_pairs={{0,7},{1,0},{2,1},{3,2},{4,3},{5,4},{6,5},{7,6},{8,15},{9,8},{10,9... | collective-permute-start | bytes 786440 | tf_op jit(solution)/shard_map/key_value_grads_ring/ppermute | solution.py:56
  78.4 9.0 %collective-permute-start.20 = (bf16[512,256]{1,0:T(8,128)(2,1)S(1)}, bf16[512,256]{1,0:T(8,128)(2,1)S(1)}, u32[]{:S(2)}, u32[]{:S(2)}) collective-permute-start(bf16[512,256]{1,0:T(8,128)(2,1)S(1)} %add_convert_fusion.4), channel_id=1, source_target_pairs={{0,1},{1,2},{2,3},{3,4},{4,5},{5,6},{6,7},{7,0},{8,9},{9,10},{10,1... | collective-permute-start | bytes 786440 | tf_op jit(solution)/shard_map/key_value_grads_ring/ppermute | solution.py:56
  87.5 8.6 %collective-permute-start.24 = (bf16[512,256]{1,0:T(8,128)(2,1)S(1)}, bf16[512,256]{1,0:T(8,128)(2,1)S(1)}, u32[]{:S(2)}, u32[]{:S(2)}) collective-permute-start(bf16[512,256]{1,0:T(8,128)(2,1)S(1)} %add_convert_fusion.3), channel_id=1, source_target_pairs={{0,7},{1,0},{2,1},{3,2},{4,3},{5,4},{6,5},{7,6},{8,15},{9,8},{10,9... | collective-permute-start | bytes 786440 | tf_op jit(solution)/shard_map/key_value_grads_ring/ppermute | solution.py:56
  90.4 9.2 %collective-permute-start.25 = (bf16[512,256]{1,0:T(8,128)(2,1)S(1)}, bf16[512,256]{1,0:T(8,128)(2,1)S(1)}, u32[]{:S(2)}, u32[]{:S(2)}) collective-permute-start(bf16[512,256]{1,0:T(8,128)(2,1)S(1)} %add_convert_fusion.2), channel_id=1, source_target_pairs={{0,1},{1,2},{2,3},{3,4},{4,5},{5,6},{6,7},{7,0},{8,9},{9,10},{10,1... | collective-permute-start | bytes 786440 | tf_op jit(solution)/shard_map/key_value_grads_ring/ppermute | solution.py:56
  99.7 7.4 %collective-permute-start.26 = (bf16[512,256]{1,0:T(8,128)(2,1)S(1)}, bf16[512,256]{1,0:T(8,128)(2,1)S(1)}, u32[]{:S(2)}, u32[]{:S(2)}) collective-permute-start(bf16[512,256]{1,0:T(8,128)(2,1)S(1)} %add_convert_fusion.1), channel_id=1, source_target_pairs={{0,7},{1,0},{2,1},{3,2},{4,3},{5,4},{6,5},{7,6},{8,15},{9,8},{10,9... | collective-permute-start | bytes 786440 | tf_op jit(solution)/shard_map/key_value_grads_ring/ppermute | solution.py:56
  107.2 6.3 %collective-permute-start.29 = (bf16[128,256]{1,0:T(8,128)(2,1)S(1)}, bf16[128,256]{1,0:T(8,128)(2,1)S(1)}, u32[]{:S(2)}, u32[]{:S(2)}) collective-permute-start(bf16[128,256]{1,0:T(8,128)(2,1)S(1)} %get-tuple-element.131), channel_id=1, source_target_pairs={{0,8},{1,9},{2,10},{3,11},{4,12},{5,13},{6,14},{7,15},{8,16},{9,17... | collective-permute-start | bytes 196616 | tf_op jit(solution)/shard_map/key_value_grads_out/ppermute | solution.py:50
  107.3 6.2 %collective-permute-start.28 = (bf16[128,256]{1,0:T(8,128)(2,1)S(1)}, bf16[128,256]{1,0:T(8,128)(2,1)S(1)}, u32[]{:S(2)}, u32[]{:S(2)}) collective-permute-start(bf16[128,256]{1,0:T(8,128)(2,1)S(1)} %get-tuple-element.132), channel_id=1, source_target_pairs={{0,16},{1,17},{2,18},{3,19},{4,20},{5,21},{6,22},{7,23},{8,24},{9,... | collective-permute-start | bytes 196616 | tf_op jit(solution)/shard_map/key_value_grads_out/ppermute | solution.py:50
  109.1 5.1 %collective-permute-start.27 = (bf16[128,256]{1,0:T(8,128)(2,1)S(1)}, bf16[128,256]{1,0:T(8,128)(2,1)S(1)}, u32[]{:S(2)}, u32[]{:S(2)}) collective-permute-start(bf16[128,256]{1,0:T(8,128)(2,1)S(1)} %get-tuple-element.133), channel_id=1, source_target_pairs={{0,24},{1,25},{2,26},{3,27},{4,28},{5,29},{6,30},{7,31},{8,0},{9,1... | collective-permute-start | bytes 196616 | tf_op jit(solution)/shard_map/key_value_grads_out/ppermute | solution.py:50
